TPU v7x, 128 devices: a whole 4x4x4 slice. The times are simulated.
128 devices in a mesh: seq: 16 (over x_lo, y, core), col: 8 (over z, x_hi).
Axes of the slice: x: 4 (x_hi: 2, x_lo: 2; x = x_hi * 2 + x_lo), y: 4, z: 4, core: 2. Of those that a mesh axis runs over, the one named last changes fastest.
Arguments:
- aligned_sequence_embeddings: bfloat16 [64, 1024, 768], P('seq', 'col'), may hold values from -6 to 6
- horizontal_scaling_factor: float32 [768], replicated, may hold values from 0.1 to 1.9
- horizontal_attend_matrices: bfloat16 [768, 2304], replicated, may hold values from -0.36084392 to 0.36084392
- horizontal_exit_matrix: bfloat16 [768, 768], replicated, may hold values from -0.21875 to 0.21875
- vertical_scaling_factor: float32 [768], replicated, may hold values from 0.1 to 1.9
- vertical_attend_matrices: bfloat16 [768, 2304], replicated, may hold values from -2.598076 to 2.598076
- vertical_exit_matrix: bfloat16 [768, 768], replicated, may hold values from -0.21875 to 0.21875
- dense_scaling_factor: float32 [768], replicated, may hold values from 0.1 to 1.9
- dense_expand_matrix: bfloat16 [768, 3072], replicated, may hold values from -0.21875 to 0.21875
- dense_shrink_matrix: bfloat16 [3072, 768], replicated, may hold values from -0.109375 to 0.109375
Outputs:
- layer_out: bfloat16 [64, 1024, 768], P('seq', 'col')
All inputs are finite; a program needn't handle non-finite values.
Results may differ from a plain program's by a relative error of at most 0.013.
Values may be sent and summed in bfloat16 or wider, within the bound.
No kernel may reach another device: no remote copies, remote signals or barrier semaphores. Data moves between devices by JAX's collectives and lax.ppermute only.
A program may use at most 128 MiB of HBM per device.

v0:
```python
import math

import jax
import jax.numpy as jnp
from jax import lax
from jax.sharding import PartitionSpec as P

HEADS = 12


def normalize(stream, gain):
    mean = jnp.mean(stream, axis=-1, keepdims=True)
    centred = stream - mean
    var = jnp.mean(centred * centred, axis=-1, keepdims=True)
    return (centred * lax.rsqrt(var + 1e-05) * gain).astype(jnp.bfloat16)


def project(normed, weight):
    return jnp.einsum("rcd,df->rcf", normed, weight, preferred_element_type=jnp.float32)


def softmax_last(scores):
    top = jnp.max(scores, axis=-1, keepdims=True)
    expo = jnp.exp(scores - top)
    return expo / jnp.sum(expo, axis=-1, keepdims=True)


def local(
    aligned_sequence_embeddings,
    horizontal_scaling_factor,
    horizontal_attend_matrices,
    horizontal_exit_matrix,
    vertical_scaling_factor,
    vertical_attend_matrices,
    vertical_exit_matrix,
    dense_scaling_factor,
    dense_expand_matrix,
    dense_shrink_matrix,
):
    horizontal_extent, vertical_extent, embedding_breadth = aligned_sequence_embeddings.shape
    head_dim = embedding_breadth // HEADS
    seq_count = lax.axis_size("seq")
    global_sequence_number = horizontal_extent * seq_count
    skip_connection0 = aligned_sequence_embeddings.astype(jnp.float32)
    row_proj = project(
        normalize(skip_connection0, horizontal_scaling_factor), horizontal_attend_matrices
    ).astype(jnp.bfloat16)
    query, keys, values = jnp.split(row_proj, 3, axis=-1)
    keys_all, values_all = (
        lax.all_gather(keys, "col", axis=1, tiled=True),
        lax.all_gather(values, "col", axis=1, tiled=True),
    )
    all_cols = keys_all.shape[1]
    query_heads = query.reshape(horizontal_extent, vertical_extent, HEADS, head_dim)
    key_heads = keys_all.reshape(horizontal_extent, all_cols, HEADS, head_dim)
    value_heads = values_all.reshape(horizontal_extent, all_cols, HEADS, head_dim)
    scale = head_dim ** (-0.5) / math.sqrt(global_sequence_number)
    partial_scores = jnp.einsum(
        "rihe,rjhe->ihj", query_heads, key_heads, preferred_element_type=jnp.float32
    )
    tied = lax.psum(partial_scores, "seq") * scale
    row_weights = softmax_last(tied).astype(jnp.bfloat16)
    row_mix = jnp.einsum(
        "ihj,rjhe->rihe", row_weights, value_heads, preferred_element_type=jnp.float32
    )
    row_mix = row_mix.astype(jnp.bfloat16).reshape(
        horizontal_extent, vertical_extent, embedding_breadth
    )
    stream1 = skip_connection0 + project(row_mix, horizontal_exit_matrix)
    normed_col = normalize(stream1, vertical_scaling_factor)
    col_proj = project(normed_col, vertical_attend_matrices).astype(jnp.bfloat16)
    col_query, col_keys, col_values = jnp.split(col_proj, 3, axis=-1)
    col_query, col_keys, col_values = (
        lax.all_to_all(col_query, "seq", split_axis=1, concat_axis=0, tiled=True),
        lax.all_to_all(col_keys, "seq", split_axis=1, concat_axis=0, tiled=True),
        lax.all_to_all(col_values, "seq", split_axis=1, concat_axis=0, tiled=True),
    )
    group_cols = col_query.shape[1]
    col_query = col_query.reshape(global_sequence_number, group_cols, HEADS, head_dim)
    col_keys = col_keys.reshape(global_sequence_number, group_cols, HEADS, head_dim)
    col_values = col_values.reshape(global_sequence_number, group_cols, HEADS, head_dim)
    col_scores = jnp.einsum(
        "rche,sche->chrs", col_query, col_keys, preferred_element_type=jnp.float32
    ) * head_dim ** (-0.5)
    col_weights = softmax_last(col_scores).astype(jnp.bfloat16)
    col_mix = jnp.einsum(
        "chrs,sche->rche", col_weights, col_values, preferred_element_type=jnp.float32
    )
    col_mix = col_mix.astype(jnp.bfloat16).reshape(
        global_sequence_number, group_cols, embedding_breadth
    )
    col_home = lax.all_to_all(col_mix, "seq", split_axis=0, concat_axis=1, tiled=True)
    stream2 = stream1 + project(col_home, vertical_exit_matrix)
    hidden = jax.nn.gelu(
        project(normalize(stream2, dense_scaling_factor), dense_expand_matrix), approximate=False
    ).astype(jnp.bfloat16)
    return (stream2 + project(hidden, dense_shrink_matrix)).astype(jnp.bfloat16)


def solution(mesh):
    in_specs = (P("seq", "col", None), P(), P(), P(), P(), P(), P(), P(), P(), P())
    out_specs = P("seq", "col", None)
    return jax.shard_map(local, mesh=mesh, in_specs=in_specs, out_specs=out_specs, check_vma=False)
```

profile of v0, /device:TPU:1, one launch (start us, length us, event | category | flops | bytes accessed | tf_op | source)
XLA Modules:
  0.0 466.9 jit_solution(16481935710841390017)
XLA Ops:
  8.0 1.5 fusion.60
  9.5 3.3 convolution_convert_fusion.1
  15.6 90.7 %all-gather.5.cloned.1.call-done = bf16[4,1024,768]{2,1,0:T(8,128)(2,1)} async-done(((bf16[4,128,768]{2,1,0:T(8,128)(2,1)}), bf16[4,1024,768]{2,1,0:T(8,128)(2,1)}) %all-gather.5.cloned.1.call-update) | async-done | bytes 6291472 | tf_op jit(solution)/shard_map/all_gather | solution.py:50
  106.2 8.7 %copy.37 = bf16[4,1024,768]{1,2,0:T(8,128)(2,1)} copy(bf16[4,1024,768]{2,1,0:T(8,128)(2,1)} %all-gather.5.cloned.1.call-done) | data formatting | bytes 12582912 | tf_op jit(solution)/shard_map/all_gather | solution.py:50
  114.9 8.0 %convolution_bitcast_fusion = f32[128,12,1024]{0,2,1:T(8,128)} fusion(bf16[4,1024,12,64]{1,3,2,0:T(8,128)(2,1)} %bitcast.77, bf16[4,128,12,64]{1,3,2,0:T(8,128)(2,1)S(1)} %bitcast.79), kind=kOutput, calls=%fused_computation.74 | convolution fusion | flops 805306368 | bytes 13369344 | tf_op jit(solution)/shard_map/rihe,rjhe->ihj/dot_general | solution.py:58
  122.9 72.5 %all-gather.3.cloned.1.call-done = bf16[4,1024,768]{2,1,0:T(8,128)(2,1)} async-done(((bf16[4,128,768]{2,1,0:T(8,128)(2,1)}), bf16[4,1024,768]{2,1,0:T(8,128)(2,1)}) %all-gather.3.cloned.1.call-update) | async-done | bytes 6291472 | tf_op jit(solution)/shard_map/all_gather | solution.py:51
  195.4 8.7 %copy.36 = bf16[4,1024,768]{1,2,0:T(8,128)(2,1)} copy(bf16[4,1024,768]{2,1,0:T(8,128)(2,1)} %all-gather.3.cloned.1.call-done) | data formatting | bytes 12582912 | tf_op jit(solution)/shard_map/all_gather | solution.py:51
  204.1 127.1 %all-reduce.2.cloned.1.call-done = f32[128,12,1024]{0,2,1:T(8,128)} async-done(((f32[128,12,1024]{0,2,1:T(8,128)}), f32[128,12,1024]{0,2,1:T(8,128)}) %all-reduce.2.cloned.1.call-update) | async-done | bytes 6291472 | tf_op jit(solution)/shard_map/psum | solution.py:61
  331.2 6.3 %fusion.143 = f32[128,12]{0,1:T(8,128)S(1)} fusion(f32[128,12,1024]{0,2,1:T(8,128)} %all-reduce.2.cloned.1.call-done), kind=kOutput, calls=%fused_computation.161 | output fusion | flops 6292479 | bytes 6297600 | tf_op jit(solution)/shard_map/sub | solution.py:24
  337.5 9.5 %fusion.80 = bf16[4,128,12,64]{1,3,0,2:T(8,128)(2,1)S(1)} fusion(f32[128,12]{0,1:T(8,128)S(1)} %fusion.143, bf16[4,1024,12,64]{1,3,2,0:T(8,128)(2,1)} %bitcast.78, f32[128,12,1024]{0,2,1:T(8,128)} %all-reduce.2.cloned.1.call-done), kind=kOutput, calls=%fused_computation.99 | convolution fusion | flops 813566464 | bytes 13375488 | tf_op jit(solution)/shard_map/ihj,rjhe->rihe/dot_general | solution.py:63
  347.1 2.3 fusion.144
  349.7 2.1 convolution_convert_fusion
  352.0 1.5 copy.45
  353.5 6.2 %all-to-all-start.1 = ((bf16[4,128,768]{2,0,1:T(4,128)(2,1)}), bf16[4,128,768]{2,0,1:T(4,128)(2,1)}, u32[]{:S(2)}, u32[]{:S(2)}) async-start(bf16[4,128,768]{2,0,1:T(4,128)(2,1)} %copy.45), calls=%async_computation.1 | async-start | bytes 1572864 | tf_op jit(solution)/shard_map/all_to_all | solution.py:74
  359.8 1.5 copy.47
  361.2 11.6 %all-to-all-done.1 = bf16[4,128,768]{2,0,1:T(4,128)(2,1)} async-done(((bf16[4,128,768]{2,0,1:T(4,128)(2,1)}), bf16[4,128,768]{2,0,1:T(4,128)(2,1)}, u32[]{:S(2)}, u32[]{:S(2)}) %all-to-all-start.1) | async-done | bytes 786464 | tf_op jit(solution)/shard_map/all_to_all | solution.py:74
  372.8 4.3 all-to-all-start.2
  377.1 1.5 copy.43
  379.9 2.2 reshape.75
  382.1 8.1 %all-to-all-done.2 = bf16[4,128,768]{2,0,1:T(4,128)(2,1)S(1)} async-done(((bf16[4,128,768]{2,0,1:T(4,128)(2,1)}), bf16[4,128,768]{2,0,1:T(4,128)(2,1)S(1)}, u32[]{:S(2)}, u32[]{:S(2)}) %all-to-all-start.2) | async-done | bytes 786464 | tf_op jit(solution)/shard_map/all_to_all | solution.py:75
  390.2 4.3 all-to-all-start
  395.5 3.8 reshape.76
  399.2 4.2 fusion.64
  403.4 2.6 fusion.145
  405.9 1.6 all-to-all-done
  407.6 2.2 reshape.74
  409.9 4.9 %convolution_convert_fusion.2 = bf16[8,12,64,64]{3,2,1,0:T(8,128)(2,1)} fusion(f32[8,12,64,64]{2,3,1,0:T(8,128)} %get-tuple-element.16, bf16[64,8,12,64]{3,2,1,0:T(8,128)(2,1)} %reshape.74, f32[8,12,64]{2,1,0:T(8,128)S(1)} %get-tuple-element.15), kind=kOutput, calls=%fused_computation.80 | convolution fusion | flops 51511296 | bytes 3170304 | tf_op jit(solution)/shard_map/chrs,sche->rche/dot_general | solution.py:86
  414.8 1.9 copy.53
  416.7 16.8 %all_to_all.63 = bf16[64,8,768]{2,1,0:T(8,128)(2,1)S(1)} all-to-all(bf16[64,8,768]{2,1,0:T(8,128)(2,1)S(1)} %copy.53), channel_id=1, replica_groups=mesh['seq'=16,'col'=8] {'seq'}, dimensions={0} | all-to-all | bytes 1572864 | tf_op jit(solution)/shard_map/all_to_all | solution.py:92
  433.5 2.3 fusion.146
  436.2 6.9 %fusion.70 = (u8[128,3072]{1,0:T(8,128)(4,1)S(1)}, u8[128,3072]{1,0:T(8,128)(4,1)S(1)}, f32[4,128,3072]{2,1,0:T(8,128)S(1)}) fusion(bf16[768,3072]{1,0:T(8,128)(2,1)} %param.18, f32[4,128,768]{2,1,0:T(8,128)S(1)} %get-tuple-element.18, f32[768]{0:T(1024)S(1)} %copy-done.5, f32[4,128]{1,0:T(4,128)S(1)} %add_rsqrt_fusion, f32[4,128]{1,0:T(4,128)S(1)} %broadcast_multiply_fusion), kind=kOutput, calls=%fused_computation.96 | convolution fusion | flops 2437152768 | bytes 13376512 | tf_op jit(solution)/shard_map/rcd,df->rcf/dot_general | solution.py:19
  443.1 17.3 %add_convert_fusion = bf16[4,128,768]{2,1,0:T(8,128)(2,1)} fusion(f32[4,128,768]{2,1,0:T(8,128)S(1)} %get-tuple-element.18, bf16[3072,768]{1,0:T(8,128)(2,1)S(1)} %bitcast.89, f32[4,128,3072]{2,1,0:T(8,128)S(1)} %get-tuple-element.19, u8[128,3072]{1,0:T(8,128)(4,1)S(1)} %get-tuple-element.6, u8[128,3072]{1,0:T(8,128)(4,1)S(1)} %get-tuple-element.5), kind=kOutput, calls=%fused_computation.88 | convolution fusion | flops 2526806016 | bytes 14155776 | tf_op jit(solution)/shard_map/rcd,df->rcf/dot_general | solution.py:19
  (39 shorter events, 7.5 us)
Async XLA Ops:
  6.5 3.0 copy-start
  6.5 99.7 %all-gather.5.cloned.1.call-start = ((), (), s32[]{:S(2)}) async-start(), calls=%async_computation.5 | async-start | bytes 7077888 | tf_op jit(solution)/shard_map/all_gather | solution.py:50
  14.2 181.2 %all-gather.3.cloned.1.call-start = ((), (), s32[]{:S(2)}) async-start(), calls=%async_computation.4 | async-start | bytes 7077888 | tf_op jit(solution)/shard_map/all_gather | solution.py:51
  15.0 316.2 %all-reduce.2.cloned.1.call-start = ((), (), s32[]{:S(2)}) async-start(), calls=%async_computation.6 | async-start | bytes 12582912 | tf_op jit(solution)/shard_map/psum | solution.py:61
  337.5 9.6 %copy-start.2 = (bf16[4,128,768]{2,1,0:T(8,128)(2,1)S(1)}, bf16[4,128,768]{2,1,0:T(8,128)(2,1)}, u32[]{:S(2)}) copy-start(bf16[4,128,768]{2,1,0:T(8,128)(2,1)} %param.10) | copy-start | bytes 2359300
  347.0 2.7 copy-start.3
  347.0 2.7 copy-start.4
  353.5 19.3 %all-to-all-start.1 = ((bf16[4,128,768]{2,0,1:T(4,128)(2,1)}), bf16[4,128,768]{2,0,1:T(4,128)(2,1)}, u32[]{:S(2)}, u32[]{:S(2)}) async-start(bf16[4,128,768]{2,0,1:T(4,128)(2,1)} %copy.45), calls=%async_computation.1 | async-start | bytes 1572864 | tf_op jit(solution)/shard_map/all_to_all | solution.py:74
  372.8 17.3 %all-to-all-start.2 = ((bf16[4,128,768]{2,0,1:T(4,128)(2,1)}), bf16[4,128,768]{2,0,1:T(4,128)(2,1)S(1)}, u32[]{:S(2)}, u32[]{:S(2)}) async-start(bf16[4,128,768]{2,0,1:T(4,128)(2,1)} %copy.47), calls=%async_computation.2 | async-start | bytes 1572864 | tf_op jit(solution)/shard_map/all_to_all | solution.py:75
  390.2 17.3 %all-to-all-start = ((bf16[4,128,768]{2,0,1:T(4,128)(2,1)}), bf16[4,128,768]{2,0,1:T(4,128)(2,1)S(1)}, u32[]{:S(2)}, u32[]{:S(2)}) async-start(bf16[4,128,768]{2,0,1:T(4,128)(2,1)} %copy.43), calls=%async_computation | async-start | bytes 1572864 | tf_op jit(solution)/shard_map/all_to_all | solution.py:76
  414.8 21.3 %copy-start.5 = (f32[768]{0:T(1024)S(1)}, f32[768]{0:T(1024)}, u32[]{:S(2)}) copy-start(f32[768]{0:T(1024)} %param.17) | copy-start | bytes 9220
  433.5 9.5 %slice-start = ((s8[4718592]{0:T(1024)(128)(4,1)}), s8[4194304]{0:T(1024)(128)(4,1)S(1)}, s32[]{:S(2)}) async-start(s8[4718592]{0:T(1024)(128)(4,1)} %bitcast.88), calls=%async_computation.7 | async-start | bytes 8388608
  436.2 6.9 %slice-start.1 = ((s8[4718592]{0:T(1024)(128)(4,1)}), s8[524288]{0:T(1024)(128)(4,1)S(1)}, s32[]{:S(2)}) async-start(s8[4718592]{0:T(1024)(128)(4,1)} %bitcast.88), calls=%async_computation.8 | async-start | bytes 1048576
  443.1 17.3 %copy-start.1 = (bf16[768,2304]{1,0:T(8,128)(2,1)S(1)}, bf16[768,2304]{1,0:T(8,128)(2,1)}, u32[]{:S(2)}) copy-start(bf16[768,2304]{1,0:T(8,128)(2,1)} %param.12) | copy-start | bytes 10616836
Sparse Core Ops, SparseCore 0:
  14.4 91.8 all-gather.4
  108.6 86.8 all-gather.2
  198.0 133.1 all-reduce.1
where the time goes:
time: 468 us; the launch traced here: 467 us
  waiting for transfers between devices  312 us (67%)
  matrix products  60.7 us (13%)
  local copies, waits for them, and re-layouts  36.4 us (8%)
  blocking collectives  16.8 us (4%)
  starting transfers between devices  15 us (3%)
  between operations  13.3 us (3%)
  other arithmetic  12.5 us (3%)
    psum x1, waiting for transfers between devices, local(): tied = lax.psum(partial_scores, 'seq') * scale  127 us
    all_gather x1, waiting for transfers between devices, local(): lax.all_gather(keys, 'col', axis=1, tiled=True)  90.7 us
    all_gather x1, waiting for transfers between devices, local(): lax.all_gather(values, 'col', axis=1, tiled=True)  72.5 us
    dot_general x6, matrix products, project(): jnp.einsum('rcd,df->rcf', normed, weight, preferred_element_type=jnp.floa...  34.1 us
    all_to_all x1, blocking collectives, local(): lax.all_to_all(col_mix, 'seq', split_axis=0, concat_axis=1, tiled=True)  16.8 us
    all_to_all x1, waiting for transfers between devices, local(): lax.all_to_all(col_query, 'seq', split_axis=1, concat_axis=0, tiled=True)  11.6 us
    dot_general x1, matrix products, local(): jnp.einsum('ihj,rjhe->rihe', row_weights, value_heads, preferred_element_...  9.52 us
  transfers between devices with their start and end apart: 6, of which 6 were waited for; matrix products, arithmetic and copies ran while one was open for 9% of the time, Pallas kernels for 0%

commit v1 on v0

v1 whole, which is shorter than its diff:
```python
import math

import jax
import jax.numpy as jnp
from jax import lax
from jax.experimental import pallas as pl
from jax.experimental.pallas import tpu as pltpu
from jax.sharding import PartitionSpec as P

AXES = ("seq", "col")
HEADS = 12
E = 64
BF = jnp.bfloat16
F32 = jnp.float32
VMEM_LIMIT = 56 * 1024 * 1024


def device(xl, y, c, z, xh):
    return ((xl * 4 + y) * 2 + c) * 8 + z * 2 + xh


R2, R4 = range(2), range(4)
X_RINGS = [[device(xl, y, c, z, xh) for xh in R2 for xl in R2] for y in R4 for c in R2 for z in R4]
Y_RINGS = [[device(xl, y, c, z, xh) for y in R4] for xl in R2 for c in R2 for z in R4 for xh in R2]
Z_RINGS = [[device(xl, y, c, z, xh) for z in R4] for xl in R2 for y in R4 for c in R2 for xh in R2]
PLANES = [[device(xl, y, c, z, xh) for xh in R2 for xl in R2 for y in R4] for c in R2 for z in R4]
OTHER_CORE = [
    (device(xl, y, c, z, xh), device(xl, y, 1 - c, z, xh))
    for xl in R2 for y in R4 for c in R2 for z in R4 for xh in R2
]


def params():
    return pltpu.CompilerParams(vmem_limit_bytes=VMEM_LIMIT)


def swap(array, groups):
    return lax.all_to_all(array, AXES, split_axis=0, concat_axis=0, tiled=True, axis_index_groups=groups)


def gather(array, groups):
    return lax.all_gather(array, AXES, axis=0, tiled=False, axis_index_groups=groups)


def to_other_core(array):
    return lax.ppermute(array, AXES, OTHER_CORE)


def mm(a, b):
    return jnp.dot(a, b, preferred_element_type=F32)


def mm_t(a, b):
    return lax.dot_general(a, b, (((1,), (1,)), ((), ())), preferred_element_type=F32)


def normalize(stream, gain):
    mean = jnp.mean(stream, axis=-1, keepdims=True)
    centred = stream - mean
    var = jnp.mean(centred * centred, axis=-1, keepdims=True)
    return (centred * lax.rsqrt(var + 1e-05) * gain).astype(BF)


def write_pairs(normed, weight, out):
    low = lax.broadcasted_iota(jnp.int32, (128, 128), 1) < E
    for rp in range(2):
        first = mm(normed[2 * rp * 128 : (2 * rp + 1) * 128, :], weight)
        second = mm(normed[(2 * rp + 1) * 128 : (2 * rp + 2) * 128, :], weight)
        for t in range(6):
            a, b = first[:, t * 128 : (t + 1) * 128], second[:, t * 128 : (t + 1) * 128]
            pair = (
                jnp.where(low, a, pltpu.roll(b, E, 1)),
                jnp.where(low, pltpu.roll(a, E, 1), b),
            )
            for k in range(2):
                g, h = (2 * t + k) // 3, (2 * t + k) % 3
                out[g, rp, :, h * 128 : (h + 1) * 128] = pair[k].astype(BF)


def key_kernel(x_ref, gain_ref, w_ref, normed_ref, out_ref):
    normed_ref[...] = normalize(x_ref[...].astype(F32), gain_ref[...])
    write_pairs(normed_ref[...], w_ref[...], out_ref)


def key_proj(x, gain, weight):
    return pl.pallas_call(
        key_kernel,
        grid=(1,),
        in_specs=[
            pl.BlockSpec((512, 768), lambda i: (0, 0)),
            pl.BlockSpec((1, 768), lambda i: (0, 0)),
            pl.BlockSpec((768, 768), lambda i: (0, 1)),
        ],
        out_specs=[
            pl.BlockSpec((512, 768), lambda i: (0, 0)),
            pl.BlockSpec((4, 2, 128, 384), lambda i: (0, 0, 0, 0)),
        ],
        out_shape=[
            jax.ShapeDtypeStruct((512, 768), BF),
            jax.ShapeDtypeStruct((4, 2, 128, 384), BF),
        ],
        compiler_params=params(),
        name="key_proj",
    )(x, gain, weight)


def query_value_kernel(normed_ref, w_ref, out_ref):
    write_pairs(normed_ref[...], w_ref[...], out_ref.at[:, 0])


def query_value_proj(normed, weight):
    return pl.pallas_call(
        query_value_kernel,
        grid=(2,),
        in_specs=[
            pl.BlockSpec((512, 768), lambda i: (0, 0)),
            pl.BlockSpec((768, 768), lambda i: (0, 2 * i)),
        ],
        out_specs=pl.BlockSpec((4, 1, 2, 128, 384), lambda i: (0, i, 0, 0, 0)),
        out_shape=jax.ShapeDtypeStruct((4, 2, 2, 128, 384), BF),
        compiler_params=params(),
        name="query_value_proj",
    )(normed, weight)


def scores_kernel(q0_ref, q1_ref, k0_ref, k1_ref, out_ref):
    def query(xh):
        return jnp.concatenate(
            [q[xh * 2 + xl, rp] for q in (q0_ref, q1_ref) for xl in range(2) for rp in range(2)], axis=1
        )

    def keys(z, xh):
        return jnp.concatenate(
            [k[z, xh * 2 + xl, rp] for k in (k0_ref, k1_ref) for xl in range(2) for rp in range(2)], axis=1
        )

    left = jnp.concatenate([query(0), query(1)], axis=0)
    for z in range(4):
        right = jnp.concatenate([keys(z, 0), keys(z, 1)], axis=0)
        out_ref[:, 0, :, z * 256 : (z + 1) * 256] = mm_t(left, right).reshape(4, 32, 256)


def partial_scores(q0, q1, k0, k1):
    q_spec = pl.BlockSpec((4, 2, 64, 128), lambda h: (0, 0, 0, h))
    k_spec = pl.BlockSpec((4, 4, 2, 128, 128), lambda h: (0, 0, 0, 0, h))
    return pl.pallas_call(
        scores_kernel,
        grid=(3,),
        in_specs=[q_spec, q_spec, k_spec, k_spec],
        out_specs=pl.BlockSpec((4, 1, 32, 1024), lambda h: (0, h, 0, 0)),
        out_shape=jax.ShapeDtypeStruct((4, 3, 32, 1024), F32),
        compiler_params=params(),
        name="partial_scores",
    )(q0, q1, k0, k1)


def softmax_kernel(scale, parts_ref, out_ref):
    tied = (parts_ref[0] + parts_ref[1] + parts_ref[2] + parts_ref[3]) * scale
    expo = jnp.exp(tied - jnp.max(tied, axis=-1, keepdims=True))
    out_ref[...] = (expo / jnp.sum(expo, axis=-1, keepdims=True)).astype(BF)


def row_softmax(parts, scale):
    return pl.pallas_call(
        lambda *refs: softmax_kernel(scale, *refs),
        grid=(3,),
        in_specs=[pl.BlockSpec((4, 1, 32, 1024), lambda h: (0, h, 0, 0))],
        out_specs=pl.BlockSpec((1, 32, 1024), lambda h: (h, 0, 0)),
        out_shape=jax.ShapeDtypeStruct((3, 32, 1024), BF),
        compiler_params=params(),
        name="row_softmax",
    )(parts)


def mix_kernel(core_ref, w_ref, v0_ref, v1_ref, out_ref):
    weights = w_ref[:, 0].reshape(128, 1024)
    for k, v in enumerate((v0_ref, v1_ref)):
        owner = (core_ref[0] + k) % 2
        for xl in range(2):
            right = jnp.concatenate(
                [
                    jnp.concatenate([v[z, xh * 2 + xl, 0], v[z, xh * 2 + xl, 1]], axis=1)
                    for z in range(4)
                    for xh in range(2)
                ],
                axis=0,
            )
            mixed = mm(weights, right)
            pair = jnp.concatenate(
                [mixed[:, :128].reshape(16, 8, 128), mixed[:, 128:].reshape(16, 8, 128)], axis=1
            )
            out_ref[:, pl.ds(owner, 1), xl * 16 : (xl + 1) * 16, :] = pair.astype(BF)[:, None]


def row_mix(core, weights, v0, v1):
    v_spec = pl.BlockSpec((4, 4, 2, 128, 128), lambda h: (0, 0, 0, 0, h))
    return pl.pallas_call(
        mix_kernel,
        grid=(3,),
        in_specs=[
            pl.BlockSpec(memory_space=pltpu.SMEM),
            pl.BlockSpec((4, 1, 32, 1024), lambda h: (0, h, 0, 0)),
            v_spec,
            v_spec,
        ],
        out_specs=pl.BlockSpec((16, 2, 32, 128), lambda h: (0, 0, 0, h)),
        out_shape=jax.ShapeDtypeStruct((16, 2, 32, 384), BF),
        compiler_params=params(),
        name="row_mix",
    )(core, weights, v0, v1)


def column_kernel(
    mix_ref, x_ref, gain_col_ref, gain_ffn_ref, exit_row_hbm, attend_hbm, exit_col_hbm, expand_hbm, shrink_hbm,
    out_ref, exit_row, attend, exit_col, expand, shrink, qkv, stream, col_mix, sems,
):
    copies = [
        pltpu.make_async_copy(src, dst, sems.at[i])
        for i, (src, dst) in enumerate(
            [
                (exit_row_hbm, exit_row),
                (attend_hbm, attend),
                (exit_col_hbm, exit_col),
                (expand_hbm, expand),
                (shrink_hbm, shrink),
            ]
        )
    ]
    for copy in copies:
        copy.start()

    low = lax.broadcasted_iota(jnp.int32, (64, 128), 1) < E
    halves = ([], [])
    for y in range(4):
        tiles = ([], [])
        for t in range(6):
            (g0, h0), (g1, h1) = divmod(2 * t, 3), divmod(2 * t + 1, 3)
            a = mix_ref[g0 * 4 + y, :, h0 * 128 : (h0 + 1) * 128].astype(F32)
            b = mix_ref[g1 * 4 + y, :, h1 * 128 : (h1 + 1) * 128].astype(F32)
            tiles[0].append(jnp.where(low, a, pltpu.roll(b, E, 1)).astype(BF))
            tiles[1].append(jnp.where(low, pltpu.roll(a, E, 1), b).astype(BF))
        for k in range(2):
            halves[k].append(jnp.concatenate(tiles[k], axis=1))
    copies[0].wait()
    exits = [mm(jnp.concatenate(halves[k], axis=0), exit_row[...]).reshape(32, 1, 8, 768) for k in range(2)]
    exits = jnp.concatenate(exits, axis=1).reshape(512, 768)
    x = jnp.concatenate([x_ref[(xl * 4 + y) * 2 + c] for y in range(4) for c in range(2) for xl in range(2)], axis=0)
    stream[...] = x.astype(F32) + exits

    place = lax.broadcasted_iota(jnp.int32, (512, 512), 0)
    token = lax.broadcasted_iota(jnp.int32, (512, 512), 1)
    by_column = ((place % 64) * 8 + place // 64 == token).astype(F32).astype(BF)
    by_token = ((token % 64) * 8 + token // 64 == place).astype(F32).astype(BF)
    normed = mm(by_column, normalize(stream[...], gain_col_ref[...])).astype(BF)
    copies[1].wait()
    qkv[...] = mm(normed, attend[...]).astype(BF)
    group = lax.broadcasted_iota(jnp.int32, (256, 256), 0) // E == lax.broadcasted_iota(jnp.int32, (256, 256), 1) // E
    group = group.astype(F32).astype(BF)
    segment = lax.broadcasted_iota(jnp.int32, (64, 128), 1) < E
    for c in range(8):
        for g in range(3):
            rows, lanes = slice(c * 64, (c + 1) * 64), g * 256
            q = qkv[rows, lanes : lanes + 256]
            k = qkv[rows, 768 + lanes : 768 + lanes + 256]
            v = qkv[rows, 1536 + lanes : 1536 + lanes + 256]
            k = jnp.concatenate([k] * 4, axis=0) * group
            v = jnp.concatenate([v] * 4, axis=0) * group
            scores = mm_t(q, k) * (E ** -0.5)
            weights = []
            for half in range(2):
                s = scores[:, half * 128 : (half + 1) * 128]
                top0 = jnp.max(jnp.where(segment, s, -jnp.inf), axis=-1, keepdims=True)
                top1 = jnp.max(jnp.where(segment, -jnp.inf, s), axis=-1, keepdims=True)
                expo = jnp.exp(s - jnp.where(segment, top0, top1))
                sum0 = jnp.sum(jnp.where(segment, expo, 0.0), axis=-1, keepdims=True)
                sum1 = jnp.sum(jnp.where(segment, 0.0, expo), axis=-1, keepdims=True)
                weights.append((expo / jnp.where(segment, sum0, sum1)).astype(BF))
            col_mix[rows, lanes : lanes + 256] = mm(jnp.concatenate(weights, axis=1), v).astype(BF)
    mixed = mm(by_token, col_mix[...]).astype(BF)
    copies[2].wait()
    stream[...] += mm(mixed, exit_col[...])

    normed = normalize(stream[...], gain_ffn_ref[...])
    copies[3].wait()
    copies[4].wait()
    for f in range(6):
        cols = slice(f * 512, (f + 1) * 512)
        pre = mm(normed, expand[:, cols])
        hidden = (0.5 * pre * (1.0 + lax.erf(pre * math.sqrt(0.5)))).astype(BF)
        stream[...] += mm(hidden, shrink[cols, :])
    done = stream[...].astype(BF)
    for i, (y, c, xl) in enumerate((y, c, xl) for y in range(4) for c in range(2) for xl in range(2)):
        out_ref[(xl * 4 + y) * 2 + c] = done[i * 32 : (i + 1) * 32, :]


def column_part(mix, x, gain_col, gain_ffn, exit_row, attend, exit_col, expand, shrink):
    whole = pl.BlockSpec(memory_space=pltpu.VMEM)
    hbm = pl.BlockSpec(memory_space=pl.ANY)
    return pl.pallas_call(
        column_kernel,
        in_specs=[whole] * 4 + [hbm] * 5,
        out_specs=whole,
        out_shape=jax.ShapeDtypeStruct((16, 32, 768), BF),
        scratch_shapes=[pltpu.VMEM(w.shape, BF) for w in (exit_row, attend, exit_col, expand, shrink)]
        + [
            pltpu.VMEM((512, 2304), BF),
            pltpu.VMEM((512, 768), F32),
            pltpu.VMEM((512, 768), BF),
            pltpu.SemaphoreType.DMA((5,)),
        ],
        compiler_params=params(),
        name="column_part",
    )(mix, x, gain_col, gain_ffn, exit_row, attend, exit_col, expand, shrink)


def local(
    embeddings,
    gain_row,
    attend_row,
    exit_row,
    gain_col,
    attend_col,
    exit_col,
    gain_ffn,
    expand,
    shrink,
):
    core = lax.axis_index("seq") % 2
    scale = E ** (-0.5) / math.sqrt(embeddings.shape[0] * lax.axis_size("seq"))

    normed, keys = key_proj(embeddings.reshape(512, 768), gain_row.reshape(1, 768), attend_row)
    keys = swap(keys, X_RINGS)
    keys0 = gather(keys, Z_RINGS)
    queries_values = swap(query_value_proj(normed, attend_row), X_RINGS)
    queries, values = queries_values[:, 0], queries_values[:, 1]
    queries0 = lax.dynamic_slice_in_dim(queries, core * 64, 64, axis=2)
    queries1 = to_other_core(lax.dynamic_slice_in_dim(queries, (1 - core) * 64, 64, axis=2))
    values0 = gather(values, Z_RINGS)

    x = embeddings.reshape(4, 2, 8, 8, 768).transpose(2, 1, 0, 3, 4).reshape(16, 32, 768)
    x = lax.all_to_all(x, "seq", split_axis=0, concat_axis=0, tiled=True)

    keys1 = to_other_core(keys0)
    parts = swap(partial_scores(queries0, queries1, keys0, keys1), Y_RINGS)
    weights = row_softmax(parts, scale)
    weights = swap(jnp.broadcast_to(weights[None], (4, 3, 32, 1024)), Y_RINGS)
    values1 = to_other_core(values0)
    mix = row_mix(core.reshape(1).astype(jnp.int32), weights, values0, values1)
    mix = swap(mix, PLANES).reshape(16, 64, 384)

    out = column_part(
        mix, x, gain_col.reshape(1, 768), gain_ffn.reshape(1, 768), exit_row, attend_col, exit_col, expand, shrink
    )
    out = lax.all_to_all(out, "seq", split_axis=0, concat_axis=0, tiled=True)
    return out.reshape(8, 2, 4, 8, 768).transpose(2, 1, 0, 3, 4).reshape(4, 128, 768)


def solution(mesh):
    in_specs = (P("seq", "col", None), P(), P(), P(), P(), P(), P(), P(), P(), P())
    out_specs = P("seq", "col", None)
    return jax.shard_map(local, mesh=mesh, in_specs=in_specs, out_specs=out_specs, check_vma=False)
```

time: 468 us -> 259 us (0.55)
  waiting for transfers between devices: 312 us -> 87.7 us
  blocking collectives: 16.8 us -> 83 us
  matrix products: 60.7 us -> 0 us
  Pallas kernels: 0 us -> 46.3 us
  local copies, waits for them, and re-layouts: 36.4 us -> 12.2 us
  other arithmetic: 12.5 us -> 0 us
    psum x1 -> x0, waiting for transfers between devices: 127 us -> none  [local(): tied = lax.psum(partial_scores, 'seq') * scale]
    all_gather x2, waiting for transfers between devices: 163 us -> 54.6 us  [gather(): lax.all_gather(array, AXES, axis=0, tiled=False, axis_index_groups=groups)]
    all_to_all x1 -> x4, blocking collectives: 16.8 us -> 83 us  [the longest x3 63.7 us: swap(): lax.all_to_all(array, AXES, split_axis=0, concat_axis=0, tiled=True, axis...]
    dot_general x10 -> x0, matrix products: 60.7 us -> none  [the longest x6 34.1 us: project(): jnp.einsum('rcd,df->rcf', normed, weight, preferred_element_type=jnp.floa...]
    pallas_call x0 -> x6, Pallas kernels: none -> 46.3 us  [the longest x1 24 us: column_part(): pl.pallas_call(column_kernel, in_specs=[whole] * 4 + [hbm] * 5, out_specs...]
    all_gather x2 -> x0, local copies, waits for them, and re-layouts: 17.3 us -> none  [the longest x1 8.69 us: local(): lax.all_gather(keys, 'col', axis=1, tiled=True)]
    sub x2 -> x0, other arithmetic: 8.86 us -> none  [softmax_last(): expo = jnp.exp(scores - top)]
    all_to_all x3, waiting for transfers between devices: 21.3 us -> 29.2 us  [the longest x2 21.3 us: swap(): lax.all_to_all(array, AXES, split_axis=0, concat_axis=0, tiled=True, axis...]
  transfers between devices with their start and end apart: 6 -> 8, of which waited for: 6 -> 6; matrix products, arithmetic and copies ran while one was open for 9% -> 3% of each run, Pallas kernels for 0% -> 7%
where the time goes in v1:
time: 259 us; the launch traced here: 258 us
  waiting for transfers between devices  87.7 us (34%)
  blocking collectives  83 us (32%)
  Pallas kernels  46.3 us (18%)
  starting transfers between devices  15.8 us (6%)
  between operations  13.5 us (5%)
  local copies, waits for them, and re-layouts  12.2 us (5%)
    all_to_all x3, blocking collectives, swap(): lax.all_to_all(array, AXES, split_axis=0, concat_axis=0, tiled=True, axis...  63.7 us
    all_gather x2, waiting for transfers between devices, gather(): lax.all_gather(array, AXES, axis=0, tiled=False, axis_index_groups=groups)  54.6 us
    pallas_call x1, Pallas kernels, column_part(): pl.pallas_call(column_kernel, in_specs=[whole] * 4 + [hbm] * 5, out_specs...  24 us
    all_to_all x2, waiting for transfers between devices, swap(): lax.all_to_all(array, AXES, split_axis=0, concat_axis=0, tiled=True, axis...  21.3 us
    all_to_all x1, blocking collectives, local(): out = lax.all_to_all(out, 'seq', split_axis=0, concat_axis=0, tiled=True)  19.3 us
    all_to_all x2, starting transfers between devices, swap(): lax.all_to_all(array, AXES, split_axis=0, concat_axis=0, tiled=True, axis...  8.87 us
    all_to_all x1, waiting for transfers between devices, local(): x = lax.all_to_all(x, 'seq', split_axis=0, concat_axis=0, tiled=True)  7.86 us
    pallas_call x1, Pallas kernels, partial_scores(): pl.pallas_call(scores_kernel, grid=(3,), in_specs=[q_spec, q_spec, k_spec...  6.15 us
  transfers between devices with their start and end apart: 8, of which 6 were waited for; matrix products, arithmetic and copies ran while one was open for 3% of the time, Pallas kernels for 7%

profile of v1, /device:TPU:1, one launch (start us, length us, event | category | flops | bytes accessed | tf_op | source)
XLA Modules:
  0.0 258.5 jit_solution(8932183998861361605)
XLA Ops:
  6.5 1.3 reshape.35.gain_ref
  7.8 3.6 %key_proj.1 = (bf16[512,768]{1,0:T(8,128)(2,1)}, bf16[4,2,128,384]{3,2,1,0:T(8,128)(2,1)}) custom-call(bf16[512,768]{1,0:T(8,128)(2,1)} %bitcast.23, f32[1,768]{1,0:T(1,128)} %reshape.35.gain_ref, bf16[768,2304]{1,0:T(8,128)(2,1)} %w_ref.3), custom_call_target="tpu_custom_call" | custom-call | tf_op jit(solution)/shard_map/key_proj/pallas_call | solution.py:86
  11.4 16.3 %all_to_all.35 = bf16[4,2,128,384]{3,2,1,0:T(8,128)(2,1)} all-to-all(bf16[4,2,128,384]{3,2,1,0:T(8,128)(2,1)} %get-tuple-element.8), channel_id=1, replica_groups={{0,64,1,65},{2,66,3,67},{4,68,5,69},{6,70,7,71},{8,72,9,73},{10,74,11,7..., dimensions={0} | all-to-all | bytes 1572864 | tf_op jit(solution)/shard_map/all_to_all | solution.py:38
  27.8 4.2 %query_value_proj.1 = bf16[4,2,2,128,384]{4,3,2,1,0:T(8,128)(2,1)} custom-call(bf16[512,768]{1,0:T(8,128)(2,1)} %get-tuple-element.7.normed_ref, bf16[768,2304]{1,0:T(8,128)(2,1)} %w_ref.3), custom_call_target="tpu_custom_call" | custom-call | tf_op jit(solution)/shard_map/query_value_proj/pallas_call | solution.py:112
  32.0 22.4 %all_to_all.36 = bf16[4,2,2,128,384]{4,3,2,1,0:T(8,128)(2,1)S(1)} all-to-all(bf16[4,2,2,128,384]{4,3,2,1,0:T(8,128)(2,1)} %query_value_proj.1), channel_id=1, replica_groups={{0,64,1,65},{2,66,3,67},{4,68,5,69},{6,70,7,71},{8,72,9,73},{10,74,11,7..., dimensions={0} | all-to-all | bytes 3145728 | tf_op jit(solution)/shard_map/all_to_all | solution.py:38
  54.4 1.3 fusion
  55.7 13.8 %all-gather.5.cloned.1.call-done = bf16[16,2,128,384]{3,2,1,0:T(8,128)(2,1)} async-done(((bf16[4,2,128,384]{3,2,1,0:T(8,128)(2,1)}), bf16[16,2,128,384]{3,2,1,0:T(8,128)(2,1)}) %all-gather.5.cloned.1.call-update) | async-done | bytes 3145744 | tf_op jit(solution)/shard_map/all_gather | solution.py:42
  69.5 0.7 collective-permute-start.1
  70.2 40.8 %all-gather.7.cloned.1.call-done = bf16[16,1,2,128,384]{4,3,2,1,0:T(8,128)(2,1)} async-done(((bf16[4,1,2,128,384]{4,3,2,1,0:T(8,128)(2,1)}), bf16[16,1,2,128,384]{4,3,2,1,0:T(8,128)(2,1)}) %all-gather.7.cloned.1.call-update) | async-done | bytes 3145744 | tf_op jit(solution)/shard_map/all_gather | solution.py:42
  111.0 0.7 collective-permute-start.2
  111.7 2.0 dynamic-slice_bitcast_fusion
  113.7 3.9 %collective-permute-done.q1_ref = bf16[4,2,64,384]{3,2,1,0:T(8,128)(2,1)S(1)} collective-permute-done((bf16[4,2,64,384]{3,2,1,0:T(8,128)(2,1)S(1)}, bf16[4,2,64,384]{3,2,1,0:T(8,128)(2,1)S(1)}, u32[]{:S(2)}, u32[]{:S(2)}) %collective-permute-start) | collective-permute-done | bytes 393248 | tf_op jit(solution)/shard_map/ppermute | solution.py:46
  117.6 0.8 copy-done.5
  118.3 1.0 copy-done.2
  119.3 6.1 %partial_scores.1 = f32[4,3,32,1024]{3,2,1,0:T(8,128)} custom-call(bf16[4,2,64,384]{3,2,1,0:T(8,128)(2,1)} %get-tuple-element.12.q0_ref, bf16[4,2,64,384]{3,2,1,0:T(8,128)(2,1)} %copy-done.5, bf16[4,4,2,128,384]{4,3,2,1,0:T(8,128)(2,1)} %bitcast.19, bf16[4,4,2,128,384]{4,3,2,1,0:T(8,128)(2,1)} %copy-done.2), custom_call_target="tpu_custom_call" | custom-call | tf_op jit(solution)/shard_map/partial_scores/pallas_call | solution.py:146
  125.5 25.0 %all_to_all.37.refs_0_ = f32[4,3,32,1024]{3,2,1,0:T(8,128)} all-to-all(f32[4,3,32,1024]{3,2,1,0:T(8,128)} %partial_scores.1), channel_id=1, replica_groups={{0,16,32,48},{1,17,33,49},{2,18,34,50},{3,19,35,51},{4,20,36,52},{5,21,..., dimensions={0} | all-to-all | bytes 3145728 | tf_op jit(solution)/shard_map/all_to_all | solution.py:38
  150.5 3.2 %row_softmax.1 = bf16[3,32,1024]{2,1,0:T(8,128)(2,1)} custom-call(f32[4,3,32,1024]{3,2,1,0:T(8,128)} %all_to_all.37.refs_0_), custom_call_target="tpu_custom_call" | custom-call | tf_op jit(solution)/shard_map/row_softmax/pallas_call | solution.py:164
  153.6 1.9 broadcast_in_dim.2
  155.5 3.5 %all-to-all-start.3 = ((bf16[4,3,32,1024]{3,2,1,0:T(8,128)(2,1)}), bf16[4,3,32,1024]{3,2,1,0:T(8,128)(2,1)S(1)}, u32[]{:S(2)}, u32[]{:S(2)}) async-start(bf16[4,3,32,1024]{3,2,1,0:T(8,128)(2,1)} %broadcast_in_dim.2), calls=%async_computation.3 | async-start | bytes 1572864 | tf_op jit(solution)/shard_map/all_to_all | solution.py:38
  159.1 1.0 copy.13
  160.0 10.1 %all-to-all-done.3.w_ref = bf16[4,3,32,1024]{3,2,1,0:T(8,128)(2,1)S(1)} async-done(((bf16[4,3,32,1024]{3,2,1,0:T(8,128)(2,1)}), bf16[4,3,32,1024]{3,2,1,0:T(8,128)(2,1)S(1)}, u32[]{:S(2)}, u32[]{:S(2)}) %all-to-all-start.3) | async-done | bytes 786464 | tf_op jit(solution)/shard_map/all_to_all | solution.py:38
  170.1 5.5 %all-to-all-start.5 = ((bf16[16,32,768]{2,1,0:T(8,128)(2,1)}), bf16[16,32,768]{2,1,0:T(8,128)(2,1)S(1)}, u32[]{:S(2)}, u32[]{:S(2)}) async-start(bf16[16,32,768]{2,1,0:T(8,128)(2,1)} %bitcast.9), calls=%async_computation.5 | async-start | bytes 1572864 | tf_op jit(solution)/shard_map/all_to_all | solution.py:341
  175.7 5.2 %row_mix.1 = bf16[16,2,32,384]{3,2,1,0:T(8,128)(2,1)} custom-call(s32[1]{0:T(128)} %bitcast.core_ref, bf16[4,3,32,1024]{3,2,1,0:T(8,128)(2,1)} %copy-done.4, bf16[4,4,2,128,384]{4,3,2,1,0:T(8,128)(2,1)} %bitcast.22, bf16[4,4,2,128,384]{4,3,2,1,0:T(8,128)(2,1)} %collective-permute-done.2.v1_ref), custom_call_target="tpu_custom_call" | custom-call | tf_op jit(solution)/shard_map/row_mix/pallas_call | solution.py:197
  180.9 7.9 %all-to-all-done.5.x_ref = bf16[16,32,768]{2,1,0:T(8,128)(2,1)S(1)} async-done(((bf16[16,32,768]{2,1,0:T(8,128)(2,1)}), bf16[16,32,768]{2,1,0:T(8,128)(2,1)S(1)}, u32[]{:S(2)}, u32[]{:S(2)}) %all-to-all-start.5) | async-done | bytes 786464 | tf_op jit(solution)/shard_map/all_to_all | solution.py:341
  188.7 5.4 %all-to-all-start.4 = ((bf16[16,2,32,384]{3,2,1,0:T(8,128)(2,1)}), bf16[16,2,32,384]{3,2,1,0:T(8,128)(2,1)S(1)}, u32[]{:S(2)}, u32[]{:S(2)}) async-start(bf16[16,2,32,384]{3,2,1,0:T(8,128)(2,1)} %row_mix.1), calls=%async_computation.4 | async-start | bytes 1572864 | tf_op jit(solution)/shard_map/all_to_all | solution.py:38
  194.1 0.6 reshape.39.gain_col_ref
  194.7 0.6 reshape.40.gain_ffn_ref
  195.3 11.2 %all-to-all-done.4 = bf16[16,2,32,384]{3,2,1,0:T(8,128)(2,1)S(1)} async-done(((bf16[16,2,32,384]{3,2,1,0:T(8,128)(2,1)}), bf16[16,2,32,384]{3,2,1,0:T(8,128)(2,1)S(1)}, u32[]{:S(2)}, u32[]{:S(2)}) %all-to-all-start.4) | async-done | bytes 786464 | tf_op jit(solution)/shard_map/all_to_all | solution.py:38
  206.5 0.9 copy-done.1
  207.4 24.0 %column_part.1 = bf16[16,32,768]{2,1,0:T(8,128)(2,1)} custom-call(bf16[16,64,384]{2,1,0:T(8,128)(2,1)} %bitcast.17, bf16[16,32,768]{2,1,0:T(8,128)(2,1)} %copy-done, f32[1,768]{1,0:T(1,128)} %reshape.39.gain_col_ref, f32[1,768]{1,0:T(1,128)} %reshape.40.gain_ffn_ref, bf16[768,768]{1,0:T(8,128)(2,1)} %exit_row_hbm.1, bf16[768,2304]{1,0:T(8,128)(2,1)} %attend_hbm.1, ...), custom_call_target="tpu_custom_call" | custom-call | tf_op jit(solution)/shard_map/column_part/pallas_call | solution.py:299
  231.4 19.3 %all_to_all.38 = bf16[16,32,768]{2,1,0:T(8,128)(2,1)S(1)} all-to-all(bf16[16,32,768]{2,1,0:T(8,128)(2,1)} %column_part.1), channel_id=1, replica_groups=mesh['seq'=16,'col'=8] {'seq'}, dimensions={0} | all-to-all | bytes 1572864 | tf_op jit(solution)/shard_map/all_to_all | solution.py:354
  250.7 0.9 copy.14
  (20 shorter events, 0.1 us)
Async XLA Ops:
  6.5 63.0 %all-gather.5.cloned.1.call-start = ((), (), s32[]{:S(2)}) async-start(), calls=%async_computation.7 | async-start | bytes 3932160 | tf_op jit(solution)/shard_map/all_gather | solution.py:42
  27.8 83.3 %all-gather.7.cloned.1.call-start = ((), (), s32[]{:S(2)}) async-start(), calls=%async_computation.8 | async-start | bytes 3932160 | tf_op jit(solution)/shard_map/all_gather | solution.py:42
  69.5 48.0 %collective-permute-start.1 = (bf16[4,4,2,128,384]{4,3,2,1,0:T(8,128)(2,1)}, bf16[4,4,2,128,384]{4,3,2,1,0:T(8,128)(2,1)S(1)}, u32[]{:S(2)}, u32[]{:S(2)}) collective-permute-start(bf16[4,4,2,128,384]{4,3,2,1,0:T(8,128)(2,1)} %bitcast.18), channel_id=1, source_target_pairs={{0,8},{1,9},{2,10},{3,11},{4,12},{5,13},{6,14},{7,15},{8,0},{9,1},... | collective-permute-start | bytes 9437192 | tf_op jit(solution)/shard_map/ppermute | solution.py:46
  111.0 64.6 %collective-permute-start.2 = (bf16[4,4,2,128,384]{4,3,2,1,0:T(8,128)(2,1)}, bf16[4,4,2,128,384]{4,3,2,1,0:T(8,128)(2,1)}, u32[]{:S(2)}, u32[]{:S(2)}) collective-permute-start(bf16[4,4,2,128,384]{4,3,2,1,0:T(8,128)(2,1)} %bitcast.21), channel_id=1, source_target_pairs={{0,8},{1,9},{2,10},{3,11},{4,12},{5,13},{6,14},{7,15},{8,0},{9,1},... | collective-permute-start | bytes 9437192 | tf_op jit(solution)/shard_map/ppermute | solution.py:46
  113.7 3.9 %collective-permute-start = (bf16[4,2,64,384]{3,2,1,0:T(8,128)(2,1)S(1)}, bf16[4,2,64,384]{3,2,1,0:T(8,128)(2,1)S(1)}, u32[]{:S(2)}, u32[]{:S(2)}) collective-permute-start(bf16[4,2,64,384]{3,2,1,0:T(8,128)(2,1)S(1)} %get-tuple-element.11), channel_id=1, source_target_pairs={{0,8},{1,9},{2,10},{3,11},{4,12},{5,13},{6,14},{7,15},{8,0},{9,1},... | collective-permute-start | bytes 1179656 | tf_op jit(solution)/shard_map/ppermute | solution.py:46
  117.6 0.8 copy-start.5
  117.6 1.8 copy-start.2
  125.5 33.6 %copy-start.3 = (bf16[4,128,768]{2,1,0:T(8,128)(2,1)S(1)}, bf16[4,128,768]{2,1,0:T(8,128)(2,1)}, u32[]{:S(2)}) copy-start(bf16[4,128,768]{2,1,0:T(8,128)(2,1)} %param.10) | copy-start | bytes 2359300
  155.5 14.6 %all-to-all-start.3 = ((bf16[4,3,32,1024]{3,2,1,0:T(8,128)(2,1)}), bf16[4,3,32,1024]{3,2,1,0:T(8,128)(2,1)S(1)}, u32[]{:S(2)}, u32[]{:S(2)}) async-start(bf16[4,3,32,1024]{3,2,1,0:T(8,128)(2,1)} %broadcast_in_dim.2), calls=%async_computation.3 | async-start | bytes 1572864 | tf_op jit(solution)/shard_map/all_to_all | solution.py:38
  170.1 5.6 %copy-start.4 = (bf16[4,3,32,1024]{3,2,1,0:T(8,128)(2,1)}, bf16[4,3,32,1024]{3,2,1,0:T(8,128)(2,1)S(1)}, u32[]{:S(2)}) copy-start(bf16[4,3,32,1024]{3,2,1,0:T(8,128)(2,1)S(1)} %all-to-all-done.3.w_ref) | copy-start | bytes 2359300
  170.1 18.6 %all-to-all-start.5 = ((bf16[16,32,768]{2,1,0:T(8,128)(2,1)}), bf16[16,32,768]{2,1,0:T(8,128)(2,1)S(1)}, u32[]{:S(2)}, u32[]{:S(2)}) async-start(bf16[16,32,768]{2,1,0:T(8,128)(2,1)} %bitcast.9), calls=%async_computation.5 | async-start | bytes 1572864 | tf_op jit(solution)/shard_map/all_to_all | solution.py:341
  175.7 18.4 %copy-start.6 = (f32[768]{0:T(1024)S(1)}, f32[768]{0:T(1024)}, u32[]{:S(2)}) copy-start(f32[768]{0:T(1024)} %param.14) | copy-start | bytes 9220
  175.7 19.0 %copy-start.7 = (f32[768]{0:T(1024)S(1)}, f32[768]{0:T(1024)}, u32[]{:S(2)}) copy-start(f32[768]{0:T(1024)} %param.17) | copy-start | bytes 9220
  188.7 17.8 %copy-start = (bf16[16,32,768]{2,1,0:T(8,128)(2,1)}, bf16[16,32,768]{2,1,0:T(8,128)(2,1)S(1)}, u32[]{:S(2)}) copy-start(bf16[16,32,768]{2,1,0:T(8,128)(2,1)S(1)} %all-to-all-done.5.x_ref) | copy-start | bytes 2359300
  188.7 17.8 %all-to-all-start.4 = ((bf16[16,2,32,384]{3,2,1,0:T(8,128)(2,1)}), bf16[16,2,32,384]{3,2,1,0:T(8,128)(2,1)S(1)}, u32[]{:S(2)}, u32[]{:S(2)}) async-start(bf16[16,2,32,384]{3,2,1,0:T(8,128)(2,1)} %row_mix.1), calls=%async_computation.4 | async-start | bytes 1572864 | tf_op jit(solution)/shard_map/all_to_all | solution.py:38
  206.5 0.9 copy-start.1
Sparse Core Ops, SparseCore 0:
  27.9 41.6 all-gather.4
  71.2 39.7 all-gather.6

commit v2 on v1

--- a/solution.py
+++ b/solution.py
@@ -20,14 +20,20 @@
 
 
 R2, R4 = range(2), range(4)
-X_RINGS = [[device(xl, y, c, z, xh) for xh in R2 for xl in R2] for y in R4 for c in R2 for z in R4]
 Y_RINGS = [[device(xl, y, c, z, xh) for y in R4] for xl in R2 for c in R2 for z in R4 for xh in R2]
 Z_RINGS = [[device(xl, y, c, z, xh) for z in R4] for xl in R2 for y in R4 for c in R2 for xh in R2]
 PLANES = [[device(xl, y, c, z, xh) for xh in R2 for xl in R2 for y in R4] for c in R2 for z in R4]
-OTHER_CORE = [
-    (device(xl, y, c, z, xh), device(xl, y, 1 - c, z, xh))
-    for xl in R2 for y in R4 for c in R2 for z in R4 for xh in R2
-]
+
+
+def shifts(dx=0, dy=0, dz=0, dc=0):
+    pairs = []
+    for x in R4:
+        for y in R4:
+            for c in R2:
+                for z in R4:
+                    to = ((x + dx) % 4, (y + dy) % 4, (c + dc) % 2, (z + dz) % 4)
+                    pairs.append((device(x % 2, y, c, z, x // 2), device(to[0] % 2, *to[1:], to[0] // 2)))
+    return pairs
 
 
 def params():
@@ -42,8 +48,12 @@
     return lax.all_gather(array, AXES, axis=0, tiled=False, axis_index_groups=groups)
 
 
+def send(array, **by):
+    return lax.ppermute(array, AXES, shifts(**by))
+
+
 def to_other_core(array):
-    return lax.ppermute(array, AXES, OTHER_CORE)
+    return send(array, dc=1)
 
 
 def mm(a, b):
@@ -61,7 +71,11 @@
     return (centred * lax.rsqrt(var + 1e-05) * gain).astype(BF)
 
 
-def write_pairs(normed, weight, out):
+CORE, X, Y, Z = range(4)
+SCALARS = pl.BlockSpec(memory_space=pltpu.SMEM)
+
+
+def write_pieces(place_ref, normed, weight, pieces, outs):
     low = lax.broadcasted_iota(jnp.int32, (128, 128), 1) < E
     for rp in range(2):
         first = mm(normed[2 * rp * 128 : (2 * rp + 1) * 128, :], weight)
@@ -74,84 +88,95 @@
             )
             for k in range(2):
                 g, h = (2 * t + k) // 3, (2 * t + k) % 3
-                out[g, rp, :, h * 128 : (h + 1) * 128] = pair[k].astype(BF)
-
-
-def key_kernel(x_ref, gain_ref, w_ref, normed_ref, out_ref):
-    normed_ref[...] = normalize(x_ref[...].astype(F32), gain_ref[...])
-    write_pairs(normed_ref[...], w_ref[...], out_ref)
-
-
-def key_proj(x, gain, weight):
+                pieces[g, rp, :, h * 128 : (h + 1) * 128] = pair[k].astype(BF)
+    for s, out in enumerate(outs):
+        out[...] = pieces[(place_ref[X] + s) % 4].reshape(out.shape)
+
+
+def key_kernel(place_ref, x_ref, gain_ref, w_ref, normed_ref, *refs):
+    normed_ref[...] = normalize(x_ref[...].astype(F32), gain_ref[...][None, :])
+    write_pieces(place_ref, normed_ref[...], w_ref[...], refs[4], refs[:4])
+
+
+def key_proj(place, x, gain, weight):
+    piece = (2, 128, 384)
     return pl.pallas_call(
         key_kernel,
         grid=(1,),
         in_specs=[
+            SCALARS,
             pl.BlockSpec((512, 768), lambda i: (0, 0)),
-            pl.BlockSpec((1, 768), lambda i: (0, 0)),
+            pl.BlockSpec((768,), lambda i: (0,)),
             pl.BlockSpec((768, 768), lambda i: (0, 1)),
         ],
-        out_specs=[
-            pl.BlockSpec((512, 768), lambda i: (0, 0)),
-            pl.BlockSpec((4, 2, 128, 384), lambda i: (0, 0, 0, 0)),
-        ],
-        out_shape=[
-            jax.ShapeDtypeStruct((512, 768), BF),
-            jax.ShapeDtypeStruct((4, 2, 128, 384), BF),
-        ],
+        out_specs=[pl.BlockSpec((512, 768), lambda i: (0, 0))] + [pl.BlockSpec(piece, lambda i: (0, 0, 0))] * 4,
+        out_shape=[jax.ShapeDtypeStruct((512, 768), BF)] + [jax.ShapeDtypeStruct(piece, BF)] * 4,
+        scratch_shapes=[pltpu.VMEM((4,) + piece, BF)],
         compiler_params=params(),
         name="key_proj",
-    )(x, gain, weight)
-
-
-def query_value_kernel(normed_ref, w_ref, out_ref):
-    write_pairs(normed_ref[...], w_ref[...], out_ref.at[:, 0])
-
-
-def query_value_proj(normed, weight):
+    )(place, x, gain, weight)
+
+
+def query_value_kernel(place_ref, normed_ref, w_ref, *refs):
+    write_pieces(place_ref, normed_ref[...], w_ref[...], refs[4], refs[:4])
+
+
+def query_value_proj(place, normed, weight):
+    piece = (1, 2, 128, 384)
     return pl.pallas_call(
         query_value_kernel,
         grid=(2,),
         in_specs=[
+            SCALARS,
             pl.BlockSpec((512, 768), lambda i: (0, 0)),
             pl.BlockSpec((768, 768), lambda i: (0, 2 * i)),
         ],
-        out_specs=pl.BlockSpec((4, 1, 2, 128, 384), lambda i: (0, i, 0, 0, 0)),
-        out_shape=jax.ShapeDtypeStruct((4, 2, 2, 128, 384), BF),
+        out_specs=[pl.BlockSpec(piece, lambda i: (i, 0, 0, 0))] * 4,
+        out_shape=[jax.ShapeDtypeStruct((2,) + piece[1:], BF)] * 4,
+        scratch_shapes=[pltpu.VMEM((4,) + piece[1:], BF)],
         compiler_params=params(),
         name="query_value_proj",
-    )(normed, weight)
-
-
-def scores_kernel(q0_ref, q1_ref, k0_ref, k1_ref, out_ref):
-    def query(xh):
+    )(place, normed, weight)
+
+
+def over_x(pieces):
+    return [pieces[0], send(pieces[3], dx=3), send(pieces[2], dx=2), send(pieces[1], dx=1)]
+
+
+def scores_kernel(place_ref, q0_ref, q1_ref, *refs):
+    keys, out_ref = refs[:16], refs[16]
+
+    def source(xh, xl):
+        return (xh * 2 + xl + 4 - place_ref[X]) % 4
+
+    def query_rows(xh):
         return jnp.concatenate(
-            [q[xh * 2 + xl, rp] for q in (q0_ref, q1_ref) for xl in range(2) for rp in range(2)], axis=1
+            [q[source(xh, xl), rp] for q in (q0_ref, q1_ref) for xl in range(2) for rp in range(2)], axis=1
         )
 
-    def keys(z, xh):
+    def key_rows(d, xh):
         return jnp.concatenate(
-            [k[z, xh * 2 + xl, rp] for k in (k0_ref, k1_ref) for xl in range(2) for rp in range(2)], axis=1
+            [keys[k * 8 + d * 2 + rp][source(xh, xl)] for k in range(2) for xl in range(2) for rp in range(2)], axis=1
         )
 
-    left = jnp.concatenate([query(0), query(1)], axis=0)
-    for z in range(4):
-        right = jnp.concatenate([keys(z, 0), keys(z, 1)], axis=0)
-        out_ref[:, 0, :, z * 256 : (z + 1) * 256] = mm_t(left, right).reshape(4, 32, 256)
-
-
-def partial_scores(q0, q1, k0, k1):
+    left = jnp.concatenate([query_rows(0), query_rows(1)], axis=0)
+    for d in range(4):
+        right = jnp.concatenate([key_rows(d, 0), key_rows(d, 1)], axis=0)
+        out_ref[:, 0, :, d * 256 : (d + 1) * 256] = mm_t(left, right).reshape(4, 32, 256)
+
+
+def partial_scores(place, q0, q1, k0, k1):
     q_spec = pl.BlockSpec((4, 2, 64, 128), lambda h: (0, 0, 0, h))
-    k_spec = pl.BlockSpec((4, 4, 2, 128, 128), lambda h: (0, 0, 0, 0, h))
+    k_spec = pl.BlockSpec((4, 128, 128), lambda h: (0, 0, h))
     return pl.pallas_call(
         scores_kernel,
         grid=(3,),
-        in_specs=[q_spec, q_spec, k_spec, k_spec],
+        in_specs=[SCALARS, q_spec, q_spec] + [k_spec] * 16,
         out_specs=pl.BlockSpec((4, 1, 32, 1024), lambda h: (0, h, 0, 0)),
         out_shape=jax.ShapeDtypeStruct((4, 3, 32, 1024), F32),
         compiler_params=params(),
         name="partial_scores",
-    )(q0, q1, k0, k1)
+    )(place, q0, q1, *k0, *k1)
 
 
 def softmax_kernel(scale, parts_ref, out_ref):
@@ -172,42 +197,39 @@
     )(parts)
 
 
-def mix_kernel(core_ref, w_ref, v0_ref, v1_ref, out_ref):
-    weights = w_ref[:, 0].reshape(128, 1024)
+def mix_kernel(place_ref, w0_ref, w1_ref, w2_ref, w3_ref, v0_ref, v1_ref, out_ref, weights):
+    for d, w in enumerate((w0_ref, w1_ref, w2_ref, w3_ref)):
+        share = (place_ref[Y] + d) % 4
+        weights[pl.ds(pl.multiple_of(share * 32, 32), 32), :] = w[0]
     for k, v in enumerate((v0_ref, v1_ref)):
-        owner = (core_ref[0] + k) % 2
+        owner = (place_ref[CORE] + k) % 2
         for xl in range(2):
-            right = jnp.concatenate(
-                [
-                    jnp.concatenate([v[z, xh * 2 + xl, 0], v[z, xh * 2 + xl, 1]], axis=1)
-                    for z in range(4)
-                    for xh in range(2)
-                ],
-                axis=0,
-            )
-            mixed = mm(weights, right)
+            right = []
+            for dz in (0, 3, 1, 2):
+                z = (place_ref[Z] + dz) % 4
+                for xh in range(2):
+                    x = (xh * 2 + xl + 4 - place_ref[X]) % 4
+                    right.append(jnp.concatenate([v[z, x, 0], v[z, x, 1]], axis=1))
+            mixed = mm(weights[...], jnp.concatenate(right, axis=0))
             pair = jnp.concatenate(
                 [mixed[:, :128].reshape(16, 8, 128), mixed[:, 128:].reshape(16, 8, 128)], axis=1
             )
             out_ref[:, pl.ds(owner, 1), xl * 16 : (xl + 1) * 16, :] = pair.astype(BF)[:, None]
 
 
-def row_mix(core, weights, v0, v1):
+def row_mix(place, weights, v0, v1):
+    w_spec = pl.BlockSpec((1, 32, 1024), lambda h: (h, 0, 0))
     v_spec = pl.BlockSpec((4, 4, 2, 128, 128), lambda h: (0, 0, 0, 0, h))
     return pl.pallas_call(
         mix_kernel,
         grid=(3,),
-        in_specs=[
-            pl.BlockSpec(memory_space=pltpu.SMEM),
-            pl.BlockSpec((4, 1, 32, 1024), lambda h: (0, h, 0, 0)),
-            v_spec,
-            v_spec,
-        ],
+        in_specs=[SCALARS] + [w_spec] * 4 + [v_spec] * 2,
         out_specs=pl.BlockSpec((16, 2, 32, 128), lambda h: (0, 0, 0, h)),
         out_shape=jax.ShapeDtypeStruct((16, 2, 32, 384), BF),
+        scratch_shapes=[pltpu.VMEM((128, 1024), BF)],
         compiler_params=params(),
         name="row_mix",
-    )(core, weights, v0, v1)
+    )(place, *weights, v0, v1)
 
 
 def column_kernel(
@@ -251,7 +273,7 @@
     token = lax.broadcasted_iota(jnp.int32, (512, 512), 1)
     by_column = ((place % 64) * 8 + place // 64 == token).astype(F32).astype(BF)
     by_token = ((token % 64) * 8 + token // 64 == place).astype(F32).astype(BF)
-    normed = mm(by_column, normalize(stream[...], gain_col_ref[...])).astype(BF)
+    normed = mm(by_column, normalize(stream[...], gain_col_ref[...][None, :])).astype(BF)
     copies[1].wait()
     qkv[...] = mm(normed, attend[...]).astype(BF)
     group = lax.broadcasted_iota(jnp.int32, (256, 256), 0) // E == lax.broadcasted_iota(jnp.int32, (256, 256), 1) // E
@@ -280,7 +302,7 @@
     copies[2].wait()
     stream[...] += mm(mixed, exit_col[...])
 
-    normed = normalize(stream[...], gain_ffn_ref[...])
+    normed = normalize(stream[...], gain_ffn_ref[...][None, :])
     copies[3].wait()
     copies[4].wait()
     for f in range(6):
@@ -325,32 +347,42 @@
     expand,
     shrink,
 ):
-    core = lax.axis_index("seq") % 2
+    seq, col = lax.axis_index("seq"), lax.axis_index("col")
+    core, y, z = seq % 2, seq // 2 % 4, col // 2
+    place = jnp.stack([core, col % 2 * 2 + seq // 8, y, z]).astype(jnp.int32)
     scale = E ** (-0.5) / math.sqrt(embeddings.shape[0] * lax.axis_size("seq"))
 
-    normed, keys = key_proj(embeddings.reshape(512, 768), gain_row.reshape(1, 768), attend_row)
-    keys = swap(keys, X_RINGS)
-    keys0 = gather(keys, Z_RINGS)
-    queries_values = swap(query_value_proj(normed, attend_row), X_RINGS)
-    queries, values = queries_values[:, 0], queries_values[:, 1]
+    normed, *keys = key_proj(place, embeddings.reshape(512, 768), gain_row, attend_row)
+    keys = over_x(keys)
+    queries_values = query_value_proj(place, normed, attend_row)
+    x = embeddings.reshape(4, 2, 8, 8, 768).transpose(2, 1, 0, 3, 4).reshape(16, 32, 768)
+    even, odd = (jnp.stack([k[rp] for k in keys]) for rp in range(2))
+    even, odd, x, queries_values = lax.optimization_barrier((even, odd, x, queries_values))
+
+    even_below, odd_above = send(even, dz=1), send(odd, dz=3)
+    odd_below, even_above = send(odd, dz=1), send(even, dz=3)
+    queries_values = over_x(queries_values)
+    x = lax.all_to_all(x, "seq", split_axis=0, concat_axis=0, tiled=True)
+    even_below, odd_above, x = lax.optimization_barrier((even_below, odd_above, x))
+    even_far, odd_far = send(even_below, dz=1), send(odd_above, dz=3)
+    keys0 = [even, odd, even_below, odd_below, even_above, odd_above, even_far, odd_far]
+    keys1 = [to_other_core(k) for k in keys0]
+
+    queries = jnp.stack([qv[0] for qv in queries_values])
+    values = jnp.stack([qv[1] for qv in queries_values])
     queries0 = lax.dynamic_slice_in_dim(queries, core * 64, 64, axis=2)
     queries1 = to_other_core(lax.dynamic_slice_in_dim(queries, (1 - core) * 64, 64, axis=2))
+    values, keys0[6], keys0[7] = lax.optimization_barrier((values, keys0[6], keys0[7]))
     values0 = gather(values, Z_RINGS)
 
-    x = embeddings.reshape(4, 2, 8, 8, 768).transpose(2, 1, 0, 3, 4).reshape(16, 32, 768)
-    x = lax.all_to_all(x, "seq", split_axis=0, concat_axis=0, tiled=True)
-
-    keys1 = to_other_core(keys0)
-    parts = swap(partial_scores(queries0, queries1, keys0, keys1), Y_RINGS)
-    weights = row_softmax(parts, scale)
-    weights = swap(jnp.broadcast_to(weights[None], (4, 3, 32, 1024)), Y_RINGS)
-    values1 = to_other_core(values0)
-    mix = row_mix(core.reshape(1).astype(jnp.int32), weights, values0, values1)
+    scores = partial_scores(place, queries0, queries1, keys0, keys1)
+    weights = row_softmax(swap(scores, Y_RINGS), scale)
+    weights, values0 = lax.optimization_barrier((weights, values0))
+    weights = [weights] + [send(weights, dy=dy) for dy in (3, 2, 1)]
+    mix = row_mix(place, weights, values0, to_other_core(values0))
     mix = swap(mix, PLANES).reshape(16, 64, 384)
 
-    out = column_part(
-        mix, x, gain_col.reshape(1, 768), gain_ffn.reshape(1, 768), exit_row, attend_col, exit_col, expand, shrink
-    )
+    out = column_part(mix, x, gain_col, gain_ffn, exit_row, attend_col, exit_col, expand, shrink)
     out = lax.all_to_all(out, "seq", split_axis=0, concat_axis=0, tiled=True)
     return out.reshape(8, 2, 4, 8, 768).transpose(2, 1, 0, 3, 4).reshape(4, 128, 768)
 

time: 259 us -> 207 us (0.80)
  waiting for transfers between devices: 87.7 us -> 41.3 us
  blocking collectives: 83 us -> 61.4 us
  starting transfers between devices: 15.8 us -> 33.7 us
  local copies, waits for them, and re-layouts: 12.2 us -> 8.2 us
    all_gather x2 -> x1, waiting for transfers between devices: 54.6 us -> 0.01 us  [gather(): lax.all_gather(array, AXES, axis=0, tiled=False, axis_index_groups=groups)]
    ppermute x3 -> x25, waiting for transfers between devices: 3.9 us -> 41.3 us  [send(): return lax.ppermute(array, AXES, shifts(**by))]
    ppermute x3 -> x25, starting transfers between devices: 1.35 us -> 28.7 us  [send(): return lax.ppermute(array, AXES, shifts(**by))]
    all_to_all x2 -> x0, waiting for transfers between devices: 21.3 us -> none  [swap(): lax.all_to_all(array, AXES, split_axis=0, concat_axis=0, tiled=True, axis...]
    all_to_all x3 -> x2, blocking collectives: 63.7 us -> 43.3 us  [swap(): lax.all_to_all(array, AXES, split_axis=0, concat_axis=0, tiled=True, axis...]
    all_to_all x2 -> x0, starting transfers between devices: 8.87 us -> none  [swap(): lax.all_to_all(array, AXES, split_axis=0, concat_axis=0, tiled=True, axis...]
    all_to_all x1, waiting for transfers between devices: 7.86 us -> 0.01 us  [local(): x = lax.all_to_all(x, 'seq', split_axis=0, concat_axis=0, tiled=True)]
  transfers between devices with their start and end apart: 8 -> 27, of which waited for: 6 -> 15; matrix products, arithmetic and copies ran while one was open for 3% -> 3% of each run, Pallas kernels for 7% -> 7%
where the time goes in v2:
time: 207 us
  blocking collectives  61.4 us (30%)
  Pallas kernels  46.6 us (23%)
  waiting for transfers between devices  41.3 us (20%)
  starting transfers between devices  33.7 us (16%)
  between operations  13.6 us (7%)
  local copies, waits for them, and re-layouts  8.2 us (4%)
    all_to_all x2, blocking collectives, swap(): lax.all_to_all(array, AXES, split_axis=0, concat_axis=0, tiled=True, axis...  43.3 us
    ppermute x25, waiting for transfers between devices, send(): return lax.ppermute(array, AXES, shifts(**by))  41.3 us
    ppermute x25, starting transfers between devices, send(): return lax.ppermute(array, AXES, shifts(**by))  28.7 us
    pallas_call x1, Pallas kernels, column_part(): pl.pallas_call(column_kernel, in_specs=[whole] * 4 + [hbm] * 5, out_specs...  24 us
    all_to_all x1, blocking collectives, local(): out = lax.all_to_all(out, 'seq', split_axis=0, concat_axis=0, tiled=True)  18.1 us
    pallas_call x1, Pallas kernels, partial_scores(): pl.pallas_call(scores_kernel, grid=(3,), in_specs=[SCALARS, q_spec, q_spe...  6.29 us
    pallas_call x1, Pallas kernels, row_mix(): pl.pallas_call(mix_kernel, grid=(3,), in_specs=[SCALARS] + [w_spec] * 4 +...  5.21 us
    all_to_all x1, starting transfers between devices, local(): x = lax.all_to_all(x, 'seq', split_axis=0, concat_axis=0, tiled=True)  4.99 us
  transfers between devices with their start and end apart: 27, of which 15 were waited for; matrix products, arithmetic and copies ran while one was open for 3% of the time, Pallas kernels for 7%

profile of v2, /device:TPU:1, one launch (start us, length us, event | category | flops | bytes accessed | tf_op | source)
XLA Modules:
  0.0 206.6 jit_solution(16865219775291236377)
XLA Ops:
  7.1 3.6 %key_proj.1 = (bf16[512,768]{1,0:T(8,128)(2,1)}, bf16[2,128,384]{2,1,0:T(8,128)(2,1)}, bf16[2,128,384]{2,1,0:T(8,128)(2,1)}, bf16[2,128,384]{2,1,0:T(8,128)(2,1)}, bf16[2,128,384]{2,1,0:T(8,128)(2,1)}) custom-call(s32[4]{0:T(128)} %pad_add_fusion.place_ref, bf16[512,768]{1,0:T(8,128)(2,1)} %bitcast.19, f32[768]{0:T(1024)} %gain_ref.1, bf16[768,2304]{1,0:T(8,128)(2,1)} %w_ref.3), custom_call_target="tpu_custom_call" | custom-call | tf_op jit(solution)/shard_map/key_proj/pallas_call | solution.py:103
  10.7 3.3 %collective-permute-start = (bf16[2,128,384]{2,1,0:T(8,128)(2,1)}, bf16[2,128,384]{2,1,0:T(8,128)(2,1)S(1)}, u32[]{:S(2)}, u32[]{:S(2)}) collective-permute-start(bf16[2,128,384]{2,1,0:T(8,128)(2,1)} %get-tuple-element.30), channel_id=1, source_target_pairs={{0,65},{2,67},{4,69},{6,71},{8,73},{10,75},{12,77},{14,79},{16,81}... | collective-permute-start | bytes 589832 | tf_op jit(solution)/shard_map/ppermute | solution.py:52
  15.2 4.3 %query_value_proj.1 = (bf16[2,2,128,384]{3,2,1,0:T(8,128)(2,1)}, bf16[2,2,128,384]{3,2,1,0:T(8,128)(2,1)}, bf16[2,2,128,384]{3,2,1,0:T(8,128)(2,1)}, bf16[2,2,128,384]{3,2,1,0:T(8,128)(2,1)}) custom-call(s32[4]{0:T(128)} %pad_add_fusion.place_ref, bf16[512,768]{1,0:T(8,128)(2,1)} %get-tuple-element.33.normed_ref, bf16[768,2304]{1,0:T(8,128)(2,1)} %w_ref.3), custom_call_target="tpu_custom_call" | custom-call | tf_op jit(solution)/shard_map/query_value_proj/pallas_call | solution.py:126
  21.3 5.5 %collective-permute-done.2 = bf16[2,128,384]{2,1,0:T(8,128)(2,1)S(1)} collective-permute-done((bf16[2,128,384]{2,1,0:T(8,128)(2,1)}, bf16[2,128,384]{2,1,0:T(8,128)(2,1)S(1)}, u32[]{:S(2)}, u32[]{:S(2)}) %collective-permute-start.2) | collective-permute-done | bytes 196640 | tf_op jit(solution)/shard_map/ppermute | solution.py:52
  27.0 5.0 %all-to-all-start = ((bf16[16,32,768]{2,1,0:T(8,128)(2,1)}), bf16[16,32,768]{2,1,0:T(8,128)(2,1)S(1)}, u32[]{:S(2)}, u32[]{:S(2)}) async-start(bf16[16,32,768]{2,1,0:T(8,128)(2,1)} %bitcast.7), calls=%async_computation | async-start | bytes 1572864 | tf_op jit(solution)/shard_map/all_to_all | solution.py:365
  32.0 1.5 collective-permute-start.3
  33.5 1.7 collective-permute-start.4
  35.3 1.6 collective-permute-start.7
  36.9 2.1 %collective-permute-start.8 = (bf16[4,128,384]{2,1,0:T(8,128)(2,1)S(1)}, bf16[4,128,384]{2,1,0:T(8,128)(2,1)S(1)}, u32[]{:S(2)}, u32[]{:S(2)}) collective-permute-start(bf16[4,128,384]{2,1,0:T(8,128)(2,1)S(1)} %get-tuple-element.43.refs_1_), channel_id=1, source_target_pairs={{0,6},{2,0},{4,2},{6,4},{8,14},{10,8},{12,10},{14,12},{16,22},{18,... | collective-permute-start | bytes 1179656 | tf_op jit(solution)/shard_map/ppermute | solution.py:52
  39.1 12.3 %collective-permute-done.3 = bf16[2,2,128,384]{3,2,1,0:T(8,128)(2,1)S(1)} collective-permute-done((bf16[2,2,128,384]{3,2,1,0:T(8,128)(2,1)}, bf16[2,2,128,384]{3,2,1,0:T(8,128)(2,1)S(1)}, u32[]{:S(2)}, u32[]{:S(2)}) %collective-permute-start.3) | collective-permute-done | bytes 393248 | tf_op jit(solution)/shard_map/ppermute | solution.py:52
  51.5 1.7 collective-permute-start.11
  53.2 2.2 %collective-permute-start.12 = (bf16[4,128,384]{2,1,0:T(8,128)(2,1)S(1)}, bf16[4,128,384]{2,1,0:T(8,128)(2,1)}, u32[]{:S(2)}, u32[]{:S(2)}) collective-permute-start(bf16[4,128,384]{2,1,0:T(8,128)(2,1)S(1)} %collective-permute-done.8.refs_5_), channel_id=1, source_target_pairs={{0,6},{2,0},{4,2},{6,4},{8,14},{10,8},{12,10},{14,12},{16,22},{18,... | collective-permute-start | bytes 1179656 | tf_op jit(solution)/shard_map/ppermute | solution.py:52
  56.4 1.6 collective-permute-done.5
  60.1 3.5 %collective-permute-done.11.refs_6_ = bf16[4,128,384]{2,1,0:T(8,128)(2,1)} collective-permute-done((bf16[4,128,384]{2,1,0:T(8,128)(2,1)S(1)}, bf16[4,128,384]{2,1,0:T(8,128)(2,1)}, u32[]{:S(2)}, u32[]{:S(2)}) %collective-permute-start.11) | collective-permute-done | bytes 393248 | tf_op jit(solution)/shard_map/ppermute | solution.py:52
  64.1 2.3 %collective-permute-start.10 = (bf16[4,128,384]{2,1,0:T(8,128)(2,1)S(1)}, bf16[4,128,384]{2,1,0:T(8,128)(2,1)S(1)}, u32[]{:S(2)}, u32[]{:S(2)}) collective-permute-start(bf16[4,128,384]{2,1,0:T(8,128)(2,1)S(1)} %get-tuple-element.42.refs_0_), channel_id=1, source_target_pairs={{0,6},{2,0},{4,2},{6,4},{8,14},{10,8},{12,10},{14,12},{16,22},{18,... | collective-permute-start | bytes 1179656 | tf_op jit(solution)/shard_map/ppermute | solution.py:52
  66.4 2.4 %collective-permute-start.13 = (bf16[4,128,384]{2,1,0:T(8,128)(2,1)S(1)}, bf16[4,128,384]{2,1,0:T(8,128)(2,1)S(1)}, u32[]{:S(2)}, u32[]{:S(2)}) collective-permute-start(bf16[4,128,384]{2,1,0:T(8,128)(2,1)S(1)} %get-tuple-element.42.refs_0_), channel_id=1, source_target_pairs={{0,8},{2,10},{4,12},{6,14},{8,0},{10,2},{12,4},{14,6},{16,24},{18,... | collective-permute-start | bytes 1179656 | tf_op jit(solution)/shard_map/ppermute | solution.py:52
  70.3 3.3 %collective-permute-done.9.refs_3_ = bf16[4,128,384]{2,1,0:T(8,128)(2,1)S(1)} collective-permute-done((bf16[4,128,384]{2,1,0:T(8,128)(2,1)S(1)}, bf16[4,128,384]{2,1,0:T(8,128)(2,1)S(1)}, u32[]{:S(2)}, u32[]{:S(2)}) %collective-permute-start.9) | collective-permute-done | bytes 393248 | tf_op jit(solution)/shard_map/ppermute | solution.py:52
  73.6 2.8 %collective-permute-start.16 = (bf16[4,128,384]{2,1,0:T(8,128)(2,1)S(1)}, bf16[4,128,384]{2,1,0:T(8,128)(2,1)S(1)}, u32[]{:S(2)}, u32[]{:S(2)}) collective-permute-start(bf16[4,128,384]{2,1,0:T(8,128)(2,1)S(1)} %collective-permute-done.9.refs_3_), channel_id=1, source_target_pairs={{0,8},{2,10},{4,12},{6,14},{8,0},{10,2},{12,4},{14,6},{16,24},{18,... | collective-permute-start | bytes 1179656 | tf_op jit(solution)/shard_map/ppermute | solution.py:52
  78.9 1.1 collective-permute-done.18.refs_13_
  81.6 6.3 %partial_scores.1 = f32[4,3,32,1024]{3,2,1,0:T(8,128)} custom-call(s32[4]{0:T(128)} %pad_add_fusion.place_ref, bf16[4,2,64,384]{3,2,1,0:T(8,128)(2,1)} %get-tuple-element.54.q0_ref, bf16[4,2,64,384]{3,2,1,0:T(8,128)(2,1)} %copy-done.11, bf16[4,128,384]{2,1,0:T(8,128)(2,1)} %copy-done.3, bf16[4,128,384]{2,1,0:T(8,128)(2,1)} %copy-done.4, ...), custom_call_target="tpu_custom_call" | custom-call | tf_op jit(solution)/shard_map/partial_scores/pallas_call | solution.py:171
  87.9 24.9 %all_to_all.20.refs_0_ = f32[4,3,32,1024]{3,2,1,0:T(8,128)} all-to-all(f32[4,3,32,1024]{3,2,1,0:T(8,128)} %partial_scores.1), channel_id=1, replica_groups={{0,16,32,48},{1,17,33,49},{2,18,34,50},{3,19,35,51},{4,20,36,52},{5,21,..., dimensions={0} | all-to-all | bytes 3145728 | tf_op jit(solution)/shard_map/all_to_all | solution.py:44
  112.7 3.2 %row_softmax.1.w0_ref = bf16[3,32,1024]{2,1,0:T(8,128)(2,1)} custom-call(f32[4,3,32,1024]{3,2,1,0:T(8,128)} %all_to_all.20.refs_0_), custom_call_target="tpu_custom_call" | custom-call | tf_op jit(solution)/shard_map/row_softmax/pallas_call | solution.py:189
  115.9 1.2 collective-permute-start.24
  118.0 1.2 collective-permute-start.22
  119.2 4.7 %collective-permute-done.21.w1_ref = bf16[3,32,1024]{2,1,0:T(8,128)(2,1)S(1)} collective-permute-done((bf16[3,32,1024]{2,1,0:T(8,128)(2,1)}, bf16[3,32,1024]{2,1,0:T(8,128)(2,1)S(1)}, u32[]{:S(2)}, u32[]{:S(2)}) %collective-permute-start.21) | collective-permute-done | bytes 196640 | tf_op jit(solution)/shard_map/ppermute | solution.py:52
  123.9 2.1 %collective-permute-done.22.w2_ref = bf16[3,32,1024]{2,1,0:T(8,128)(2,1)S(1)} collective-permute-done((bf16[3,32,1024]{2,1,0:T(8,128)(2,1)}, bf16[3,32,1024]{2,1,0:T(8,128)(2,1)S(1)}, u32[]{:S(2)}, u32[]{:S(2)}) %collective-permute-start.22) | collective-permute-done | bytes 196640 | tf_op jit(solution)/shard_map/ppermute | solution.py:52
  126.0 4.8 %collective-permute-done.23.w3_ref = bf16[3,32,1024]{2,1,0:T(8,128)(2,1)S(1)} collective-permute-done((bf16[3,32,1024]{2,1,0:T(8,128)(2,1)}, bf16[3,32,1024]{2,1,0:T(8,128)(2,1)S(1)}, u32[]{:S(2)}, u32[]{:S(2)}) %collective-permute-start.23) | collective-permute-done | bytes 196640 | tf_op jit(solution)/shard_map/ppermute | solution.py:52
  131.4 1.7 copy-done.1
  133.1 5.2 %row_mix.1 = bf16[16,2,32,384]{3,2,1,0:T(8,128)(2,1)} custom-call(s32[4]{0:T(128)} %pad_add_fusion.place_ref, bf16[3,32,1024]{2,1,0:T(8,128)(2,1)} %row_softmax.1.w0_ref, bf16[3,32,1024]{2,1,0:T(8,128)(2,1)} %copy-done.20, bf16[3,32,1024]{2,1,0:T(8,128)(2,1)} %copy-done.21, bf16[3,32,1024]{2,1,0:T(8,128)(2,1)} %copy-done.22, ...), custom_call_target="tpu_custom_call" | custom-call | tf_op jit(solution)/shard_map/row_mix/pallas_call | solution.py:223
  138.3 18.4 %all_to_all.21 = bf16[16,2,32,384]{3,2,1,0:T(8,128)(2,1)} all-to-all(bf16[16,2,32,384]{3,2,1,0:T(8,128)(2,1)} %row_mix.1), channel_id=1, replica_groups={{0,16,32,48,64,80,96,112,1,17,33,49,65,81,97,113},{2,18,34,50,66,82,98,..., dimensions={0} | all-to-all | bytes 1572864 | tf_op jit(solution)/shard_map/all_to_all | solution.py:44
  156.7 24.0 %column_part.1 = bf16[16,32,768]{2,1,0:T(8,128)(2,1)} custom-call(bf16[16,64,384]{2,1,0:T(8,128)(2,1)} %bitcast.15, bf16[16,32,768]{2,1,0:T(8,128)(2,1)} %copy-done, f32[768]{0:T(1024)} %gain_col_ref.1, f32[768]{0:T(1024)} %gain_ffn_ref.1, bf16[768,768]{1,0:T(8,128)(2,1)} %exit_row_hbm.1, bf16[768,2304]{1,0:T(8,128)(2,1)} %attend_hbm.1, ...), custom_call_target="tpu_custom_call" | custom-call | tf_op jit(solution)/shard_map/column_part/pallas_call | solution.py:321
  180.7 18.1 %all_to_all.22 = bf16[16,32,768]{2,1,0:T(8,128)(2,1)S(1)} all-to-all(bf16[16,32,768]{2,1,0:T(8,128)(2,1)} %column_part.1), channel_id=1, replica_groups=mesh['seq'=16,'col'=8] {'seq'}, dimensions={0} | all-to-all | bytes 1572864 | tf_op jit(solution)/shard_map/all_to_all | solution.py:386
  (93 shorter events, 15.4 us)
Async XLA Ops:
  10.7 9.8 %collective-permute-start = (bf16[2,128,384]{2,1,0:T(8,128)(2,1)}, bf16[2,128,384]{2,1,0:T(8,128)(2,1)S(1)}, u32[]{:S(2)}, u32[]{:S(2)}) collective-permute-start(bf16[2,128,384]{2,1,0:T(8,128)(2,1)} %get-tuple-element.30), channel_id=1, source_target_pairs={{0,65},{2,67},{4,69},{6,71},{8,73},{10,75},{12,77},{14,79},{16,81}... | collective-permute-start | bytes 589832 | tf_op jit(solution)/shard_map/ppermute | solution.py:52
  14.1 7.2 %collective-permute-start.1 = (bf16[2,128,384]{2,1,0:T(8,128)(2,1)}, bf16[2,128,384]{2,1,0:T(8,128)(2,1)S(1)}, u32[]{:S(2)}, u32[]{:S(2)}) collective-permute-start(bf16[2,128,384]{2,1,0:T(8,128)(2,1)} %get-tuple-element.31), channel_id=1, source_target_pairs={{0,1},{2,3},{4,5},{6,7},{8,9},{10,11},{12,13},{14,15},{16,17},{18,... | collective-permute-start | bytes 589832 | tf_op jit(solution)/shard_map/ppermute | solution.py:52
  14.6 12.2 %collective-permute-start.2 = (bf16[2,128,384]{2,1,0:T(8,128)(2,1)}, bf16[2,128,384]{2,1,0:T(8,128)(2,1)S(1)}, u32[]{:S(2)}, u32[]{:S(2)}) collective-permute-start(bf16[2,128,384]{2,1,0:T(8,128)(2,1)} %get-tuple-element.32), channel_id=1, source_target_pairs={{0,64},{2,66},{4,68},{6,70},{8,72},{10,74},{12,76},{14,78},{16,80}... | collective-permute-start | bytes 589832 | tf_op jit(solution)/shard_map/ppermute | solution.py:52
  19.5 19.5 %copy-start.18 = (bf16[2,2,128,384]{3,2,1,0:T(8,128)(2,1)S(1)}, bf16[2,2,128,384]{3,2,1,0:T(8,128)(2,1)}, u32[]{:S(2)}) copy-start(bf16[2,2,128,384]{3,2,1,0:T(8,128)(2,1)} %get-tuple-element.38) | copy-start | bytes 1179652
  27.0 39.4 %copy-start.3 = (bf16[4,128,384]{2,1,0:T(8,128)(2,1)}, bf16[4,128,384]{2,1,0:T(8,128)(2,1)S(1)}, u32[]{:S(2)}) copy-start(bf16[4,128,384]{2,1,0:T(8,128)(2,1)S(1)} %get-tuple-element.42.refs_0_) | copy-start | bytes 1179652
  27.0 41.8 %copy-start.4 = (bf16[4,128,384]{2,1,0:T(8,128)(2,1)}, bf16[4,128,384]{2,1,0:T(8,128)(2,1)S(1)}, u32[]{:S(2)}) copy-start(bf16[4,128,384]{2,1,0:T(8,128)(2,1)S(1)} %get-tuple-element.43.refs_1_) | copy-start | bytes 1179652
  27.0 24.4 %all-to-all-start = ((bf16[16,32,768]{2,1,0:T(8,128)(2,1)}), bf16[16,32,768]{2,1,0:T(8,128)(2,1)S(1)}, u32[]{:S(2)}, u32[]{:S(2)}) async-start(bf16[16,32,768]{2,1,0:T(8,128)(2,1)} %bitcast.7), calls=%async_computation | async-start | bytes 1572864 | tf_op jit(solution)/shard_map/all_to_all | solution.py:365
  32.0 83.9 %all-gather.3.cloned.1.call-start = ((), (), s32[]{:S(2)}) async-start(), calls=%async_computation.4 | async-start | bytes 3932160 | tf_op jit(solution)/shard_map/all_gather | solution.py:48
  32.0 19.3 %collective-permute-start.3 = (bf16[2,2,128,384]{3,2,1,0:T(8,128)(2,1)}, bf16[2,2,128,384]{3,2,1,0:T(8,128)(2,1)S(1)}, u32[]{:S(2)}, u32[]{:S(2)}) collective-permute-start(bf16[2,2,128,384]{3,2,1,0:T(8,128)(2,1)} %get-tuple-element.39), channel_id=1, source_target_pairs={{0,65},{2,67},{4,69},{6,71},{8,73},{10,75},{12,77},{14,79},{16,81}... | collective-permute-start | bytes 1179656 | tf_op jit(solution)/shard_map/ppermute | solution.py:52
  33.5 21.8 %collective-permute-start.4 = (bf16[2,2,128,384]{3,2,1,0:T(8,128)(2,1)}, bf16[2,2,128,384]{3,2,1,0:T(8,128)(2,1)}, u32[]{:S(2)}, u32[]{:S(2)}) collective-permute-start(bf16[2,2,128,384]{3,2,1,0:T(8,128)(2,1)} %get-tuple-element.40), channel_id=1, source_target_pairs={{0,1},{2,3},{4,5},{6,7},{8,9},{10,11},{12,13},{14,15},{16,17},{18,... | collective-permute-start | bytes 1179656 | tf_op jit(solution)/shard_map/ppermute | solution.py:52
  35.3 22.8 %collective-permute-start.5 = (bf16[2,2,128,384]{3,2,1,0:T(8,128)(2,1)}, bf16[2,2,128,384]{3,2,1,0:T(8,128)(2,1)}, u32[]{:S(2)}, u32[]{:S(2)}) collective-permute-start(bf16[2,2,128,384]{3,2,1,0:T(8,128)(2,1)} %get-tuple-element.41), channel_id=1, source_target_pairs={{0,64},{2,66},{4,68},{6,70},{8,72},{10,74},{12,76},{14,78},{16,80}... | collective-permute-start | bytes 1179656 | tf_op jit(solution)/shard_map/ppermute | solution.py:52
  35.3 16.1 %collective-permute-start.7 = (bf16[4,128,384]{2,1,0:T(8,128)(2,1)S(1)}, bf16[4,128,384]{2,1,0:T(8,128)(2,1)S(1)}, u32[]{:S(2)}, u32[]{:S(2)}) collective-permute-start(bf16[4,128,384]{2,1,0:T(8,128)(2,1)S(1)} %get-tuple-element.42.refs_0_), channel_id=1, source_target_pairs={{0,2},{2,4},{4,6},{6,0},{8,10},{10,12},{12,14},{14,8},{16,18},{18,... | collective-permute-start | bytes 1179656 | tf_op jit(solution)/shard_map/ppermute | solution.py:52
  36.9 14.5 %collective-permute-start.8 = (bf16[4,128,384]{2,1,0:T(8,128)(2,1)S(1)}, bf16[4,128,384]{2,1,0:T(8,128)(2,1)S(1)}, u32[]{:S(2)}, u32[]{:S(2)}) collective-permute-start(bf16[4,128,384]{2,1,0:T(8,128)(2,1)S(1)} %get-tuple-element.43.refs_1_), channel_id=1, source_target_pairs={{0,6},{2,0},{4,2},{6,4},{8,14},{10,8},{12,10},{14,12},{16,22},{18,... | collective-permute-start | bytes 1179656 | tf_op jit(solution)/shard_map/ppermute | solution.py:52
  51.4 25.1 %copy-start.5 = (bf16[4,128,384]{2,1,0:T(8,128)(2,1)}, bf16[4,128,384]{2,1,0:T(8,128)(2,1)S(1)}, u32[]{:S(2)}) copy-start(bf16[4,128,384]{2,1,0:T(8,128)(2,1)S(1)} %collective-permute-done.7.refs_2_) | copy-start | bytes 1179652
  51.4 25.6 %copy-start.6 = (bf16[4,128,384]{2,1,0:T(8,128)(2,1)}, bf16[4,128,384]{2,1,0:T(8,128)(2,1)S(1)}, u32[]{:S(2)}) copy-start(bf16[4,128,384]{2,1,0:T(8,128)(2,1)S(1)} %collective-permute-done.8.refs_5_) | copy-start | bytes 1179652
  51.5 12.1 %collective-permute-start.11 = (bf16[4,128,384]{2,1,0:T(8,128)(2,1)S(1)}, bf16[4,128,384]{2,1,0:T(8,128)(2,1)}, u32[]{:S(2)}, u32[]{:S(2)}) collective-permute-start(bf16[4,128,384]{2,1,0:T(8,128)(2,1)S(1)} %collective-permute-done.7.refs_2_), channel_id=1, source_target_pairs={{0,2},{2,4},{4,6},{6,0},{8,10},{10,12},{12,14},{14,8},{16,18},{18,... | collective-permute-start | bytes 1179656 | tf_op jit(solution)/shard_map/ppermute | solution.py:52
  53.2 10.4 %collective-permute-start.12 = (bf16[4,128,384]{2,1,0:T(8,128)(2,1)S(1)}, bf16[4,128,384]{2,1,0:T(8,128)(2,1)}, u32[]{:S(2)}, u32[]{:S(2)}) collective-permute-start(bf16[4,128,384]{2,1,0:T(8,128)(2,1)S(1)} %collective-permute-done.8.refs_5_), channel_id=1, source_target_pairs={{0,6},{2,0},{4,2},{6,4},{8,14},{10,8},{12,10},{14,12},{16,22},{18,... | collective-permute-start | bytes 1179656 | tf_op jit(solution)/shard_map/ppermute | solution.py:52
  63.6 10.0 %collective-permute-start.9 = (bf16[4,128,384]{2,1,0:T(8,128)(2,1)S(1)}, bf16[4,128,384]{2,1,0:T(8,128)(2,1)S(1)}, u32[]{:S(2)}, u32[]{:S(2)}) collective-permute-start(bf16[4,128,384]{2,1,0:T(8,128)(2,1)S(1)} %get-tuple-element.43.refs_1_), channel_id=1, source_target_pairs={{0,2},{2,4},{4,6},{6,0},{8,10},{10,12},{12,14},{14,8},{16,18},{18,... | collective-permute-start | bytes 1179656 | tf_op jit(solution)/shard_map/ppermute | solution.py:52
  64.1 12.3 %collective-permute-start.10 = (bf16[4,128,384]{2,1,0:T(8,128)(2,1)S(1)}, bf16[4,128,384]{2,1,0:T(8,128)(2,1)S(1)}, u32[]{:S(2)}, u32[]{:S(2)}) collective-permute-start(bf16[4,128,384]{2,1,0:T(8,128)(2,1)S(1)} %get-tuple-element.42.refs_0_), channel_id=1, source_target_pairs={{0,6},{2,0},{4,2},{6,4},{8,14},{10,8},{12,10},{14,12},{16,22},{18,... | collective-permute-start | bytes 1179656 | tf_op jit(solution)/shard_map/ppermute | solution.py:52
  66.4 10.2 %collective-permute-start.13 = (bf16[4,128,384]{2,1,0:T(8,128)(2,1)S(1)}, bf16[4,128,384]{2,1,0:T(8,128)(2,1)S(1)}, u32[]{:S(2)}, u32[]{:S(2)}) collective-permute-start(bf16[4,128,384]{2,1,0:T(8,128)(2,1)S(1)} %get-tuple-element.42.refs_0_), channel_id=1, source_target_pairs={{0,8},{2,10},{4,12},{6,14},{8,0},{10,2},{12,4},{14,6},{16,24},{18,... | collective-permute-start | bytes 1179656 | tf_op jit(solution)/shard_map/ppermute | solution.py:52
  68.8 8.2 %collective-permute-start.14 = (bf16[4,128,384]{2,1,0:T(8,128)(2,1)S(1)}, bf16[4,128,384]{2,1,0:T(8,128)(2,1)S(1)}, u32[]{:S(2)}, u32[]{:S(2)}) collective-permute-start(bf16[4,128,384]{2,1,0:T(8,128)(2,1)S(1)} %get-tuple-element.43.refs_1_), channel_id=1, source_target_pairs={{0,8},{2,10},{4,12},{6,14},{8,0},{10,2},{12,4},{14,6},{16,24},{18,... | collective-permute-start | bytes 1179656 | tf_op jit(solution)/shard_map/ppermute | solution.py:52
  69.9 7.3 %collective-permute-start.6 = (bf16[4,2,64,384]{3,2,1,0:T(8,128)(2,1)S(1)}, bf16[4,2,64,384]{3,2,1,0:T(8,128)(2,1)S(1)}, u32[]{:S(2)}, u32[]{:S(2)}) collective-permute-start(bf16[4,2,64,384]{3,2,1,0:T(8,128)(2,1)S(1)} %get-tuple-element.53), channel_id=1, source_target_pairs={{0,8},{2,10},{4,12},{6,14},{8,0},{10,2},{12,4},{14,6},{16,24},{18,... | collective-permute-start | bytes 1179656 | tf_op jit(solution)/shard_map/ppermute | solution.py:52
  73.6 4.1 %collective-permute-start.16 = (bf16[4,128,384]{2,1,0:T(8,128)(2,1)S(1)}, bf16[4,128,384]{2,1,0:T(8,128)(2,1)S(1)}, u32[]{:S(2)}, u32[]{:S(2)}) collective-permute-start(bf16[4,128,384]{2,1,0:T(8,128)(2,1)S(1)} %collective-permute-done.9.refs_3_), channel_id=1, source_target_pairs={{0,8},{2,10},{4,12},{6,14},{8,0},{10,2},{12,4},{14,6},{16,24},{18,... | collective-permute-start | bytes 1179656 | tf_op jit(solution)/shard_map/ppermute | solution.py:52
  76.4 1.9 collective-permute-start.17
  76.5 2.4 %collective-permute-start.15 = (bf16[4,128,384]{2,1,0:T(8,128)(2,1)S(1)}, bf16[4,128,384]{2,1,0:T(8,128)(2,1)S(1)}, u32[]{:S(2)}, u32[]{:S(2)}) collective-permute-start(bf16[4,128,384]{2,1,0:T(8,128)(2,1)S(1)} %collective-permute-done.7.refs_2_), channel_id=1, source_target_pairs={{0,8},{2,10},{4,12},{6,14},{8,0},{10,2},{12,4},{14,6},{16,24},{18,... | collective-permute-start | bytes 1179656 | tf_op jit(solution)/shard_map/ppermute | solution.py:52
  77.0 3.0 %collective-permute-start.18 = (bf16[4,128,384]{2,1,0:T(8,128)(2,1)S(1)}, bf16[4,128,384]{2,1,0:T(8,128)(2,1)S(1)}, u32[]{:S(2)}, u32[]{:S(2)}) collective-permute-start(bf16[4,128,384]{2,1,0:T(8,128)(2,1)S(1)} %collective-permute-done.8.refs_5_), channel_id=1, source_target_pairs={{0,8},{2,10},{4,12},{6,14},{8,0},{10,2},{12,4},{14,6},{16,24},{18,... | collective-permute-start | bytes 1179656 | tf_op jit(solution)/shard_map/ppermute | solution.py:52
  77.2 3.0 %collective-permute-start.19 = (bf16[4,128,384]{2,1,0:T(8,128)(2,1)}, bf16[4,128,384]{2,1,0:T(8,128)(2,1)S(1)}, u32[]{:S(2)}, u32[]{:S(2)}) collective-permute-start(bf16[4,128,384]{2,1,0:T(8,128)(2,1)} %collective-permute-done.11.refs_6_), channel_id=1, source_target_pairs={{0,8},{2,10},{4,12},{6,14},{8,0},{10,2},{12,4},{14,6},{16,24},{18,... | collective-permute-start | bytes 1179656 | tf_op jit(solution)/shard_map/ppermute | solution.py:52
  77.8 3.0 %collective-permute-start.20 = (bf16[4,128,384]{2,1,0:T(8,128)(2,1)}, bf16[4,128,384]{2,1,0:T(8,128)(2,1)S(1)}, u32[]{:S(2)}, u32[]{:S(2)}) collective-permute-start(bf16[4,128,384]{2,1,0:T(8,128)(2,1)} %collective-permute-done.12.refs_7_), channel_id=1, source_target_pairs={{0,8},{2,10},{4,12},{6,14},{8,0},{10,2},{12,4},{14,6},{16,24},{18,... | collective-permute-start | bytes 1179656 | tf_op jit(solution)/shard_map/ppermute | solution.py:52
  115.9 14.8 %collective-permute-start.24 = (bf16[4,4,2,128,384]{4,3,2,1,0:T(8,128)(2,1)}, bf16[4,4,2,128,384]{4,3,2,1,0:T(8,128)(2,1)S(1)}, u32[]{:S(2)}, u32[]{:S(2)}) collective-permute-start(bf16[4,4,2,128,384]{4,3,2,1,0:T(8,128)(2,1)} %bitcast.17), channel_id=1, source_target_pairs={{0,8},{2,10},{4,12},{6,14},{8,0},{10,2},{12,4},{14,6},{16,24},{18,... | collective-permute-start | bytes 9437192 | tf_op jit(solution)/shard_map/ppermute | solution.py:52
  117.1 6.7 %collective-permute-start.21 = (bf16[3,32,1024]{2,1,0:T(8,128)(2,1)}, bf16[3,32,1024]{2,1,0:T(8,128)(2,1)S(1)}, u32[]{:S(2)}, u32[]{:S(2)}) collective-permute-start(bf16[3,32,1024]{2,1,0:T(8,128)(2,1)} %row_softmax.1.w0_ref), channel_id=1, source_target_pairs={{0,48},{2,50},{4,52},{6,54},{8,56},{10,58},{12,60},{14,62},{16,0},... | collective-permute-start | bytes 589832 | tf_op jit(solution)/shard_map/ppermute | solution.py:52
  118.0 8.0 %collective-permute-start.22 = (bf16[3,32,1024]{2,1,0:T(8,128)(2,1)}, bf16[3,32,1024]{2,1,0:T(8,128)(2,1)S(1)}, u32[]{:S(2)}, u32[]{:S(2)}) collective-permute-start(bf16[3,32,1024]{2,1,0:T(8,128)(2,1)} %row_softmax.1.w0_ref), channel_id=1, source_target_pairs={{0,32},{2,34},{4,36},{6,38},{8,40},{10,42},{12,44},{14,46},{16,48}... | collective-permute-start | bytes 589832 | tf_op jit(solution)/shard_map/ppermute | solution.py:52
  119.2 11.6 %collective-permute-start.23 = (bf16[3,32,1024]{2,1,0:T(8,128)(2,1)}, bf16[3,32,1024]{2,1,0:T(8,128)(2,1)S(1)}, u32[]{:S(2)}, u32[]{:S(2)}) collective-permute-start(bf16[3,32,1024]{2,1,0:T(8,128)(2,1)} %row_softmax.1.w0_ref), channel_id=1, source_target_pairs={{0,16},{2,18},{4,20},{6,22},{8,24},{10,26},{12,28},{14,30},{16,32}... | collective-permute-start | bytes 589832 | tf_op jit(solution)/shard_map/ppermute | solution.py:52
  (18 other events, 84.2 us)
Sparse Core Ops, SparseCore 0:
  63.7 41.1 all-gather.2

commit v3 on v2

--- a/solution.py
+++ b/solution.py
@@ -22,6 +22,7 @@
 R2, R4 = range(2), range(4)
 Y_RINGS = [[device(xl, y, c, z, xh) for y in R4] for xl in R2 for c in R2 for z in R4 for xh in R2]
 Z_RINGS = [[device(xl, y, c, z, xh) for z in R4] for xl in R2 for y in R4 for c in R2 for xh in R2]
+X_RINGS = [[device(xl, y, c, z, xh) for xh in R2 for xl in R2] for y in R4 for c in R2 for z in R4]
 PLANES = [[device(xl, y, c, z, xh) for xh in R2 for xl in R2 for y in R4] for c in R2 for z in R4]
 
 
@@ -75,7 +76,7 @@
 SCALARS = pl.BlockSpec(memory_space=pltpu.SMEM)
 
 
-def write_pieces(place_ref, normed, weight, pieces, outs):
+def write_pairs(normed, weight, out):
     low = lax.broadcasted_iota(jnp.int32, (128, 128), 1) < E
     for rp in range(2):
         first = mm(normed[2 * rp * 128 : (2 * rp + 1) * 128, :], weight)
@@ -88,14 +89,15 @@
             )
             for k in range(2):
                 g, h = (2 * t + k) // 3, (2 * t + k) % 3
-                pieces[g, rp, :, h * 128 : (h + 1) * 128] = pair[k].astype(BF)
-    for s, out in enumerate(outs):
-        out[...] = pieces[(place_ref[X] + s) % 4].reshape(out.shape)
+                out[g, rp, :, h * 128 : (h + 1) * 128] = pair[k].astype(BF)
 
 
 def key_kernel(place_ref, x_ref, gain_ref, w_ref, normed_ref, *refs):
     normed_ref[...] = normalize(x_ref[...].astype(F32), gain_ref[...][None, :])
-    write_pieces(place_ref, normed_ref[...], w_ref[...], refs[4], refs[:4])
+    outs, pieces = refs[:4], refs[4]
+    write_pairs(normed_ref[...], w_ref[...], pieces)
+    for s, out in enumerate(outs):
+        out[...] = pieces[(place_ref[X] + s) % 4]
 
 
 def key_proj(place, x, gain, weight):
@@ -117,26 +119,23 @@
     )(place, x, gain, weight)
 
 
-def query_value_kernel(place_ref, normed_ref, w_ref, *refs):
-    write_pieces(place_ref, normed_ref[...], w_ref[...], refs[4], refs[:4])
-
-
-def query_value_proj(place, normed, weight):
-    piece = (1, 2, 128, 384)
+def query_value_kernel(normed_ref, w_ref, out_ref):
+    write_pairs(normed_ref[...], w_ref[...], out_ref.at[:, 0])
+
+
+def query_value_proj(normed, weight):
     return pl.pallas_call(
         query_value_kernel,
         grid=(2,),
         in_specs=[
-            SCALARS,
             pl.BlockSpec((512, 768), lambda i: (0, 0)),
             pl.BlockSpec((768, 768), lambda i: (0, 2 * i)),
         ],
-        out_specs=[pl.BlockSpec(piece, lambda i: (i, 0, 0, 0))] * 4,
-        out_shape=[jax.ShapeDtypeStruct((2,) + piece[1:], BF)] * 4,
-        scratch_shapes=[pltpu.VMEM((4,) + piece[1:], BF)],
+        out_specs=pl.BlockSpec((4, 1, 2, 128, 384), lambda i: (0, i, 0, 0, 0)),
+        out_shape=jax.ShapeDtypeStruct((4, 2, 2, 128, 384), BF),
         compiler_params=params(),
         name="query_value_proj",
-    )(place, normed, weight)
+    )(normed, weight)
 
 
 def over_x(pieces):
@@ -144,20 +143,16 @@
 
 
 def scores_kernel(place_ref, q0_ref, q1_ref, *refs):
-    keys, out_ref = refs[:16], refs[16]
-
-    def source(xh, xl):
-        return (xh * 2 + xl + 4 - place_ref[X]) % 4
+    keys, out_ref = (refs[:4], refs[4:8]), refs[8]
 
     def query_rows(xh):
         return jnp.concatenate(
-            [q[source(xh, xl), rp] for q in (q0_ref, q1_ref) for xl in range(2) for rp in range(2)], axis=1
+            [q[xh * 2 + xl, rp] for q in (q0_ref, q1_ref) for xl in range(2) for rp in range(2)], axis=1
         )
 
     def key_rows(d, xh):
-        return jnp.concatenate(
-            [keys[k * 8 + d * 2 + rp][source(xh, xl)] for k in range(2) for xl in range(2) for rp in range(2)], axis=1
-        )
+        sources = [(xh * 2 + xl + 4 - place_ref[X]) % 4 for xl in range(2)]
+        return jnp.concatenate([keys[k][d][x, rp] for k in range(2) for x in sources for rp in range(2)], axis=1)
 
     left = jnp.concatenate([query_rows(0), query_rows(1)], axis=0)
     for d in range(4):
@@ -167,11 +162,11 @@
 
 def partial_scores(place, q0, q1, k0, k1):
     q_spec = pl.BlockSpec((4, 2, 64, 128), lambda h: (0, 0, 0, h))
-    k_spec = pl.BlockSpec((4, 128, 128), lambda h: (0, 0, h))
+    k_spec = pl.BlockSpec((4, 2, 128, 128), lambda h: (0, 0, 0, h))
     return pl.pallas_call(
         scores_kernel,
         grid=(3,),
-        in_specs=[SCALARS, q_spec, q_spec] + [k_spec] * 16,
+        in_specs=[SCALARS, q_spec, q_spec] + [k_spec] * 8,
         out_specs=pl.BlockSpec((4, 1, 32, 1024), lambda h: (0, h, 0, 0)),
         out_shape=jax.ShapeDtypeStruct((4, 3, 32, 1024), F32),
         compiler_params=params(),
@@ -207,8 +202,7 @@
             right = []
             for dz in (0, 3, 1, 2):
                 z = (place_ref[Z] + dz) % 4
-                for xh in range(2):
-                    x = (xh * 2 + xl + 4 - place_ref[X]) % 4
+                for x in (xl, 2 + xl):
                     right.append(jnp.concatenate([v[z, x, 0], v[z, x, 1]], axis=1))
             mixed = mm(weights[...], jnp.concatenate(right, axis=0))
             pair = jnp.concatenate(
@@ -354,25 +348,18 @@
 
     normed, *keys = key_proj(place, embeddings.reshape(512, 768), gain_row, attend_row)
     keys = over_x(keys)
-    queries_values = query_value_proj(place, normed, attend_row)
+    queries_values = query_value_proj(normed, attend_row)
     x = embeddings.reshape(4, 2, 8, 8, 768).transpose(2, 1, 0, 3, 4).reshape(16, 32, 768)
-    even, odd = (jnp.stack([k[rp] for k in keys]) for rp in range(2))
-    even, odd, x, queries_values = lax.optimization_barrier((even, odd, x, queries_values))
-
-    even_below, odd_above = send(even, dz=1), send(odd, dz=3)
-    odd_below, even_above = send(odd, dz=1), send(even, dz=3)
-    queries_values = over_x(queries_values)
+    keys, queries_values = lax.optimization_barrier((jnp.stack(keys), queries_values))
+
+    keys0 = [keys] + [send(keys, dz=dz) for dz in (1, 3, 2)]
+    keys1 = [to_other_core(k) for k in keys0]
+    queries_values, x = lax.optimization_barrier((swap(queries_values, X_RINGS), x))
     x = lax.all_to_all(x, "seq", split_axis=0, concat_axis=0, tiled=True)
-    even_below, odd_above, x = lax.optimization_barrier((even_below, odd_above, x))
-    even_far, odd_far = send(even_below, dz=1), send(odd_above, dz=3)
-    keys0 = [even, odd, even_below, odd_below, even_above, odd_above, even_far, odd_far]
-    keys1 = [to_other_core(k) for k in keys0]
-
-    queries = jnp.stack([qv[0] for qv in queries_values])
-    values = jnp.stack([qv[1] for qv in queries_values])
+    queries, values = queries_values[:, 0], queries_values[:, 1]
     queries0 = lax.dynamic_slice_in_dim(queries, core * 64, 64, axis=2)
     queries1 = to_other_core(lax.dynamic_slice_in_dim(queries, (1 - core) * 64, 64, axis=2))
-    values, keys0[6], keys0[7] = lax.optimization_barrier((values, keys0[6], keys0[7]))
+    values = lax.optimization_barrier((values, queries1, x, *keys0))[0]
     values0 = gather(values, Z_RINGS)
 
     scores = partial_scores(place, queries0, queries1, keys0, keys1)

time: 207 us -> 202 us (0.976)
  starting transfers between devices: 33.7 us -> 28.9 us
    all_to_all x0 -> x1, waiting for transfers between devices: none -> 12.5 us  [swap(): lax.all_to_all(array, AXES, split_axis=0, concat_axis=0, tiled=True, axis...]
    ppermute x25 -> x15, starting transfers between devices: 28.7 us -> 17.5 us  [send(): return lax.ppermute(array, AXES, shifts(**by))]
    ppermute x25 -> x15, waiting for transfers between devices: 41.3 us -> 30.4 us  [send(): return lax.ppermute(array, AXES, shifts(**by))]
    all_to_all x0 -> x1, starting transfers between devices: none -> 3.73 us  [swap(): lax.all_to_all(array, AXES, split_axis=0, concat_axis=0, tiled=True, axis...]
    all_to_all x1, starting transfers between devices: 4.99 us -> 7.65 us  [local(): x = lax.all_to_all(x, 'seq', split_axis=0, concat_axis=0, tiled=True)]
    slice x8 -> x0, local copies, waits for them, and re-layouts: 2.29 us -> none  [the longest x4 2.21 us: local(): values = jnp.stack([qv[1] for qv in queries_values])]
  transfers between devices with their start and end apart: 27 -> 18, of which waited for: 15 -> 11; matrix products, arithmetic and copies ran while one was open for 3% -> 1% of each run, Pallas kernels for 7% -> 7%
where the time goes in v3:
time: 202 us; the launch traced here: 201 us
  blocking collectives  61.4 us (30%)
  Pallas kernels  46.5 us (23%)
  waiting for transfers between devices  43.2 us (21%)
  starting transfers between devices  28.9 us (14%)
  between operations  13.5 us (7%)
  local copies, waits for them, and re-layouts  7.09 us (4%)
    all_to_all x2, blocking collectives, swap(): lax.all_to_all(array, AXES, split_axis=0, concat_axis=0, tiled=True, axis...  43.3 us
    ppermute x15, waiting for transfers between devices, send(): return lax.ppermute(array, AXES, shifts(**by))  30.4 us
    pallas_call x1, Pallas kernels, column_part(): pl.pallas_call(column_kernel, in_specs=[whole] * 4 + [hbm] * 5, out_specs...  24 us
    all_to_all x1, blocking collectives, local(): out = lax.all_to_all(out, 'seq', split_axis=0, concat_axis=0, tiled=True)  18.1 us
    ppermute x15, starting transfers between devices, send(): return lax.ppermute(array, AXES, shifts(**by))  17.5 us
    all_to_all x1, waiting for transfers between devices, swap(): lax.all_to_all(array, AXES, split_axis=0, concat_axis=0, tiled=True, axis...  12.5 us
    all_to_all x1, starting transfers between devices, local(): x = lax.all_to_all(x, 'seq', split_axis=0, concat_axis=0, tiled=True)  7.65 us
    pallas_call x1, Pallas kernels, partial_scores(): pl.pallas_call(scores_kernel, grid=(3,), in_specs=[SCALARS, q_spec, q_spe...  6.29 us
  transfers between devices with their start and end apart: 18, of which 11 were waited for; matrix products, arithmetic and copies ran while one was open for 1% of the time, Pallas kernels for 7%

profile of v3, /device:TPU:1, one launch (start us, length us, event | category | flops | bytes accessed | tf_op | source)
XLA Modules:
  0.0 201.4 jit_solution(18312939286114022538)
XLA Ops:
  7.2 3.6 %key_proj.1 = (bf16[512,768]{1,0:T(8,128)(2,1)}, bf16[2,128,384]{2,1,0:T(8,128)(2,1)}, bf16[2,128,384]{2,1,0:T(8,128)(2,1)}, bf16[2,128,384]{2,1,0:T(8,128)(2,1)}, bf16[2,128,384]{2,1,0:T(8,128)(2,1)}) custom-call(s32[4]{0:T(128)} %pad_add_fusion.place_ref, bf16[512,768]{1,0:T(8,128)(2,1)} %bitcast.30, f32[768]{0:T(1024)} %gain_ref.1, bf16[768,2304]{1,0:T(8,128)(2,1)} %w_ref.3), custom_call_target="tpu_custom_call" | custom-call | tf_op jit(solution)/shard_map/key_proj/pallas_call | solution.py:105
  10.8 2.0 %collective-permute-start.2 = (bf16[2,128,384]{2,1,0:T(8,128)(2,1)}, bf16[2,128,384]{2,1,0:T(8,128)(2,1)S(1)}, u32[]{:S(2)}, u32[]{:S(2)}) collective-permute-start(bf16[2,128,384]{2,1,0:T(8,128)(2,1)} %get-tuple-element.20), channel_id=1, source_target_pairs={{0,64},{2,66},{4,68},{6,70},{8,72},{10,74},{12,76},{14,78},{16,80}... | collective-permute-start | bytes 589832 | tf_op jit(solution)/shard_map/ppermute | solution.py:53
  12.9 2.5 %collective-permute-start.1 = (bf16[2,128,384]{2,1,0:T(8,128)(2,1)}, bf16[2,128,384]{2,1,0:T(8,128)(2,1)S(1)}, u32[]{:S(2)}, u32[]{:S(2)}) collective-permute-start(bf16[2,128,384]{2,1,0:T(8,128)(2,1)} %get-tuple-element.19), channel_id=1, source_target_pairs={{0,1},{2,3},{4,5},{6,7},{8,9},{10,11},{12,13},{14,15},{16,17},{18,... | collective-permute-start | bytes 589832 | tf_op jit(solution)/shard_map/ppermute | solution.py:53
  15.3 1.2 collective-permute-start
  16.5 4.2 %query_value_proj.1 = bf16[4,2,2,128,384]{4,3,2,1,0:T(8,128)(2,1)} custom-call(bf16[512,768]{1,0:T(8,128)(2,1)} %get-tuple-element.21.normed_ref, bf16[768,2304]{1,0:T(8,128)(2,1)} %w_ref.3), custom_call_target="tpu_custom_call" | custom-call | tf_op jit(solution)/shard_map/query_value_proj/pallas_call | solution.py:127
  20.7 3.3 %collective-permute-done.1 = bf16[2,128,384]{2,1,0:T(8,128)(2,1)S(1)} collective-permute-done((bf16[2,128,384]{2,1,0:T(8,128)(2,1)}, bf16[2,128,384]{2,1,0:T(8,128)(2,1)S(1)}, u32[]{:S(2)}, u32[]{:S(2)}) %collective-permute-start.1) | collective-permute-done | bytes 196640 | tf_op jit(solution)/shard_map/ppermute | solution.py:53
  24.2 3.7 %all-to-all-start = ((bf16[4,2,2,128,384]{4,3,2,1,0:T(8,128)(2,1)}), bf16[4,2,2,128,384]{4,3,2,1,0:T(8,128)(2,1)S(1)}, u32[]{:S(2)}, u32[]{:S(2)}) async-start(bf16[4,2,2,128,384]{4,3,2,1,0:T(8,128)(2,1)} %query_value_proj.1), calls=%async_computation | async-start | bytes 3145728 | tf_op jit(solution)/shard_map/all_to_all | solution.py:45
  28.9 2.0 collective-permute-start.4
  30.9 2.1 %collective-permute-start.5 = (bf16[4,2,128,384]{3,2,1,0:T(8,128)(2,1)S(1)}, bf16[4,2,128,384]{3,2,1,0:T(8,128)(2,1)}, u32[]{:S(2)}, u32[]{:S(2)}) collective-permute-start(bf16[4,2,128,384]{3,2,1,0:T(8,128)(2,1)S(1)} %pad_maximum_fusion.refs_0_), channel_id=1, source_target_pairs={{0,6},{2,0},{4,2},{6,4},{8,14},{10,8},{12,10},{14,12},{16,22},{18,... | collective-permute-start | bytes 2359304 | tf_op jit(solution)/shard_map/ppermute | solution.py:53
  33.0 1.3 collective-permute-start.6
  34.3 12.5 %all-to-all-done = bf16[4,2,2,128,384]{4,3,2,1,0:T(8,128)(2,1)S(1)} async-done(((bf16[4,2,2,128,384]{4,3,2,1,0:T(8,128)(2,1)}), bf16[4,2,2,128,384]{4,3,2,1,0:T(8,128)(2,1)S(1)}, u32[]{:S(2)}, u32[]{:S(2)}) %all-to-all-start) | async-done | bytes 1572896 | tf_op jit(solution)/shard_map/all_to_all | solution.py:45
  46.8 7.7 %all-to-all-start.2 = ((bf16[16,32,768]{2,1,0:T(8,128)(2,1)}), bf16[16,32,768]{2,1,0:T(8,128)(2,1)S(1)}, u32[]{:S(2)}, u32[]{:S(2)}) async-start(bf16[16,32,768]{2,1,0:T(8,128)(2,1)} %bitcast.26), calls=%async_computation.2 | async-start | bytes 1572864 | tf_op jit(solution)/shard_map/all_to_all | solution.py:358
  54.5 1.1 slice_bitcast_fusion
  56.5 10.7 %collective-permute-done.6.refs_3_ = bf16[4,2,128,384]{3,2,1,0:T(8,128)(2,1)} collective-permute-done((bf16[4,2,128,384]{3,2,1,0:T(8,128)(2,1)S(1)}, bf16[4,2,128,384]{3,2,1,0:T(8,128)(2,1)}, u32[]{:S(2)}, u32[]{:S(2)}) %collective-permute-start.6) | collective-permute-done | bytes 786464 | tf_op jit(solution)/shard_map/ppermute | solution.py:53
  67.5 2.2 %collective-permute-start.7 = (bf16[4,2,128,384]{3,2,1,0:T(8,128)(2,1)S(1)}, bf16[4,2,128,384]{3,2,1,0:T(8,128)(2,1)S(1)}, u32[]{:S(2)}, u32[]{:S(2)}) collective-permute-start(bf16[4,2,128,384]{3,2,1,0:T(8,128)(2,1)S(1)} %pad_maximum_fusion.refs_0_), channel_id=1, source_target_pairs={{0,8},{2,10},{4,12},{6,14},{8,0},{10,2},{12,4},{14,6},{16,24},{18,... | collective-permute-start | bytes 2359304 | tf_op jit(solution)/shard_map/ppermute | solution.py:53
  70.4 1.5 collective-permute-done.7.refs_4_
  71.9 1.1 collective-permute-done.8.refs_5_
  73.0 1.1 collective-permute-done.9.refs_6_
  74.1 1.1 collective-permute-done.10.refs_7_
  76.1 6.3 %partial_scores.1 = f32[4,3,32,1024]{3,2,1,0:T(8,128)} custom-call(s32[4]{0:T(128)} %pad_add_fusion.place_ref, bf16[4,2,64,384]{3,2,1,0:T(8,128)(2,1)} %get-tuple-element.32.q0_ref, bf16[4,2,64,384]{3,2,1,0:T(8,128)(2,1)} %copy-done.8, bf16[4,2,128,384]{3,2,1,0:T(8,128)(2,1)} %copy-done.1, bf16[4,2,128,384]{3,2,1,0:T(8,128)(2,1)} %collective-permute-done.4.refs_1_, ...), custom_call_target="tpu_custom_call" | custom-call | tf_op jit(solution)/shard_map/partial_scores/pallas_call | solution.py:166
  82.4 24.7 %all_to_all.25.refs_0_ = f32[4,3,32,1024]{3,2,1,0:T(8,128)} all-to-all(f32[4,3,32,1024]{3,2,1,0:T(8,128)} %partial_scores.1), channel_id=1, replica_groups={{0,16,32,48},{1,17,33,49},{2,18,34,50},{3,19,35,51},{4,20,36,52},{5,21,..., dimensions={0} | all-to-all | bytes 3145728 | tf_op jit(solution)/shard_map/all_to_all | solution.py:45
  107.1 3.1 %row_softmax.1.w0_ref = bf16[3,32,1024]{2,1,0:T(8,128)(2,1)} custom-call(f32[4,3,32,1024]{3,2,1,0:T(8,128)} %all_to_all.25.refs_0_), custom_call_target="tpu_custom_call" | custom-call | tf_op jit(solution)/shard_map/row_softmax/pallas_call | solution.py:184
  110.3 1.4 collective-permute-start.14
  112.5 1.3 collective-permute-start.12
  113.8 4.6 %collective-permute-done.11.w1_ref = bf16[3,32,1024]{2,1,0:T(8,128)(2,1)S(1)} collective-permute-done((bf16[3,32,1024]{2,1,0:T(8,128)(2,1)}, bf16[3,32,1024]{2,1,0:T(8,128)(2,1)S(1)}, u32[]{:S(2)}, u32[]{:S(2)}) %collective-permute-start.11) | collective-permute-done | bytes 196640 | tf_op jit(solution)/shard_map/ppermute | solution.py:53
  118.4 2.1 %collective-permute-done.12.w2_ref = bf16[3,32,1024]{2,1,0:T(8,128)(2,1)S(1)} collective-permute-done((bf16[3,32,1024]{2,1,0:T(8,128)(2,1)}, bf16[3,32,1024]{2,1,0:T(8,128)(2,1)S(1)}, u32[]{:S(2)}, u32[]{:S(2)}) %collective-permute-start.12) | collective-permute-done | bytes 196640 | tf_op jit(solution)/shard_map/ppermute | solution.py:53
  120.5 4.8 %collective-permute-done.13.w3_ref = bf16[3,32,1024]{2,1,0:T(8,128)(2,1)S(1)} collective-permute-done((bf16[3,32,1024]{2,1,0:T(8,128)(2,1)}, bf16[3,32,1024]{2,1,0:T(8,128)(2,1)S(1)}, u32[]{:S(2)}, u32[]{:S(2)}) %collective-permute-start.13) | collective-permute-done | bytes 196640 | tf_op jit(solution)/shard_map/ppermute | solution.py:53
  126.0 1.7 copy-done.2
  127.7 5.2 %row_mix.1 = bf16[16,2,32,384]{3,2,1,0:T(8,128)(2,1)} custom-call(s32[4]{0:T(128)} %pad_add_fusion.place_ref, bf16[3,32,1024]{2,1,0:T(8,128)(2,1)} %row_softmax.1.w0_ref, bf16[3,32,1024]{2,1,0:T(8,128)(2,1)} %copy-done.10, bf16[3,32,1024]{2,1,0:T(8,128)(2,1)} %copy-done.11, bf16[3,32,1024]{2,1,0:T(8,128)(2,1)} %copy-done.12, ...), custom_call_target="tpu_custom_call" | custom-call | tf_op jit(solution)/shard_map/row_mix/pallas_call | solution.py:217
  132.9 18.6 %all_to_all.26 = bf16[16,2,32,384]{3,2,1,0:T(8,128)(2,1)} all-to-all(bf16[16,2,32,384]{3,2,1,0:T(8,128)(2,1)} %row_mix.1), channel_id=1, replica_groups={{0,16,32,48,64,80,96,112,1,17,33,49,65,81,97,113},{2,18,34,50,66,82,98,..., dimensions={0} | all-to-all | bytes 1572864 | tf_op jit(solution)/shard_map/all_to_all | solution.py:45
  151.5 24.0 %column_part.1 = bf16[16,32,768]{2,1,0:T(8,128)(2,1)} custom-call(bf16[16,64,384]{2,1,0:T(8,128)(2,1)} %bitcast.25, bf16[16,32,768]{2,1,0:T(8,128)(2,1)} %copy-done, f32[768]{0:T(1024)} %gain_col_ref.1, f32[768]{0:T(1024)} %gain_ffn_ref.1, bf16[768,768]{1,0:T(8,128)(2,1)} %exit_row_hbm.1, bf16[768,2304]{1,0:T(8,128)(2,1)} %attend_hbm.1, ...), custom_call_target="tpu_custom_call" | custom-call | tf_op jit(solution)/shard_map/column_part/pallas_call | solution.py:315
  175.5 18.1 %all_to_all.27 = bf16[16,32,768]{2,1,0:T(8,128)(2,1)S(1)} all-to-all(bf16[16,32,768]{2,1,0:T(8,128)(2,1)} %column_part.1), channel_id=1, replica_groups=mesh['seq'=16,'col'=8] {'seq'}, dimensions={0} | all-to-all | bytes 1572864 | tf_op jit(solution)/shard_map/all_to_all | solution.py:373
  (46 shorter events, 7.1 us)
Async XLA Ops:
  10.8 9.9 %collective-permute-start.2 = (bf16[2,128,384]{2,1,0:T(8,128)(2,1)}, bf16[2,128,384]{2,1,0:T(8,128)(2,1)S(1)}, u32[]{:S(2)}, u32[]{:S(2)}) collective-permute-start(bf16[2,128,384]{2,1,0:T(8,128)(2,1)} %get-tuple-element.20), channel_id=1, source_target_pairs={{0,64},{2,66},{4,68},{6,70},{8,72},{10,74},{12,76},{14,78},{16,80}... | collective-permute-start | bytes 589832 | tf_op jit(solution)/shard_map/ppermute | solution.py:53
  12.9 11.2 %collective-permute-start.1 = (bf16[2,128,384]{2,1,0:T(8,128)(2,1)}, bf16[2,128,384]{2,1,0:T(8,128)(2,1)S(1)}, u32[]{:S(2)}, u32[]{:S(2)}) collective-permute-start(bf16[2,128,384]{2,1,0:T(8,128)(2,1)} %get-tuple-element.19), channel_id=1, source_target_pairs={{0,1},{2,3},{4,5},{6,7},{8,9},{10,11},{12,13},{14,15},{16,17},{18,... | collective-permute-start | bytes 589832 | tf_op jit(solution)/shard_map/ppermute | solution.py:53
  15.3 8.7 %collective-permute-start = (bf16[2,128,384]{2,1,0:T(8,128)(2,1)}, bf16[2,128,384]{2,1,0:T(8,128)(2,1)S(1)}, u32[]{:S(2)}, u32[]{:S(2)}) collective-permute-start(bf16[2,128,384]{2,1,0:T(8,128)(2,1)} %get-tuple-element.18), channel_id=1, source_target_pairs={{0,65},{2,67},{4,69},{6,71},{8,73},{10,75},{12,77},{14,79},{16,81}... | collective-permute-start | bytes 589832 | tf_op jit(solution)/shard_map/ppermute | solution.py:53
  16.5 7.6 %copy-start.9 = (bf16[2,128,384]{2,1,0:T(8,128)(2,1)S(1)}, bf16[2,128,384]{2,1,0:T(8,128)(2,1)}, u32[]{:S(2)}) copy-start(bf16[2,128,384]{2,1,0:T(8,128)(2,1)} %get-tuple-element.17) | copy-start | bytes 589828
  24.2 43.4 %copy-start.1 = (bf16[4,2,128,384]{3,2,1,0:T(8,128)(2,1)}, bf16[4,2,128,384]{3,2,1,0:T(8,128)(2,1)S(1)}, u32[]{:S(2)}) copy-start(bf16[4,2,128,384]{3,2,1,0:T(8,128)(2,1)S(1)} %pad_maximum_fusion.refs_0_) | copy-start | bytes 2359300
  24.2 3.7 %copy-start.3 = (bf16[4,128,768]{2,1,0:T(8,128)(2,1)S(1)}, bf16[4,128,768]{2,1,0:T(8,128)(2,1)}, u32[]{:S(2)}) copy-start(bf16[4,128,768]{2,1,0:T(8,128)(2,1)} %param.10) | copy-start | bytes 2359300
  24.2 22.6 %all-to-all-start = ((bf16[4,2,2,128,384]{4,3,2,1,0:T(8,128)(2,1)}), bf16[4,2,2,128,384]{4,3,2,1,0:T(8,128)(2,1)S(1)}, u32[]{:S(2)}, u32[]{:S(2)}) async-start(bf16[4,2,2,128,384]{4,3,2,1,0:T(8,128)(2,1)} %query_value_proj.1), calls=%async_computation | async-start | bytes 3145728 | tf_op jit(solution)/shard_map/all_to_all | solution.py:45
  28.9 27.6 %collective-permute-start.4 = (bf16[4,2,128,384]{3,2,1,0:T(8,128)(2,1)S(1)}, bf16[4,2,128,384]{3,2,1,0:T(8,128)(2,1)}, u32[]{:S(2)}, u32[]{:S(2)}) collective-permute-start(bf16[4,2,128,384]{3,2,1,0:T(8,128)(2,1)S(1)} %pad_maximum_fusion.refs_0_), channel_id=1, source_target_pairs={{0,2},{2,4},{4,6},{6,0},{8,10},{10,12},{12,14},{14,8},{16,18},{18,... | collective-permute-start | bytes 2359304 | tf_op jit(solution)/shard_map/ppermute | solution.py:53
  30.9 25.6 %collective-permute-start.5 = (bf16[4,2,128,384]{3,2,1,0:T(8,128)(2,1)S(1)}, bf16[4,2,128,384]{3,2,1,0:T(8,128)(2,1)}, u32[]{:S(2)}, u32[]{:S(2)}) collective-permute-start(bf16[4,2,128,384]{3,2,1,0:T(8,128)(2,1)S(1)} %pad_maximum_fusion.refs_0_), channel_id=1, source_target_pairs={{0,6},{2,0},{4,2},{6,4},{8,14},{10,8},{12,10},{14,12},{16,22},{18,... | collective-permute-start | bytes 2359304 | tf_op jit(solution)/shard_map/ppermute | solution.py:53
  33.0 34.2 %collective-permute-start.6 = (bf16[4,2,128,384]{3,2,1,0:T(8,128)(2,1)S(1)}, bf16[4,2,128,384]{3,2,1,0:T(8,128)(2,1)}, u32[]{:S(2)}, u32[]{:S(2)}) collective-permute-start(bf16[4,2,128,384]{3,2,1,0:T(8,128)(2,1)S(1)} %pad_maximum_fusion.refs_0_), channel_id=1, source_target_pairs={{0,4},{2,6},{4,0},{6,2},{8,12},{10,14},{12,8},{14,10},{16,20},{18,... | collective-permute-start | bytes 2359304 | tf_op jit(solution)/shard_map/ppermute | solution.py:53
  46.8 20.7 %all-to-all-start.2 = ((bf16[16,32,768]{2,1,0:T(8,128)(2,1)}), bf16[16,32,768]{2,1,0:T(8,128)(2,1)S(1)}, u32[]{:S(2)}, u32[]{:S(2)}) async-start(bf16[16,32,768]{2,1,0:T(8,128)(2,1)} %bitcast.26), calls=%async_computation.2 | async-start | bytes 1572864 | tf_op jit(solution)/shard_map/all_to_all | solution.py:358
  54.4 55.8 %all-gather.3.cloned.1.call-start = ((), (), s32[]{:S(2)}) async-start(), calls=%async_computation.5 | async-start | bytes 3932160 | tf_op jit(solution)/shard_map/all_gather | solution.py:49
  56.4 10.8 %collective-permute-start.3 = (bf16[4,2,64,384]{3,2,1,0:T(8,128)(2,1)S(1)}, bf16[4,2,64,384]{3,2,1,0:T(8,128)(2,1)S(1)}, u32[]{:S(2)}, u32[]{:S(2)}) collective-permute-start(bf16[4,2,64,384]{3,2,1,0:T(8,128)(2,1)S(1)} %get-tuple-element.31), channel_id=1, source_target_pairs={{0,8},{2,10},{4,12},{6,14},{8,0},{10,2},{12,4},{14,6},{16,24},{18,... | collective-permute-start | bytes 1179656 | tf_op jit(solution)/shard_map/ppermute | solution.py:53
  67.2 8.1 %copy-start.8 = (bf16[4,2,64,384]{3,2,1,0:T(8,128)(2,1)}, bf16[4,2,64,384]{3,2,1,0:T(8,128)(2,1)S(1)}, u32[]{:S(2)}) copy-start(bf16[4,2,64,384]{3,2,1,0:T(8,128)(2,1)S(1)} %collective-permute-done.3.q1_ref) | copy-start | bytes 1179652
  67.5 14.9 %copy-start = (bf16[16,32,768]{2,1,0:T(8,128)(2,1)}, bf16[16,32,768]{2,1,0:T(8,128)(2,1)S(1)}, u32[]{:S(2)}) copy-start(bf16[16,32,768]{2,1,0:T(8,128)(2,1)S(1)} %all-to-all-done.2.x_ref) | copy-start | bytes 2359300
  67.5 4.3 %collective-permute-start.7 = (bf16[4,2,128,384]{3,2,1,0:T(8,128)(2,1)S(1)}, bf16[4,2,128,384]{3,2,1,0:T(8,128)(2,1)S(1)}, u32[]{:S(2)}, u32[]{:S(2)}) collective-permute-start(bf16[4,2,128,384]{3,2,1,0:T(8,128)(2,1)S(1)} %pad_maximum_fusion.refs_0_), channel_id=1, source_target_pairs={{0,8},{2,10},{4,12},{6,14},{8,0},{10,2},{12,4},{14,6},{16,24},{18,... | collective-permute-start | bytes 2359304 | tf_op jit(solution)/shard_map/ppermute | solution.py:53
  69.8 3.2 %collective-permute-start.8 = (bf16[4,2,128,384]{3,2,1,0:T(8,128)(2,1)}, bf16[4,2,128,384]{3,2,1,0:T(8,128)(2,1)S(1)}, u32[]{:S(2)}, u32[]{:S(2)}) collective-permute-start(bf16[4,2,128,384]{3,2,1,0:T(8,128)(2,1)} %collective-permute-done.4.refs_1_), channel_id=1, source_target_pairs={{0,8},{2,10},{4,12},{6,14},{8,0},{10,2},{12,4},{14,6},{16,24},{18,... | collective-permute-start | bytes 2359304 | tf_op jit(solution)/shard_map/ppermute | solution.py:53
  69.9 4.3 %collective-permute-start.9 = (bf16[4,2,128,384]{3,2,1,0:T(8,128)(2,1)}, bf16[4,2,128,384]{3,2,1,0:T(8,128)(2,1)S(1)}, u32[]{:S(2)}, u32[]{:S(2)}) collective-permute-start(bf16[4,2,128,384]{3,2,1,0:T(8,128)(2,1)} %collective-permute-done.5.refs_2_), channel_id=1, source_target_pairs={{0,8},{2,10},{4,12},{6,14},{8,0},{10,2},{12,4},{14,6},{16,24},{18,... | collective-permute-start | bytes 2359304 | tf_op jit(solution)/shard_map/ppermute | solution.py:53
  70.3 5.0 %collective-permute-start.10 = (bf16[4,2,128,384]{3,2,1,0:T(8,128)(2,1)}, bf16[4,2,128,384]{3,2,1,0:T(8,128)(2,1)S(1)}, u32[]{:S(2)}, u32[]{:S(2)}) collective-permute-start(bf16[4,2,128,384]{3,2,1,0:T(8,128)(2,1)} %collective-permute-done.6.refs_3_), channel_id=1, source_target_pairs={{0,8},{2,10},{4,12},{6,14},{8,0},{10,2},{12,4},{14,6},{16,24},{18,... | collective-permute-start | bytes 2359304 | tf_op jit(solution)/shard_map/ppermute | solution.py:53
  71.9 3.4 %copy-start.4 = (bf16[4,2,128,384]{3,2,1,0:T(8,128)(2,1)}, bf16[4,2,128,384]{3,2,1,0:T(8,128)(2,1)S(1)}, u32[]{:S(2)}) copy-start(bf16[4,2,128,384]{3,2,1,0:T(8,128)(2,1)S(1)} %collective-permute-done.7.refs_4_) | copy-start | bytes 2359300
  73.0 2.3 %copy-start.5 = (bf16[4,2,128,384]{3,2,1,0:T(8,128)(2,1)}, bf16[4,2,128,384]{3,2,1,0:T(8,128)(2,1)S(1)}, u32[]{:S(2)}) copy-start(bf16[4,2,128,384]{3,2,1,0:T(8,128)(2,1)S(1)} %collective-permute-done.8.refs_5_) | copy-start | bytes 2359300
  74.1 1.1 copy-start.6
  75.3 0.9 copy-start.7
  110.3 15.0 %collective-permute-start.14 = (bf16[4,4,2,128,384]{4,3,2,1,0:T(8,128)(2,1)}, bf16[4,4,2,128,384]{4,3,2,1,0:T(8,128)(2,1)S(1)}, u32[]{:S(2)}, u32[]{:S(2)}) collective-permute-start(bf16[4,4,2,128,384]{4,3,2,1,0:T(8,128)(2,1)} %bitcast.28), channel_id=1, source_target_pairs={{0,8},{2,10},{4,12},{6,14},{8,0},{10,2},{12,4},{14,6},{16,24},{18,... | collective-permute-start | bytes 9437192 | tf_op jit(solution)/shard_map/ppermute | solution.py:53
  111.7 6.7 %collective-permute-start.11 = (bf16[3,32,1024]{2,1,0:T(8,128)(2,1)}, bf16[3,32,1024]{2,1,0:T(8,128)(2,1)S(1)}, u32[]{:S(2)}, u32[]{:S(2)}) collective-permute-start(bf16[3,32,1024]{2,1,0:T(8,128)(2,1)} %row_softmax.1.w0_ref), channel_id=1, source_target_pairs={{0,48},{2,50},{4,52},{6,54},{8,56},{10,58},{12,60},{14,62},{16,0},... | collective-permute-start | bytes 589832 | tf_op jit(solution)/shard_map/ppermute | solution.py:53
  112.5 8.0 %collective-permute-start.12 = (bf16[3,32,1024]{2,1,0:T(8,128)(2,1)}, bf16[3,32,1024]{2,1,0:T(8,128)(2,1)S(1)}, u32[]{:S(2)}, u32[]{:S(2)}) collective-permute-start(bf16[3,32,1024]{2,1,0:T(8,128)(2,1)} %row_softmax.1.w0_ref), channel_id=1, source_target_pairs={{0,32},{2,34},{4,36},{6,38},{8,40},{10,42},{12,44},{14,46},{16,48}... | collective-permute-start | bytes 589832 | tf_op jit(solution)/shard_map/ppermute | solution.py:53
  113.8 11.5 %collective-permute-start.13 = (bf16[3,32,1024]{2,1,0:T(8,128)(2,1)}, bf16[3,32,1024]{2,1,0:T(8,128)(2,1)S(1)}, u32[]{:S(2)}, u32[]{:S(2)}) collective-permute-start(bf16[3,32,1024]{2,1,0:T(8,128)(2,1)} %row_softmax.1.w0_ref), channel_id=1, source_target_pairs={{0,16},{2,18},{4,20},{6,22},{8,24},{10,26},{12,28},{14,30},{16,32}... | collective-permute-start | bytes 589832 | tf_op jit(solution)/shard_map/ppermute | solution.py:53
  118.4 6.9 %copy-start.10 = (bf16[3,32,1024]{2,1,0:T(8,128)(2,1)}, bf16[3,32,1024]{2,1,0:T(8,128)(2,1)S(1)}, u32[]{:S(2)}) copy-start(bf16[3,32,1024]{2,1,0:T(8,128)(2,1)S(1)} %collective-permute-done.11.w1_ref) | copy-start | bytes 589828
  120.5 4.8 %copy-start.11 = (bf16[3,32,1024]{2,1,0:T(8,128)(2,1)}, bf16[3,32,1024]{2,1,0:T(8,128)(2,1)S(1)}, u32[]{:S(2)}) copy-start(bf16[3,32,1024]{2,1,0:T(8,128)(2,1)S(1)} %collective-permute-done.12.w2_ref) | copy-start | bytes 589828
  125.3 0.7 copy-start.12
  126.0 1.7 copy-start.2
Sparse Core Ops, SparseCore 0:
  67.7 41.5 all-gather.2

commit v4 on v3

v4 whole, which is shorter than its diff:
```python
import math

import jax
import jax.numpy as jnp
from jax import lax
from jax.experimental import pallas as pl
from jax.experimental.pallas import tpu as pltpu
from jax.sharding import PartitionSpec as P

AXES = ("seq", "col")
HEADS = 12
E = 64
BF = jnp.bfloat16
F32 = jnp.float32


def device(xl, y, c, z, xh):
    return ((xl * 4 + y) * 2 + c) * 8 + z * 2 + xh


R2, R4 = range(2), range(4)
Y_RINGS = [[device(xl, y, c, z, xh) for y in R4] for xl in R2 for c in R2 for z in R4 for xh in R2]
Z_RINGS = [[device(xl, y, c, z, xh) for z in R4] for xl in R2 for y in R4 for c in R2 for xh in R2]
X_RINGS = [[device(xl, y, c, z, xh) for xh in R2 for xl in R2] for y in R4 for c in R2 for z in R4]
PLANES = [[device(xl, y, c, z, xh) for xh in R2 for xl in R2 for y in R4] for c in R2 for z in R4]


def shifts(dx=0, dy=0, dz=0, dc=0):
    pairs = []
    for x in R4:
        for y in R4:
            for c in R2:
                for z in R4:
                    to = ((x + dx) % 4, (y + dy) % 4, (c + dc) % 2, (z + dz) % 4)
                    pairs.append((device(x % 2, y, c, z, x // 2), device(to[0] % 2, *to[1:], to[0] // 2)))
    return pairs


def params(mib):
    return pltpu.CompilerParams(vmem_limit_bytes=mib * 1024 * 1024)


def swap(array, groups):
    return lax.all_to_all(array, AXES, split_axis=0, concat_axis=0, tiled=True, axis_index_groups=groups)


def gather(array, groups):
    return lax.all_gather(array, AXES, axis=0, tiled=False, axis_index_groups=groups)


def send(array, **by):
    return lax.ppermute(array, AXES, shifts(**by))


def to_other_core(array):
    return send(array, dc=1)


def mm(a, b):
    return jnp.dot(a, b, preferred_element_type=F32)


def mm_t(a, b):
    return lax.dot_general(a, b, (((1,), (1,)), ((), ())), preferred_element_type=F32)


def centre(stream):
    mean = jnp.mean(stream, axis=-1, keepdims=True)
    centred = stream - mean
    var = jnp.mean(centred * centred, axis=-1, keepdims=True)
    return centred * lax.rsqrt(var + 1e-05)


def normalize(stream, gain):
    return (centre(stream) * gain).astype(BF)


CORE, X, Y, Z = range(4)
SCALARS = pl.BlockSpec(memory_space=pltpu.SMEM)


def write_pairs(normed, weight, out):
    low = lax.broadcasted_iota(jnp.int32, (128, 128), 1) < E
    for rp in range(2):
        first = mm(normed[2 * rp * 128 : (2 * rp + 1) * 128, :], weight)
        second = mm(normed[(2 * rp + 1) * 128 : (2 * rp + 2) * 128, :], weight)
        for t in range(6):
            a, b = first[:, t * 128 : (t + 1) * 128], second[:, t * 128 : (t + 1) * 128]
            pair = (
                jnp.where(low, a, pltpu.roll(b, E, 1)),
                jnp.where(low, pltpu.roll(a, E, 1), b),
            )
            for k in range(2):
                g, h = (2 * t + k) // 3, (2 * t + k) % 3
                out[g, h, rp] = pair[k].astype(BF)


def key_kernel(place_ref, x_ref, gain_ref, w_ref, normed_ref, *refs):
    normed_ref[...] = normalize(x_ref[...].astype(F32), gain_ref[...][None, :])
    outs, pieces = refs[:4], refs[4]
    write_pairs(normed_ref[...], w_ref[...], pieces)
    for s, out in enumerate(outs):
        out[...] = pieces[(place_ref[X] + s) % 4]


def key_proj(place, x, gain, weight):
    piece = (3, 2, 128, 128)
    return pl.pallas_call(
        key_kernel,
        grid=(1,),
        in_specs=[
            SCALARS,
            pl.BlockSpec((512, 768), lambda i: (0, 0)),
            pl.BlockSpec((768,), lambda i: (0,)),
            pl.BlockSpec((768, 768), lambda i: (0, 1)),
        ],
        out_specs=[pl.BlockSpec((512, 768), lambda i: (0, 0))] + [pl.BlockSpec(piece, lambda i: (0, 0, 0, 0))] * 4,
        out_shape=[jax.ShapeDtypeStruct((512, 768), BF)] + [jax.ShapeDtypeStruct(piece, BF)] * 4,
        scratch_shapes=[pltpu.VMEM((4,) + piece, BF)],
        compiler_params=params(56),
        name="key_proj",
    )(place, x, gain, weight)


def query_value_kernel(normed_ref, w_ref, out_ref):
    write_pairs(normed_ref[...], w_ref[...], out_ref.at[:, 0])


def query_value_proj(normed, weight):
    return pl.pallas_call(
        query_value_kernel,
        grid=(2,),
        in_specs=[
            pl.BlockSpec((512, 768), lambda i: (0, 0)),
            pl.BlockSpec((768, 768), lambda i: (0, 2 * i)),
        ],
        out_specs=pl.BlockSpec((4, 1, 3, 2, 128, 128), lambda i: (0, i, 0, 0, 0, 0)),
        out_shape=jax.ShapeDtypeStruct((4, 2, 3, 2, 128, 128), BF),
        compiler_params=params(16),
        name="query_value_proj",
    )(normed, weight)


def over_x(pieces):
    return [pieces[0], send(pieces[3], dx=3), send(pieces[2], dx=2), send(pieces[1], dx=1)]


def scores_kernel(place_ref, q0_ref, q1_ref, *refs):
    blocks, out_ref = refs[:8], refs[8]
    for h in range(3):
        left = [
            jnp.concatenate(
                [
                    q[xh * 2 + xl, h, rp]
                    for q in (q0_ref, q1_ref)
                    for xl in range(2)
                    for rp in range(2)
                ],
                axis=1,
            )
            for xh in range(2)
        ]
        left = jnp.concatenate(left, axis=0)
        for d in range(4):
            right = [
                jnp.concatenate(
                    [
                        k[(xh * 2 + xl + 4 - place_ref[X]) % 4, h, rp]
                        for k in blocks[2 * d : 2 * d + 2]
                        for xl in range(2)
                        for rp in range(2)
                    ],
                    axis=1,
                )
                for xh in range(2)
            ]
            scores = mm_t(left, jnp.concatenate(right, axis=0))
            out_ref[:, h, :, d * 256 : (d + 1) * 256] = scores.reshape(4, 32, 256)


def partial_scores(place, q0, q1, k0, k1):
    vmem = pl.BlockSpec(memory_space=pltpu.VMEM)
    return pl.pallas_call(
        scores_kernel,
        in_specs=[SCALARS] + [vmem] * 10,
        out_specs=vmem,
        out_shape=jax.ShapeDtypeStruct((4, 3, 32, 1024), F32),
        compiler_params=params(14),
        name="partial_scores",
    )(place, q0, q1, *[k for pair in zip(k0, k1) for k in pair])


def softmax_kernel(scale, parts_ref, out_ref):
    tied = (parts_ref[0] + parts_ref[1] + parts_ref[2] + parts_ref[3]) * scale
    expo = jnp.exp(tied - jnp.max(tied, axis=-1, keepdims=True))
    out_ref[...] = (expo / jnp.sum(expo, axis=-1, keepdims=True)).astype(BF)


def row_softmax(parts, scale):
    return pl.pallas_call(
        lambda *refs: softmax_kernel(scale, *refs),
        in_specs=[pl.BlockSpec(memory_space=pltpu.VMEM)],
        out_specs=pl.BlockSpec(memory_space=pltpu.VMEM),
        out_shape=jax.ShapeDtypeStruct((3, 32, 1024), BF),
        compiler_params=params(8),
        name="row_softmax",
    )(parts)


def mix_kernel(place_ref, w0_ref, w1_ref, w2_ref, w3_ref, v0_ref, v1_ref, out_ref, weights, values, sem):
    copy = pltpu.make_async_copy(v0_ref, values, sem)
    copy.start()
    for d, w in enumerate((w0_ref, w1_ref, w2_ref, w3_ref)):
        share = (place_ref[Y] + d) % 4
        weights[:, pl.ds(pl.multiple_of(share * 32, 32), 32), :] = w[...]
    for k, v in ((1, v1_ref), (0, values)):
        if k == 0:
            copy.wait()
        owner = (place_ref[CORE] + k) % 2
        for xl in range(2):
            for h in range(3):
                right = [
                    jnp.concatenate([v[(place_ref[Z] + dz) % 4, xh * 2 + xl, h, rp] for rp in range(2)], axis=1)
                    for dz in (0, 3, 1, 2)
                    for xh in range(2)
                ]
                mixed = mm(weights[h], jnp.concatenate(right, axis=0))
                pair = jnp.concatenate(
                    [mixed[:, :128].reshape(16, 8, 128), mixed[:, 128:].reshape(16, 8, 128)], axis=1
                )
                out_ref[:, h, pl.ds(owner, 1), xl * 16 : (xl + 1) * 16, :] = pair.astype(BF)[:, None]


def row_mix(place, weights, v0, v1):
    vmem = pl.BlockSpec(memory_space=pltpu.VMEM)
    return pl.pallas_call(
        mix_kernel,
        in_specs=[SCALARS] + [vmem] * 4 + [pl.BlockSpec(memory_space=pltpu.HBM), vmem],
        out_specs=vmem,
        out_shape=jax.ShapeDtypeStruct((16, 3, 2, 32, 128), BF),
        scratch_shapes=[pltpu.VMEM((3, 128, 1024), BF), pltpu.VMEM(v0.shape, BF), pltpu.SemaphoreType.DMA],
        compiler_params=params(18),
        name="row_mix",
    )(place, *weights, v0, v1)


def column_kernel(
    mix_ref, x_ref, gain_col_ref, gain_ffn_ref, exit_row, attend, exit_col, expand_hbm, shrink_hbm,
    out_ref, qkv, stream, scratch, expand, shrink, sems,
):
    copies = [
        pltpu.make_async_copy(expand_hbm, expand, sems.at[0]),
        pltpu.make_async_copy(shrink_hbm, shrink, sems.at[1]),
    ]
    for copy in copies:
        copy.start()
    low = lax.broadcasted_iota(jnp.int32, (64, 128), 1) < E
    halves = ([], [])
    for y in range(4):
        tiles = ([], [])
        for t in range(6):
            (g0, h0), (g1, h1) = divmod(2 * t, 3), divmod(2 * t + 1, 3)
            a = mix_ref[g0 * 4 + y, h0].astype(F32)
            b = mix_ref[g1 * 4 + y, h1].astype(F32)
            tiles[0].append(jnp.where(low, a, pltpu.roll(b, E, 1)).astype(BF))
            tiles[1].append(jnp.where(low, pltpu.roll(a, E, 1), b).astype(BF))
        for k in range(2):
            halves[k].append(jnp.concatenate(tiles[k], axis=1))
    exits = [mm(jnp.concatenate(halves[k], axis=0), exit_row[...]).reshape(32, 1, 8, 768) for k in range(2)]
    exits = jnp.concatenate(exits, axis=1).reshape(512, 768)
    x = jnp.concatenate([x_ref[(xl * 4 + y) * 2 + c] for y in range(4) for c in range(2) for xl in range(2)], axis=0)
    stream[...] = x.astype(F32) + exits

    normed = centre(stream[...]) * gain_col_ref[...][None, :]
    for t in range(6):
        scratch[t] = normed[:, t * 128 : (t + 1) * 128]
    normed = jnp.concatenate(
        [
            jnp.concatenate([scratch[t, pl.ds(c, 64, stride=8), :] for c in range(8)], axis=0).astype(BF)
            for t in range(6)
        ],
        axis=1,
    )
    qkv[...] = mm(normed, attend[...]).astype(BF)
    group = lax.broadcasted_iota(jnp.int32, (256, 256), 0) // E == lax.broadcasted_iota(jnp.int32, (256, 256), 1) // E
    group = group.astype(F32).astype(BF)
    zeros = jnp.zeros((E, 256), BF)

    def tile(part, c, g):
        return qkv[c * 64 : (c + 1) * 64, part * 768 + g * 256 : part * 768 + (g + 1) * 256]

    def by_head(part, c, g):
        return jnp.concatenate([tile(part, c, g)] * 4, axis=0) * group

    for c in range(0, 8, 2):
        for g in range(3):
            k = jnp.concatenate([by_head(1, c, g), by_head(1, c + 1, g)], axis=1)
            q = jnp.concatenate(
                [
                    jnp.concatenate([tile(0, c, g), zeros], axis=1),
                    jnp.concatenate([zeros, tile(0, c + 1, g)], axis=1),
                ],
                axis=0,
            )
            scores = (mm_t(k, q) * (E ** -0.5)).reshape(4, 64, 128)
            expo = jnp.exp(scores - jnp.max(scores, axis=1, keepdims=True))
            weights = expo * (1.0 / jnp.sum(expo, axis=1, keepdims=True))
            weights = weights.reshape(256, 128).astype(BF)
            for k in range(2):
                mixed = lax.dot_general(
                    weights, by_head(2, c + k, g), (((0,), (0,)), ((), ())), preferred_element_type=F32
                )
                for t in range(2):
                    scratch[g * 2 + t, pl.ds(c + k, 64, stride=8), :] = mixed[
                        k * 64 : (k + 1) * 64, t * 128 : (t + 1) * 128
                    ]
    mixed = jnp.concatenate([scratch[t].astype(BF) for t in range(6)], axis=1)
    stream[...] += mm(mixed, exit_col[...])

    normed = normalize(stream[...], gain_ffn_ref[...][None, :])
    for copy in copies:
        copy.wait()
    for f in range(6):
        cols = slice(f * 512, (f + 1) * 512)
        pre = mm(normed, expand[:, cols])
        hidden = (0.5 * pre * (1.0 + lax.erf(pre * math.sqrt(0.5)))).astype(BF)
        stream[...] += mm(hidden, shrink[cols, :])
    done = stream[...].astype(BF)
    for i, (y, c, xl) in enumerate((y, c, xl) for y in range(4) for c in range(2) for xl in range(2)):
        out_ref[(xl * 4 + y) * 2 + c] = done[i * 32 : (i + 1) * 32, :]


def column_part(mix, x, gain_col, gain_ffn, exit_row, attend, exit_col, expand, shrink):
    vmem = pl.BlockSpec(memory_space=pltpu.VMEM)
    return pl.pallas_call(
        column_kernel,
        in_specs=[vmem] * 7 + [pl.BlockSpec(memory_space=pltpu.HBM)] * 2,
        out_specs=vmem,
        out_shape=jax.ShapeDtypeStruct((16, 32, 768), BF),
        scratch_shapes=[
            pltpu.VMEM((512, 2304), BF),
            pltpu.VMEM((512, 768), F32),
            pltpu.VMEM((6, 512, 128), F32),
            pltpu.VMEM(expand.shape, BF),
            pltpu.VMEM(shrink.shape, BF),
            pltpu.SemaphoreType.DMA((2,)),
        ],
        compiler_params=params(36),
        name="column_part",
    )(mix, x, gain_col, gain_ffn, exit_row, attend, exit_col, expand, shrink)


def local(
    embeddings,
    gain_row,
    attend_row,
    exit_row,
    gain_col,
    attend_col,
    exit_col,
    gain_ffn,
    expand,
    shrink,
):
    seq, col = lax.axis_index("seq"), lax.axis_index("col")
    core, y, z = seq % 2, seq // 2 % 4, col // 2
    place = jnp.stack([core, col % 2 * 2 + seq // 8, y, z]).astype(jnp.int32)
    scale = E ** (-0.5) / math.sqrt(embeddings.shape[0] * lax.axis_size("seq"))

    normed, *keys = key_proj(place, embeddings.reshape(512, 768), gain_row, attend_row)
    keys = over_x(keys)
    queries_values = query_value_proj(normed, attend_row)
    x = embeddings.reshape(4, 2, 8, 8, 768).transpose(2, 1, 0, 3, 4).reshape(16, 32, 768)
    keys, queries_values = lax.optimization_barrier((jnp.stack(keys), queries_values))

    keys0 = [keys] + [send(keys, dz=dz) for dz in (1, 3, 2)]
    keys1 = [to_other_core(k) for k in keys0]
    queries_values, x = lax.optimization_barrier((swap(queries_values, X_RINGS), x))
    x = lax.all_to_all(x, "seq", split_axis=0, concat_axis=0, tiled=True)
    queries, values = queries_values[:, 0], queries_values[:, 1]
    values = lax.optimization_barrier((values, x, keys1[0], *keys0))[0]
    values0 = gather(values, Z_RINGS)

    queries0 = lax.dynamic_slice_in_dim(queries, core * 64, 64, axis=3)
    queries1 = to_other_core(lax.dynamic_slice_in_dim(queries, (1 - core) * 64, 64, axis=3))
    scores = partial_scores(place, queries0, queries1, keys0, keys1)
    scores, x = lax.optimization_barrier((scores, x))
    weights = row_softmax(swap(scores, Y_RINGS), scale)
    weights, values0 = lax.optimization_barrier((weights, values0))
    weights = [weights] + [send(weights, dy=dy) for dy in (3, 2, 1)]
    mix = row_mix(place, weights, values0, to_other_core(values0))
    mix = swap(mix, PLANES).reshape(16, 3, 64, 128)

    out = column_part(mix, x, gain_col, gain_ffn, exit_row, attend_col, exit_col, expand, shrink)
    out = lax.all_to_all(out, "seq", split_axis=0, concat_axis=0, tiled=True)
    return out.reshape(8, 2, 4, 8, 768).transpose(2, 1, 0, 3, 4).reshape(4, 128, 768)


def solution(mesh):
    in_specs = (P("seq", "col", None), P(), P(), P(), P(), P(), P(), P(), P(), P())
    out_specs = P("seq", "col", None)
    return jax.shard_map(local, mesh=mesh, in_specs=in_specs, out_specs=out_specs, check_vma=False)
```

time: 202 us -> 192 us (0.950)
  Pallas kernels: 46.5 us -> 28.8 us
  waiting for transfers between devices: 43.2 us -> 48.6 us
  local copies, waits for them, and re-layouts: 7.09 us -> 11.3 us
    pallas_call x4, Pallas kernels: 38.6 us -> 22.2 us  [the longest x1 15.4 us: column_part(): pl.pallas_call(column_kernel, in_specs=[vmem] * 7 + [pl.BlockSpec(memory_...]
    all_gather x1, waiting for transfers between devices: 0.01 us -> 6.51 us  [gather(): lax.all_gather(array, AXES, axis=0, tiled=False, axis_index_groups=groups)]
    unnamed x26 -> x28, local copies, waits for them, and re-layouts: 3.29 us -> 5.41 us
  transfers between devices with their start and end apart: 18 -> 18, of which waited for: 11 -> 11; matrix products, arithmetic and copies ran while one was open for 1% -> 3% of each run, Pallas kernels for 7% -> 4%
where the time goes in v4:
time: 192 us; the launch traced here: 191 us
  blocking collectives  60.2 us (31%)
  waiting for transfers between devices  48.6 us (25%)
  Pallas kernels  28.8 us (15%)
  starting transfers between devices  28.4 us (15%)
  between operations  13.6 us (7%)
  local copies, waits for them, and re-layouts  11.3 us (6%)
    all_to_all x2, blocking collectives, swap(): lax.all_to_all(array, AXES, split_axis=0, concat_axis=0, tiled=True, axis...  42.2 us
    ppermute x15, waiting for transfers between devices, send(): return lax.ppermute(array, AXES, shifts(**by))  28.5 us
    ppermute x15, starting transfers between devices, send(): return lax.ppermute(array, AXES, shifts(**by))  18 us
    all_to_all x1, blocking collectives, local(): out = lax.all_to_all(out, 'seq', split_axis=0, concat_axis=0, tiled=True)  18 us
    pallas_call x1, Pallas kernels, column_part(): pl.pallas_call(column_kernel, in_specs=[vmem] * 7 + [pl.BlockSpec(memory_...  15.4 us
    all_to_all x1, waiting for transfers between devices, swap(): lax.all_to_all(array, AXES, split_axis=0, concat_axis=0, tiled=True, axis...  12.9 us
    all_gather x1, waiting for transfers between devices, gather(): lax.all_gather(array, AXES, axis=0, tiled=False, axis_index_groups=groups)  6.51 us
    all_to_all x1, starting transfers between devices, local(): x = lax.all_to_all(x, 'seq', split_axis=0, concat_axis=0, tiled=True)  5.82 us
  transfers between devices with their start and end apart: 18, of which 11 were waited for; matrix products, arithmetic and copies ran while one was open for 3% of the time, Pallas kernels for 4%

profile of v4, /device:TPU:1, one launch (start us, length us, event | category | flops | bytes accessed | tf_op | source)
XLA Modules:
  0.0 191.4 jit_solution(5136338451586987057)
XLA Ops:
  7.1 3.8 %key_proj.1 = (bf16[512,768]{1,0:T(8,128)(2,1)}, bf16[3,2,128,128]{3,2,1,0:T(8,128)(2,1)}, bf16[3,2,128,128]{3,2,1,0:T(8,128)(2,1)}, bf16[3,2,128,128]{3,2,1,0:T(8,128)(2,1)}, bf16[3,2,128,128]{3,2,1,0:T(8,128)(2,1)}) custom-call(s32[4]{0:T(128)} %pad_add_fusion.place_ref, bf16[512,768]{1,0:T(8,128)(2,1)} %bitcast.32, f32[768]{0:T(1024)} %gain_ref.1, ...), custom_call_target="tpu_custom_call" | custom-call | tf_op jit(solution)/shard_map/key_proj/pallas_call | solution.py:108
  10.9 3.3 %collective-permute-start = (bf16[3,2,128,128]{3,2,1,0:T(8,128)(2,1)}, bf16[3,2,128,128]{3,2,1,0:T(8,128)(2,1)S(1)}, u32[]{:S(2)}, u32[]{:S(2)}) collective-permute-start(bf16[3,2,128,128]{3,2,1,0:T(8,128)(2,1)} %get-tuple-element.20), channel_id=1, source_target_pairs={{0,65},{2,67},{4,69},{6,71},{8,73},{10,75},{12,77},{14,79},{16,81}... | collective-permute-start | bytes 589832 | tf_op jit(solution)/shard_map/ppermute | solution.py:52
  15.3 1.1 copy-done.6
  16.5 2.9 %query_value_proj.1 = bf16[4,2,3,2,128,128]{5,4,3,2,1,0:T(8,128)(2,1)} custom-call(bf16[512,768]{1,0:T(8,128)(2,1)S(1)} %copy-done.6, bf16[768,2304]{1,0:T(8,128)(2,1)S(1)} %copy-done), custom_call_target="tpu_custom_call" | custom-call | tf_op jit(solution)/shard_map/query_value_proj/pallas_call | solution.py:130
  19.4 2.1 %collective-permute-done.1 = bf16[3,2,128,128]{3,2,1,0:T(8,128)(2,1)S(1)} collective-permute-done((bf16[3,2,128,128]{3,2,1,0:T(8,128)(2,1)}, bf16[3,2,128,128]{3,2,1,0:T(8,128)(2,1)S(1)}, u32[]{:S(2)}, u32[]{:S(2)}) %collective-permute-start.1) | collective-permute-done | bytes 196640 | tf_op jit(solution)/shard_map/ppermute | solution.py:52
  21.4 5.5 %collective-permute-done.2 = bf16[3,2,128,128]{3,2,1,0:T(8,128)(2,1)S(1)} collective-permute-done((bf16[3,2,128,128]{3,2,1,0:T(8,128)(2,1)}, bf16[3,2,128,128]{3,2,1,0:T(8,128)(2,1)S(1)}, u32[]{:S(2)}, u32[]{:S(2)}) %collective-permute-start.2) | collective-permute-done | bytes 196640 | tf_op jit(solution)/shard_map/ppermute | solution.py:52
  27.1 4.5 %all-to-all-start = ((bf16[4,2,3,2,128,128]{5,4,3,2,1,0:T(8,128)(2,1)}), bf16[4,2,3,2,128,128]{5,4,3,2,1,0:T(8,128)(2,1)}, u32[]{:S(2)}, u32[]{:S(2)}) async-start(bf16[4,2,3,2,128,128]{5,4,3,2,1,0:T(8,128)(2,1)} %query_value_proj.1), calls=%async_computation | async-start | bytes 3145728 | tf_op jit(solution)/shard_map/all_to_all | solution.py:44
  31.6 3.7 %collective-permute-start.9 = (bf16[4,3,2,128,128]{4,3,2,1,0:T(8,128)(2,1)S(1)}, bf16[4,3,2,128,128]{4,3,2,1,0:T(8,128)(2,1)S(1)}, u32[]{:S(2)}, u32[]{:S(2)}) collective-permute-start(bf16[4,3,2,128,128]{4,3,2,1,0:T(8,128)(2,1)S(1)} %pad_maximum_fusion.refs_0_), channel_id=1, source_target_pairs={{0,4},{2,6},{4,0},{6,2},{8,12},{10,14},{12,8},{14,10},{16,20},{18,... | collective-permute-start | bytes 2359304 | tf_op jit(solution)/shard_map/ppermute | solution.py:52
  35.7 1.0 collective-permute-start.5
  36.7 1.3 collective-permute-start.4
  38.1 1.0 copy.13
  39.0 12.9 %all-to-all-done = bf16[4,2,3,2,128,128]{5,4,3,2,1,0:T(8,128)(2,1)} async-done(((bf16[4,2,3,2,128,128]{5,4,3,2,1,0:T(8,128)(2,1)}), bf16[4,2,3,2,128,128]{5,4,3,2,1,0:T(8,128)(2,1)}, u32[]{:S(2)}, u32[]{:S(2)}) %all-to-all-start) | async-done | bytes 1572896 | tf_op jit(solution)/shard_map/all_to_all | solution.py:44
  52.0 5.8 %all-to-all-start.1 = ((bf16[16,32,768]{2,1,0:T(8,128)(2,1)}), bf16[16,32,768]{2,1,0:T(8,128)(2,1)S(1)}, u32[]{:S(2)}, u32[]{:S(2)}) async-start(bf16[16,32,768]{2,1,0:T(8,128)(2,1)} %bitcast.30), calls=%async_computation.1 | async-start | bytes 1572864 | tf_op jit(solution)/shard_map/all_to_all | solution.py:379
  57.8 2.8 %slice_bitcast_fusion = (bf16[4,3,2,128,128]{4,3,2,1,0:T(8,128)(2,1)}, bf16[4,1,3,2,128,128]{5,4,3,2,1,0:T(8,128)(2,1)}) fusion(bf16[4,2,3,2,128,128]{5,4,3,2,1,0:T(8,128)(2,1)} %all-to-all-done), kind=kLoop, calls=%fused_computation.1 | loop fusion | bytes 3145728 | tf_op jit(solution)/shard_map/squeeze | solution.py:380
  60.6 9.5 %collective-permute-done.7.refs_4_ = bf16[4,3,2,128,128]{4,3,2,1,0:T(8,128)(2,1)} collective-permute-done((bf16[4,3,2,128,128]{4,3,2,1,0:T(8,128)(2,1)S(1)}, bf16[4,3,2,128,128]{4,3,2,1,0:T(8,128)(2,1)}, u32[]{:S(2)}, u32[]{:S(2)}) %collective-permute-start.7) | collective-permute-done | bytes 786464 | tf_op jit(solution)/shard_map/ppermute | solution.py:52
  70.8 1.0 collective-permute-start.10
  72.3 1.2 dynamic-slice_bitcast_fusion
  73.6 2.7 %collective-permute-done.3.q1_ref = bf16[4,3,2,64,128]{4,3,2,1,0:T(8,128)(2,1)S(1)} collective-permute-done((bf16[4,3,2,64,128]{4,3,2,1,0:T(8,128)(2,1)S(1)}, bf16[4,3,2,64,128]{4,3,2,1,0:T(8,128)(2,1)S(1)}, u32[]{:S(2)}, u32[]{:S(2)}) %collective-permute-start.3) | collective-permute-done | bytes 393248 | tf_op jit(solution)/shard_map/ppermute | solution.py:52
  76.8 4.5 %partial_scores.1 = f32[4,3,32,1024]{3,2,1,0:T(8,128)S(1)} custom-call(s32[4]{0:T(128)S(1)} %copy-done.7, bf16[4,3,2,64,128]{4,3,2,1,0:T(8,128)(2,1)S(1)} %get-tuple-element.36.q0_ref, bf16[4,3,2,64,128]{4,3,2,1,0:T(8,128)(2,1)S(1)} %collective-permute-done.3.q1_ref, bf16[4,3,2,128,128]{4,3,2,1,0:T(8,128)(2,1)S(1)} %pad_maximum_fusion.refs_0_, ...), custom_call_target="tpu_custom_call" | custom-call | tf_op jit(solution)/shard_map/partial_scores/pallas_call | solution.py:183
  81.3 23.7 %all_to_all.25.refs_0_ = f32[4,3,32,1024]{3,2,1,0:T(8,128)S(1)} all-to-all(f32[4,3,32,1024]{3,2,1,0:T(8,128)S(1)} %partial_scores.1), channel_id=1, replica_groups={{0,16,32,48},{1,17,33,49},{2,18,34,50},{3,19,35,51},{4,20,36,52},{5,21,..., dimensions={0} | all-to-all | bytes 3145728 | tf_op jit(solution)/shard_map/all_to_all | solution.py:44
  105.3 6.5 %all-gather.3.cloned.1.call-done = bf16[16,3,2,128,128]{4,3,2,1,0:T(8,128)(2,1)} async-done(((bf16[4,3,2,128,128]{4,3,2,1,0:T(8,128)(2,1)}), bf16[16,3,2,128,128]{4,3,2,1,0:T(8,128)(2,1)}) %all-gather.3.cloned.1.call-update) | async-done | bytes 3145744 | tf_op jit(solution)/shard_map/all_gather | solution.py:48
  112.5 1.2 collective-permute-start.13
  113.7 2.4 %collective-permute-start.12 = (bf16[3,32,1024]{2,1,0:T(8,128)(2,1)S(1)}, bf16[3,32,1024]{2,1,0:T(8,128)(2,1)S(1)}, u32[]{:S(2)}, u32[]{:S(2)}) collective-permute-start(bf16[3,32,1024]{2,1,0:T(8,128)(2,1)S(1)} %row_softmax.1.w0_ref), channel_id=1, source_target_pairs={{0,32},{2,34},{4,36},{6,38},{8,40},{10,42},{12,44},{14,46},{16,48}... | collective-permute-start | bytes 589832 | tf_op jit(solution)/shard_map/ppermute | solution.py:52
  116.2 1.2 collective-permute-start.11
  117.3 2.9 %collective-permute-done.13.w3_ref = bf16[3,32,1024]{2,1,0:T(8,128)(2,1)S(1)} collective-permute-done((bf16[3,32,1024]{2,1,0:T(8,128)(2,1)S(1)}, bf16[3,32,1024]{2,1,0:T(8,128)(2,1)S(1)}, u32[]{:S(2)}, u32[]{:S(2)}) %collective-permute-start.13) | collective-permute-done | bytes 196640 | tf_op jit(solution)/shard_map/ppermute | solution.py:52
  120.3 5.2 %collective-permute-done.12.w2_ref = bf16[3,32,1024]{2,1,0:T(8,128)(2,1)S(1)} collective-permute-done((bf16[3,32,1024]{2,1,0:T(8,128)(2,1)S(1)}, bf16[3,32,1024]{2,1,0:T(8,128)(2,1)S(1)}, u32[]{:S(2)}, u32[]{:S(2)}) %collective-permute-start.12) | collective-permute-done | bytes 196640 | tf_op jit(solution)/shard_map/ppermute | solution.py:52
  125.5 1.9 copy-done.3
  127.3 2.0 %row_mix.1 = bf16[16,3,2,32,128]{4,3,2,1,0:T(8,128)(2,1)S(1)} custom-call(s32[4]{0:T(128)S(1)} %copy-done.7, bf16[3,32,1024]{2,1,0:T(8,128)(2,1)S(1)} %row_softmax.1.w0_ref, bf16[3,32,1024]{2,1,0:T(8,128)(2,1)S(1)} %collective-permute-done.11.w1_ref, bf16[3,32,1024]{2,1,0:T(8,128)(2,1)S(1)} %collective-permute-done.12.w2_ref, ...), custom_call_target="tpu_custom_call" | custom-call | tf_op jit(solution)/shard_map/row_mix/pallas_call | solution.py:236
  129.4 18.5 %all_to_all.26 = bf16[16,3,2,32,128]{4,3,2,1,0:T(8,128)(2,1)S(1)} all-to-all(bf16[16,3,2,32,128]{4,3,2,1,0:T(8,128)(2,1)S(1)} %row_mix.1), channel_id=1, replica_groups={{0,16,32,48,64,80,96,112,1,17,33,49,65,81,97,113},{2,18,34,50,66,82,98,..., dimensions={0} | all-to-all | bytes 1572864 | tf_op jit(solution)/shard_map/all_to_all | solution.py:44
  148.0 2.3 %copy-done.1 = bf16[3072,768]{1,0:T(8,128)(2,1)S(1)} copy-done((bf16[3072,768]{1,0:T(8,128)(2,1)S(1)}, bf16[3072,768]{1,0:T(8,128)(2,1)}, u32[]{:S(2)}) %copy-start.1) | copy-done | bytes 4718616
  150.3 15.4 %column_part.1 = bf16[16,32,768]{2,1,0:T(8,128)(2,1)S(1)} custom-call(bf16[16,3,64,128]{3,2,1,0:T(8,128)(2,1)S(1)} %bitcast.27, bf16[16,32,768]{2,1,0:T(8,128)(2,1)S(1)} %all-to-all-done.1.x_ref, f32[768]{0:T(1024)S(1)} %copy-done.8, f32[768]{0:T(1024)S(1)} %copy-done.9, bf16[768,768]{1,0:T(8,128)(2,1)S(1)} %copy-done.4, bf16[768,2304]{1,0:T(8,128)(2,1)S(1)} %copy-done.2, ...), custom_call_target="tpu_custom_call" | custom-call | tf_op jit(solution)/shard_map/column_part/pallas_call | solution.py:335
  165.7 18.0 %all_to_all.27 = bf16[16,32,768]{2,1,0:T(8,128)(2,1)S(1)} all-to-all(bf16[16,32,768]{2,1,0:T(8,128)(2,1)S(1)} %column_part.1), channel_id=1, replica_groups=mesh['seq'=16,'col'=8] {'seq'}, dimensions={0} | all-to-all | bytes 1572864 | tf_op jit(solution)/shard_map/all_to_all | solution.py:395
  (49 shorter events, 6.0 us)
Async XLA Ops:
  7.1 8.2 %copy-start = (bf16[768,2304]{1,0:T(8,128)(2,1)S(1)}, bf16[768,2304]{1,0:T(8,128)(2,1)}, u32[]{:S(2)}) copy-start(bf16[768,2304]{1,0:T(8,128)(2,1)} %w_ref.3) | copy-start | bytes 10616836
  10.9 8.4 %collective-permute-start = (bf16[3,2,128,128]{3,2,1,0:T(8,128)(2,1)}, bf16[3,2,128,128]{3,2,1,0:T(8,128)(2,1)S(1)}, u32[]{:S(2)}, u32[]{:S(2)}) collective-permute-start(bf16[3,2,128,128]{3,2,1,0:T(8,128)(2,1)} %get-tuple-element.20), channel_id=1, source_target_pairs={{0,65},{2,67},{4,69},{6,71},{8,73},{10,75},{12,77},{14,79},{16,81}... | collective-permute-start | bytes 589832 | tf_op jit(solution)/shard_map/ppermute | solution.py:52
  14.2 7.2 %collective-permute-start.1 = (bf16[3,2,128,128]{3,2,1,0:T(8,128)(2,1)}, bf16[3,2,128,128]{3,2,1,0:T(8,128)(2,1)S(1)}, u32[]{:S(2)}, u32[]{:S(2)}) collective-permute-start(bf16[3,2,128,128]{3,2,1,0:T(8,128)(2,1)} %get-tuple-element.21), channel_id=1, source_target_pairs={{0,1},{2,3},{4,5},{6,7},{8,9},{10,11},{12,13},{14,15},{16,17},{18,... | collective-permute-start | bytes 589832 | tf_op jit(solution)/shard_map/ppermute | solution.py:52
  14.7 12.2 %collective-permute-start.2 = (bf16[3,2,128,128]{3,2,1,0:T(8,128)(2,1)}, bf16[3,2,128,128]{3,2,1,0:T(8,128)(2,1)S(1)}, u32[]{:S(2)}, u32[]{:S(2)}) collective-permute-start(bf16[3,2,128,128]{3,2,1,0:T(8,128)(2,1)} %get-tuple-element.22), channel_id=1, source_target_pairs={{0,64},{2,66},{4,68},{6,70},{8,72},{10,74},{12,76},{14,78},{16,80}... | collective-permute-start | bytes 589832 | tf_op jit(solution)/shard_map/ppermute | solution.py:52
  15.3 1.1 copy-start.6
  16.5 10.5 %copy-start.11 = (bf16[3,2,128,128]{3,2,1,0:T(8,128)(2,1)S(1)}, bf16[3,2,128,128]{3,2,1,0:T(8,128)(2,1)}, u32[]{:S(2)}) copy-start(bf16[3,2,128,128]{3,2,1,0:T(8,128)(2,1)} %get-tuple-element.19) | copy-start | bytes 589828
  27.1 11.0 %copy-start.10 = (bf16[4,128,768]{2,1,0:T(8,128)(2,1)S(1)}, bf16[4,128,768]{2,1,0:T(8,128)(2,1)}, u32[]{:S(2)}) copy-start(bf16[4,128,768]{2,1,0:T(8,128)(2,1)} %param.10) | copy-start | bytes 2359300
  27.1 24.9 %all-to-all-start = ((bf16[4,2,3,2,128,128]{5,4,3,2,1,0:T(8,128)(2,1)}), bf16[4,2,3,2,128,128]{5,4,3,2,1,0:T(8,128)(2,1)}, u32[]{:S(2)}, u32[]{:S(2)}) async-start(bf16[4,2,3,2,128,128]{5,4,3,2,1,0:T(8,128)(2,1)} %query_value_proj.1), calls=%async_computation | async-start | bytes 3145728 | tf_op jit(solution)/shard_map/all_to_all | solution.py:44
  31.6 29.0 %collective-permute-start.9 = (bf16[4,3,2,128,128]{4,3,2,1,0:T(8,128)(2,1)S(1)}, bf16[4,3,2,128,128]{4,3,2,1,0:T(8,128)(2,1)S(1)}, u32[]{:S(2)}, u32[]{:S(2)}) collective-permute-start(bf16[4,3,2,128,128]{4,3,2,1,0:T(8,128)(2,1)S(1)} %pad_maximum_fusion.refs_0_), channel_id=1, source_target_pairs={{0,4},{2,6},{4,0},{6,2},{8,12},{10,14},{12,8},{14,10},{16,20},{18,... | collective-permute-start | bytes 2359304 | tf_op jit(solution)/shard_map/ppermute | solution.py:52
  35.3 34.9 %collective-permute-start.7 = (bf16[4,3,2,128,128]{4,3,2,1,0:T(8,128)(2,1)S(1)}, bf16[4,3,2,128,128]{4,3,2,1,0:T(8,128)(2,1)}, u32[]{:S(2)}, u32[]{:S(2)}) collective-permute-start(bf16[4,3,2,128,128]{4,3,2,1,0:T(8,128)(2,1)S(1)} %pad_maximum_fusion.refs_0_), channel_id=1, source_target_pairs={{0,6},{2,0},{4,2},{6,4},{8,14},{10,8},{12,10},{14,12},{16,22},{18,... | collective-permute-start | bytes 2359304 | tf_op jit(solution)/shard_map/ppermute | solution.py:52
  35.7 34.5 %collective-permute-start.5 = (bf16[4,3,2,128,128]{4,3,2,1,0:T(8,128)(2,1)S(1)}, bf16[4,3,2,128,128]{4,3,2,1,0:T(8,128)(2,1)}, u32[]{:S(2)}, u32[]{:S(2)}) collective-permute-start(bf16[4,3,2,128,128]{4,3,2,1,0:T(8,128)(2,1)S(1)} %pad_maximum_fusion.refs_0_), channel_id=1, source_target_pairs={{0,2},{2,4},{4,6},{6,0},{8,10},{10,12},{12,14},{14,8},{16,18},{18,... | collective-permute-start | bytes 2359304 | tf_op jit(solution)/shard_map/ppermute | solution.py:52
  36.7 33.5 %collective-permute-start.4 = (bf16[4,3,2,128,128]{4,3,2,1,0:T(8,128)(2,1)S(1)}, bf16[4,3,2,128,128]{4,3,2,1,0:T(8,128)(2,1)}, u32[]{:S(2)}, u32[]{:S(2)}) collective-permute-start(bf16[4,3,2,128,128]{4,3,2,1,0:T(8,128)(2,1)S(1)} %pad_maximum_fusion.refs_0_), channel_id=1, source_target_pairs={{0,8},{2,10},{4,12},{6,14},{8,0},{10,2},{12,4},{14,6},{16,24},{18,... | collective-permute-start | bytes 2359304 | tf_op jit(solution)/shard_map/ppermute | solution.py:52
  52.0 18.8 %all-to-all-start.1 = ((bf16[16,32,768]{2,1,0:T(8,128)(2,1)}), bf16[16,32,768]{2,1,0:T(8,128)(2,1)S(1)}, u32[]{:S(2)}, u32[]{:S(2)}) async-start(bf16[16,32,768]{2,1,0:T(8,128)(2,1)} %bitcast.30), calls=%async_computation.1 | async-start | bytes 1572864 | tf_op jit(solution)/shard_map/all_to_all | solution.py:379
  57.8 54.0 %all-gather.3.cloned.1.call-start = ((), (), s32[]{:S(2)}) async-start(), calls=%async_computation.5 | async-start | bytes 3932160 | tf_op jit(solution)/shard_map/all_gather | solution.py:48
  60.6 16.2 %copy-start.7 = (s32[4]{0:T(128)S(1)}, s32[4]{0:T(128)}, u32[]{:S(2)}) copy-start(s32[4]{0:T(128)} %pad_add_fusion.place_ref) | copy-start | bytes 52
  70.8 5.5 %collective-permute-start.10 = (bf16[4,3,2,128,128]{4,3,2,1,0:T(8,128)(2,1)S(1)}, bf16[4,3,2,128,128]{4,3,2,1,0:T(8,128)(2,1)}, u32[]{:S(2)}, u32[]{:S(2)}) collective-permute-start(bf16[4,3,2,128,128]{4,3,2,1,0:T(8,128)(2,1)S(1)} %collective-permute-done.9.refs_6_), channel_id=1, source_target_pairs={{0,8},{2,10},{4,12},{6,14},{8,0},{10,2},{12,4},{14,6},{16,24},{18,... | collective-permute-start | bytes 2359304 | tf_op jit(solution)/shard_map/ppermute | solution.py:52
  71.8 4.6 %collective-permute-start.8 = (bf16[4,3,2,128,128]{4,3,2,1,0:T(8,128)(2,1)}, bf16[4,3,2,128,128]{4,3,2,1,0:T(8,128)(2,1)}, u32[]{:S(2)}, u32[]{:S(2)}) collective-permute-start(bf16[4,3,2,128,128]{4,3,2,1,0:T(8,128)(2,1)} %collective-permute-done.7.refs_4_), channel_id=1, source_target_pairs={{0,8},{2,10},{4,12},{6,14},{8,0},{10,2},{12,4},{14,6},{16,24},{18,... | collective-permute-start | bytes 2359304 | tf_op jit(solution)/shard_map/ppermute | solution.py:52
  71.9 5.0 %collective-permute-start.6 = (bf16[4,3,2,128,128]{4,3,2,1,0:T(8,128)(2,1)}, bf16[4,3,2,128,128]{4,3,2,1,0:T(8,128)(2,1)}, u32[]{:S(2)}, u32[]{:S(2)}) collective-permute-start(bf16[4,3,2,128,128]{4,3,2,1,0:T(8,128)(2,1)} %collective-permute-done.5.refs_2_), channel_id=1, source_target_pairs={{0,8},{2,10},{4,12},{6,14},{8,0},{10,2},{12,4},{14,6},{16,24},{18,... | collective-permute-start | bytes 2359304 | tf_op jit(solution)/shard_map/ppermute | solution.py:52
  73.5 2.9 %collective-permute-start.3 = (bf16[4,3,2,64,128]{4,3,2,1,0:T(8,128)(2,1)S(1)}, bf16[4,3,2,64,128]{4,3,2,1,0:T(8,128)(2,1)S(1)}, u32[]{:S(2)}, u32[]{:S(2)}) collective-permute-start(bf16[4,3,2,64,128]{4,3,2,1,0:T(8,128)(2,1)S(1)} %get-tuple-element.35), channel_id=1, source_target_pairs={{0,8},{2,10},{4,12},{6,14},{8,0},{10,2},{12,4},{14,6},{16,24},{18,... | collective-permute-start | bytes 1179656 | tf_op jit(solution)/shard_map/ppermute | solution.py:52
  105.1 42.8 %slice-start = ((s8[4718592]{0:T(1024)(128)(4,1)}), s8[524288]{0:T(1024)(128)(4,1)S(1)}, s32[]{:S(2)}) async-start(s8[4718592]{0:T(1024)(128)(4,1)} %bitcast.25), calls=%async_computation.6 | async-start | bytes 1048576
  105.1 42.8 %copy-start.5 = (bf16[768,768]{1,0:T(8,128)(2,1)S(1)}, bf16[768,768]{1,0:T(8,128)(2,1)}, u32[]{:S(2)}) copy-start(bf16[768,768]{1,0:T(8,128)(2,1)} %exit_col.1) | copy-start | bytes 3538948
  111.8 36.1 %slice-start.1 = ((s8[4718592]{0:T(1024)(128)(4,1)}), s8[4194304]{0:T(1024)(128)(4,1)S(1)}, s32[]{:S(2)}) async-start(s8[4718592]{0:T(1024)(128)(4,1)} %bitcast.25), calls=%async_computation.7 | async-start | bytes 8388608
  111.8 13.6 %collective-permute-start.14 = (bf16[4,4,3,2,128,128]{5,4,3,2,1,0:T(8,128)(2,1)}, bf16[4,4,3,2,128,128]{5,4,3,2,1,0:T(8,128)(2,1)S(1)}, u32[]{:S(2)}, u32[]{:S(2)}) collective-permute-start(bf16[4,4,3,2,128,128]{5,4,3,2,1,0:T(8,128)(2,1)} %bitcast.28), channel_id=1, source_target_pairs={{0,8},{2,10},{4,12},{6,14},{8,0},{10,2},{12,4},{14,6},{16,24},{18,... | collective-permute-start | bytes 9437192 | tf_op jit(solution)/shard_map/ppermute | solution.py:52
  112.5 7.7 %collective-permute-start.13 = (bf16[3,32,1024]{2,1,0:T(8,128)(2,1)S(1)}, bf16[3,32,1024]{2,1,0:T(8,128)(2,1)S(1)}, u32[]{:S(2)}, u32[]{:S(2)}) collective-permute-start(bf16[3,32,1024]{2,1,0:T(8,128)(2,1)S(1)} %row_softmax.1.w0_ref), channel_id=1, source_target_pairs={{0,16},{2,18},{4,20},{6,22},{8,24},{10,26},{12,28},{14,30},{16,32}... | collective-permute-start | bytes 589832 | tf_op jit(solution)/shard_map/ppermute | solution.py:52
  113.7 11.7 %collective-permute-start.12 = (bf16[3,32,1024]{2,1,0:T(8,128)(2,1)S(1)}, bf16[3,32,1024]{2,1,0:T(8,128)(2,1)S(1)}, u32[]{:S(2)}, u32[]{:S(2)}) collective-permute-start(bf16[3,32,1024]{2,1,0:T(8,128)(2,1)S(1)} %row_softmax.1.w0_ref), channel_id=1, source_target_pairs={{0,32},{2,34},{4,36},{6,38},{8,40},{10,42},{12,44},{14,46},{16,48}... | collective-permute-start | bytes 589832 | tf_op jit(solution)/shard_map/ppermute | solution.py:52
  116.2 9.3 %collective-permute-start.11 = (bf16[3,32,1024]{2,1,0:T(8,128)(2,1)S(1)}, bf16[3,32,1024]{2,1,0:T(8,128)(2,1)S(1)}, u32[]{:S(2)}, u32[]{:S(2)}) collective-permute-start(bf16[3,32,1024]{2,1,0:T(8,128)(2,1)S(1)} %row_softmax.1.w0_ref), channel_id=1, source_target_pairs={{0,48},{2,50},{4,52},{6,54},{8,56},{10,58},{12,60},{14,62},{16,0},... | collective-permute-start | bytes 589832 | tf_op jit(solution)/shard_map/ppermute | solution.py:52
  125.5 1.9 copy-start.3
  127.3 20.6 %copy-start.2 = (bf16[768,2304]{1,0:T(8,128)(2,1)S(1)}, bf16[768,2304]{1,0:T(8,128)(2,1)}, u32[]{:S(2)}) copy-start(bf16[768,2304]{1,0:T(8,128)(2,1)} %attend.1) | copy-start | bytes 10616836
  129.4 18.5 %copy-start.4 = (bf16[768,768]{1,0:T(8,128)(2,1)S(1)}, bf16[768,768]{1,0:T(8,128)(2,1)}, u32[]{:S(2)}) copy-start(bf16[768,768]{1,0:T(8,128)(2,1)} %exit_row.1) | copy-start | bytes 3538948
  129.4 18.5 %copy-start.8 = (f32[768]{0:T(1024)S(1)}, f32[768]{0:T(1024)}, u32[]{:S(2)}) copy-start(f32[768]{0:T(1024)} %gain_col_ref.1) | copy-start | bytes 9220
  129.4 18.5 %copy-start.9 = (f32[768]{0:T(1024)S(1)}, f32[768]{0:T(1024)}, u32[]{:S(2)}) copy-start(f32[768]{0:T(1024)} %gain_ffn_ref.1) | copy-start | bytes 9220
  148.0 2.3 %copy-start.1 = (bf16[3072,768]{1,0:T(8,128)(2,1)S(1)}, bf16[3072,768]{1,0:T(8,128)(2,1)}, u32[]{:S(2)}) copy-start(bf16[3072,768]{1,0:T(8,128)(2,1)} %shrink_hbm.1) | copy-start | bytes 14155780
Sparse Core Ops, SparseCore 0:
  70.9 40.8 all-gather.2

commit v5 on v4

--- a/solution.py
+++ b/solution.py
@@ -20,7 +20,7 @@
 
 R2, R4 = range(2), range(4)
 Y_RINGS = [[device(xl, y, c, z, xh) for y in R4] for xl in R2 for c in R2 for z in R4 for xh in R2]
-Z_RINGS = [[device(xl, y, c, z, xh) for z in R4] for xl in R2 for y in R4 for c in R2 for xh in R2]
+Z_COLUMNS = [[device(xl, y, c, z, xh) for z in R4 for c in R2] for xl in R2 for y in R4 for xh in R2]
 X_RINGS = [[device(xl, y, c, z, xh) for xh in R2 for xl in R2] for y in R4 for c in R2 for z in R4]
 PLANES = [[device(xl, y, c, z, xh) for xh in R2 for xl in R2 for y in R4] for c in R2 for z in R4]
 
@@ -145,28 +145,38 @@
     return [pieces[0], send(pieces[3], dx=3), send(pieces[2], dx=2), send(pieces[1], dx=1)]
 
 
-def scores_kernel(place_ref, q0_ref, q1_ref, *refs):
-    blocks, out_ref = refs[:8], refs[8]
-    for h in range(3):
-        left = [
-            jnp.concatenate(
-                [
-                    q[xh * 2 + xl, h, rp]
-                    for q in (q0_ref, q1_ref)
-                    for xl in range(2)
-                    for rp in range(2)
-                ],
-                axis=1,
-            )
-            for xh in range(2)
-        ]
-        left = jnp.concatenate(left, axis=0)
-        for d in range(4):
+def scores_kernel(place_ref, q0_ref, q1_ref, keys_hbm, out_ref, keys, sems):
+    copies = [
+        pltpu.make_async_copy(keys_hbm.at[z * 2 : z * 2 + 2], keys.at[z * 2 : z * 2 + 2], sems.at[z]) for z in range(4)
+    ]
+    for copy in copies:
+        copy.start()
+    left = [
+        jnp.concatenate(
+            [
+                jnp.concatenate(
+                    [
+                        q[xh * 2 + xl, h, rp]
+                        for q in (q0_ref, q1_ref)
+                        for xl in range(2)
+                        for rp in range(2)
+                    ],
+                    axis=1,
+                )
+                for xh in range(2)
+            ],
+            axis=0,
+        )
+        for h in range(3)
+    ]
+    for z in range(4):
+        copies[z].wait()
+        for h in range(3):
             right = [
                 jnp.concatenate(
                     [
-                        k[(xh * 2 + xl + 4 - place_ref[X]) % 4, h, rp]
-                        for k in blocks[2 * d : 2 * d + 2]
+                        keys[z * 2 + (place_ref[CORE] + k) % 2, (xh * 2 + xl + 4 - place_ref[X]) % 4, h, rp]
+                        for k in range(2)
                         for xl in range(2)
                         for rp in range(2)
                     ],
@@ -174,20 +184,21 @@
                 )
                 for xh in range(2)
             ]
-            scores = mm_t(left, jnp.concatenate(right, axis=0))
-            out_ref[:, h, :, d * 256 : (d + 1) * 256] = scores.reshape(4, 32, 256)
-
-
-def partial_scores(place, q0, q1, k0, k1):
+            scores = mm_t(left[h], jnp.concatenate(right, axis=0))
+            out_ref[:, h, :, z * 256 : (z + 1) * 256] = scores.reshape(4, 32, 256)
+
+
+def partial_scores(place, q0, q1, keys):
     vmem = pl.BlockSpec(memory_space=pltpu.VMEM)
     return pl.pallas_call(
         scores_kernel,
-        in_specs=[SCALARS] + [vmem] * 10,
+        in_specs=[SCALARS, vmem, vmem, pl.BlockSpec(memory_space=pltpu.HBM)],
         out_specs=vmem,
         out_shape=jax.ShapeDtypeStruct((4, 3, 32, 1024), F32),
-        compiler_params=params(14),
+        scratch_shapes=[pltpu.VMEM(keys.shape, BF), pltpu.SemaphoreType.DMA((4,))],
+        compiler_params=params(56),
         name="partial_scores",
-    )(place, q0, q1, *[k for pair in zip(k0, k1) for k in pair])
+    )(place, q0, q1, keys)
 
 
 def softmax_kernel(scale, parts_ref, out_ref):
@@ -207,41 +218,50 @@
     )(parts)
 
 
-def mix_kernel(place_ref, w0_ref, w1_ref, w2_ref, w3_ref, v0_ref, v1_ref, out_ref, weights, values, sem):
-    copy = pltpu.make_async_copy(v0_ref, values, sem)
-    copy.start()
+def mix_kernel(place_ref, w0_ref, w1_ref, w2_ref, w3_ref, values_hbm, out_ref, weights, values, sems):
+    order = [(c, xl) for c in range(2) for xl in range(2)]
+    copies = [
+        pltpu.make_async_copy(values_hbm.at[z * 2 + c, xh * 2 + xl], values.at[z * 2 + c, xh * 2 + xl], sems.at[i, z, xh])
+        for i, (c, xl) in enumerate(order)
+        for z in range(4)
+        for xh in range(2)
+    ]
+    for copy in copies:
+        copy.start()
     for d, w in enumerate((w0_ref, w1_ref, w2_ref, w3_ref)):
         share = (place_ref[Y] + d) % 4
         weights[:, pl.ds(pl.multiple_of(share * 32, 32), 32), :] = w[...]
-    for k, v in ((1, v1_ref), (0, values)):
-        if k == 0:
+    for i, (c, xl) in enumerate(order):
+        for copy in copies[i * 8 : i * 8 + 8]:
             copy.wait()
-        owner = (place_ref[CORE] + k) % 2
-        for xl in range(2):
-            for h in range(3):
-                right = [
-                    jnp.concatenate([v[(place_ref[Z] + dz) % 4, xh * 2 + xl, h, rp] for rp in range(2)], axis=1)
-                    for dz in (0, 3, 1, 2)
-                    for xh in range(2)
-                ]
-                mixed = mm(weights[h], jnp.concatenate(right, axis=0))
-                pair = jnp.concatenate(
-                    [mixed[:, :128].reshape(16, 8, 128), mixed[:, 128:].reshape(16, 8, 128)], axis=1
-                )
-                out_ref[:, h, pl.ds(owner, 1), xl * 16 : (xl + 1) * 16, :] = pair.astype(BF)[:, None]
-
-
-def row_mix(place, weights, v0, v1):
+        for h in range(3):
+            right = [
+                jnp.concatenate([values[z * 2 + c, xh * 2 + xl, h, rp] for rp in range(2)], axis=1)
+                for z in range(4)
+                for xh in range(2)
+            ]
+            mixed = mm(weights[h], jnp.concatenate(right, axis=0))
+            pair = jnp.concatenate(
+                [mixed[:, :128].reshape(16, 8, 128), mixed[:, 128:].reshape(16, 8, 128)], axis=1
+            )
+            out_ref[:, h, c, xl * 16 : (xl + 1) * 16, :] = pair.astype(BF)
+
+
+def row_mix(place, weights, values):
     vmem = pl.BlockSpec(memory_space=pltpu.VMEM)
     return pl.pallas_call(
         mix_kernel,
-        in_specs=[SCALARS] + [vmem] * 4 + [pl.BlockSpec(memory_space=pltpu.HBM), vmem],
+        in_specs=[SCALARS] + [vmem] * 4 + [pl.BlockSpec(memory_space=pltpu.HBM)],
         out_specs=vmem,
         out_shape=jax.ShapeDtypeStruct((16, 3, 2, 32, 128), BF),
-        scratch_shapes=[pltpu.VMEM((3, 128, 1024), BF), pltpu.VMEM(v0.shape, BF), pltpu.SemaphoreType.DMA],
-        compiler_params=params(18),
+        scratch_shapes=[
+            pltpu.VMEM((3, 128, 1024), BF),
+            pltpu.VMEM(values.shape, BF),
+            pltpu.SemaphoreType.DMA((4, 4, 2)),
+        ],
+        compiler_params=params(58),
         name="row_mix",
-    )(place, *weights, v0, v1)
+    )(place, *weights, values)
 
 
 def column_kernel(
@@ -345,7 +365,7 @@
             pltpu.VMEM(shrink.shape, BF),
             pltpu.SemaphoreType.DMA((2,)),
         ],
-        compiler_params=params(36),
+        compiler_params=params(48),
         name="column_part",
     )(mix, x, gain_col, gain_ffn, exit_row, attend, exit_col, expand, shrink)
 
@@ -373,22 +393,22 @@
     x = embeddings.reshape(4, 2, 8, 8, 768).transpose(2, 1, 0, 3, 4).reshape(16, 32, 768)
     keys, queries_values = lax.optimization_barrier((jnp.stack(keys), queries_values))
 
-    keys0 = [keys] + [send(keys, dz=dz) for dz in (1, 3, 2)]
-    keys1 = [to_other_core(k) for k in keys0]
+    keys_all = gather(keys, Z_COLUMNS)
     queries_values, x = lax.optimization_barrier((swap(queries_values, X_RINGS), x))
     x = lax.all_to_all(x, "seq", split_axis=0, concat_axis=0, tiled=True)
     queries, values = queries_values[:, 0], queries_values[:, 1]
-    values = lax.optimization_barrier((values, x, keys1[0], *keys0))[0]
-    values0 = gather(values, Z_RINGS)
+    values = lax.optimization_barrier((values, keys))[0]
+    values = gather(values, Z_COLUMNS)
 
     queries0 = lax.dynamic_slice_in_dim(queries, core * 64, 64, axis=3)
     queries1 = to_other_core(lax.dynamic_slice_in_dim(queries, (1 - core) * 64, 64, axis=3))
-    scores = partial_scores(place, queries0, queries1, keys0, keys1)
+    keys = lax.optimization_barrier((keys_all, x, queries1))[0]
+    scores = partial_scores(place, queries0, queries1, keys)
     scores, x = lax.optimization_barrier((scores, x))
     weights = row_softmax(swap(scores, Y_RINGS), scale)
-    weights, values0 = lax.optimization_barrier((weights, values0))
+    values = lax.optimization_barrier((values, weights))[0]
     weights = [weights] + [send(weights, dy=dy) for dy in (3, 2, 1)]
-    mix = row_mix(place, weights, values0, to_other_core(values0))
+    mix = row_mix(place, weights, values)
     mix = swap(mix, PLANES).reshape(16, 3, 64, 128)
 
     out = column_part(mix, x, gain_col, gain_ffn, exit_row, attend_col, exit_col, expand, shrink)

time: 192 us -> 182 us (0.948)
  starting transfers between devices: 28.4 us -> 19.4 us
  Pallas kernels: 28.8 us -> 35.9 us
  local copies, waits for them, and re-layouts: 11.3 us -> 5.62 us
  waiting for transfers between devices: 48.6 us -> 44.4 us
    ppermute x15 -> x7, waiting for transfers between devices: 28.5 us -> 6.53 us  [send(): return lax.ppermute(array, AXES, shifts(**by))]
    ppermute x15 -> x7, starting transfers between devices: 18 us -> 8.01 us  [send(): return lax.ppermute(array, AXES, shifts(**by))]
    all_to_all x1, waiting for transfers between devices: 0.56 us -> 10.4 us  [local(): x = lax.all_to_all(x, 'seq', split_axis=0, concat_axis=0, tiled=True)]
    all_to_all x1, waiting for transfers between devices: 12.9 us -> 17.8 us  [swap(): lax.all_to_all(array, AXES, split_axis=0, concat_axis=0, tiled=True, axis...]
    pallas_call x1, Pallas kernels: 2.04 us -> 5.79 us  [row_mix(): pl.pallas_call(mix_kernel, in_specs=[SCALARS] + [vmem] * 4 + [pl.BlockSpe...]
    unnamed x28 -> x26, local copies, waits for them, and re-layouts: 5.41 us -> 1.85 us
    all_gather x1 -> x2, waiting for transfers between devices: 6.51 us -> 9.61 us  [gather(): lax.all_gather(array, AXES, axis=0, tiled=False, axis_index_groups=groups)]
    pallas_call x1, Pallas kernels: 4.49 us -> 6.62 us  [partial_scores(): pl.pallas_call(scores_kernel, in_specs=[SCALARS, vmem, vmem, pl.BlockSpec...]
  transfers between devices with their start and end apart: 18 -> 11, of which waited for: 11 -> 7; matrix products, arithmetic and copies ran while one was open for 3% -> 2% of each run, Pallas kernels for 4% -> 5%
where the time goes in v5:
time: 182 us; the launch traced here: 181 us
  blocking collectives  60.8 us (33%)
  waiting for transfers between devices  44.4 us (24%)
  Pallas kernels  35.9 us (20%)
  starting transfers between devices  19.4 us (11%)
  between operations  13.5 us (7%)
  local copies, waits for them, and re-layouts  5.62 us (3%)
    all_to_all x2, blocking collectives, swap(): lax.all_to_all(array, AXES, split_axis=0, concat_axis=0, tiled=True, axis...  43.8 us
    all_to_all x1, waiting for transfers between devices, swap(): lax.all_to_all(array, AXES, split_axis=0, concat_axis=0, tiled=True, axis...  17.8 us
    all_to_all x1, blocking collectives, local(): out = lax.all_to_all(out, 'seq', split_axis=0, concat_axis=0, tiled=True)  17 us
    pallas_call x1, Pallas kernels, column_part(): pl.pallas_call(column_kernel, in_specs=[vmem] * 7 + [pl.BlockSpec(memory_...  16.7 us
    all_to_all x1, waiting for transfers between devices, local(): x = lax.all_to_all(x, 'seq', split_axis=0, concat_axis=0, tiled=True)  10.4 us
    all_gather x2, waiting for transfers between devices, gather(): lax.all_gather(array, AXES, axis=0, tiled=False, axis_index_groups=groups)  9.61 us
    ppermute x7, starting transfers between devices, send(): return lax.ppermute(array, AXES, shifts(**by))  8.01 us
    all_to_all x1, starting transfers between devices, local(): x = lax.all_to_all(x, 'seq', split_axis=0, concat_axis=0, tiled=True)  7.68 us
  transfers between devices with their start and end apart: 11, of which 7 were waited for; matrix products, arithmetic and copies ran while one was open for 2% of the time, Pallas kernels for 5%

profile of v5, /device:TPU:1, one launch (start us, length us, event | category | flops | bytes accessed | tf_op | source)
XLA Modules:
  0.0 181.4 jit_solution(9153930457765308340)
XLA Ops:
  6.5 0.6 pad_add_fusion.place_ref
  7.1 3.8 %key_proj.1 = (bf16[512,768]{1,0:T(8,128)(2,1)}, bf16[3,2,128,128]{3,2,1,0:T(8,128)(2,1)}, bf16[3,2,128,128]{3,2,1,0:T(8,128)(2,1)}, bf16[3,2,128,128]{3,2,1,0:T(8,128)(2,1)}, bf16[3,2,128,128]{3,2,1,0:T(8,128)(2,1)}) custom-call(s32[4]{0:T(128)} %pad_add_fusion.place_ref, bf16[512,768]{1,0:T(8,128)(2,1)} %bitcast.30, f32[768]{0:T(1024)} %gain_ref.1, ...), custom_call_target="tpu_custom_call" | custom-call | tf_op jit(solution)/shard_map/key_proj/pallas_call | solution.py:108
  10.9 2.0 %collective-permute-start.2 = (bf16[3,2,128,128]{3,2,1,0:T(8,128)(2,1)}, bf16[3,2,128,128]{3,2,1,0:T(8,128)(2,1)S(1)}, u32[]{:S(2)}, u32[]{:S(2)}) collective-permute-start(bf16[3,2,128,128]{3,2,1,0:T(8,128)(2,1)} %get-tuple-element.22), channel_id=1, source_target_pairs={{0,64},{2,66},{4,68},{6,70},{8,72},{10,74},{12,76},{14,78},{16,80}... | collective-permute-start | bytes 589832 | tf_op jit(solution)/shard_map/ppermute | solution.py:52
  13.0 2.4 %collective-permute-start.1 = (bf16[3,2,128,128]{3,2,1,0:T(8,128)(2,1)}, bf16[3,2,128,128]{3,2,1,0:T(8,128)(2,1)S(1)}, u32[]{:S(2)}, u32[]{:S(2)}) collective-permute-start(bf16[3,2,128,128]{3,2,1,0:T(8,128)(2,1)} %get-tuple-element.21), channel_id=1, source_target_pairs={{0,1},{2,3},{4,5},{6,7},{8,9},{10,11},{12,13},{14,15},{16,17},{18,... | collective-permute-start | bytes 589832 | tf_op jit(solution)/shard_map/ppermute | solution.py:52
  15.4 1.2 collective-permute-start
  16.6 1.1 copy-done.3
  17.7 2.8 %query_value_proj.1 = bf16[4,2,3,2,128,128]{5,4,3,2,1,0:T(8,128)(2,1)} custom-call(bf16[512,768]{1,0:T(8,128)(2,1)S(1)} %copy-done.3, bf16[768,2304]{1,0:T(8,128)(2,1)S(1)} %copy-done), custom_call_target="tpu_custom_call" | custom-call | tf_op jit(solution)/shard_map/query_value_proj/pallas_call | solution.py:130
  20.5 3.6 %collective-permute-done.1 = bf16[3,2,128,128]{3,2,1,0:T(8,128)(2,1)S(1)} collective-permute-done((bf16[3,2,128,128]{3,2,1,0:T(8,128)(2,1)}, bf16[3,2,128,128]{3,2,1,0:T(8,128)(2,1)S(1)}, u32[]{:S(2)}, u32[]{:S(2)}) %collective-permute-start.1) | collective-permute-done | bytes 196640 | tf_op jit(solution)/shard_map/ppermute | solution.py:52
  24.1 1.0 pad_maximum_fusion
  25.2 3.7 %all-to-all-start = ((bf16[4,2,3,2,128,128]{5,4,3,2,1,0:T(8,128)(2,1)}), bf16[4,2,3,2,128,128]{5,4,3,2,1,0:T(8,128)(2,1)S(1)}, u32[]{:S(2)}, u32[]{:S(2)}) async-start(bf16[4,2,3,2,128,128]{5,4,3,2,1,0:T(8,128)(2,1)} %query_value_proj.1), calls=%async_computation | async-start | bytes 3145728 | tf_op jit(solution)/shard_map/all_to_all | solution.py:44
  29.0 1.0 copy.13
  29.9 17.8 %all-to-all-done = bf16[4,2,3,2,128,128]{5,4,3,2,1,0:T(8,128)(2,1)S(1)} async-done(((bf16[4,2,3,2,128,128]{5,4,3,2,1,0:T(8,128)(2,1)}), bf16[4,2,3,2,128,128]{5,4,3,2,1,0:T(8,128)(2,1)S(1)}, u32[]{:S(2)}, u32[]{:S(2)}) %all-to-all-start) | async-done | bytes 1572896 | tf_op jit(solution)/shard_map/all_to_all | solution.py:44
  47.8 1.0 slice_bitcast_fusion
  48.8 7.7 %all-to-all-start.1 = ((bf16[16,32,768]{2,1,0:T(8,128)(2,1)}), bf16[16,32,768]{2,1,0:T(8,128)(2,1)S(1)}, u32[]{:S(2)}, u32[]{:S(2)}) async-start(bf16[16,32,768]{2,1,0:T(8,128)(2,1)} %bitcast.11), calls=%async_computation.1 | async-start | bytes 1572864 | tf_op jit(solution)/shard_map/all_to_all | solution.py:398
  56.5 0.8 dynamic-slice_bitcast_fusion
  57.3 0.1 collective-permute-start.3
  57.5 1.6 collective-permute-done.3.q1_ref
  59.1 10.4 %all-to-all-done.1.x_ref = bf16[16,32,768]{2,1,0:T(8,128)(2,1)S(1)} async-done(((bf16[16,32,768]{2,1,0:T(8,128)(2,1)}), bf16[16,32,768]{2,1,0:T(8,128)(2,1)S(1)}, u32[]{:S(2)}, u32[]{:S(2)}) %all-to-all-start.1) | async-done | bytes 786464 | tf_op jit(solution)/shard_map/all_to_all | solution.py:398
  69.5 0.3 all-gather.5.cloned.1.call-done
  69.8 6.6 %partial_scores.1 = f32[4,3,32,1024]{3,2,1,0:T(8,128)} custom-call(s32[4]{0:T(128)} %pad_add_fusion.place_ref, bf16[4,3,2,64,128]{4,3,2,1,0:T(8,128)(2,1)} %get-tuple-element.36.q0_ref, bf16[4,3,2,64,128]{4,3,2,1,0:T(8,128)(2,1)} %copy-done.8, bf16[8,4,3,2,128,128]{5,4,3,2,1,0:T(8,128)(2,1)} %bitcast.28), custom_call_target="tpu_custom_call" | custom-call | tf_op jit(solution)/shard_map/partial_scores/pallas_call | solution.py:193
  76.4 24.3 %all_to_all.25.refs_0_ = f32[4,3,32,1024]{3,2,1,0:T(8,128)S(1)} all-to-all(f32[4,3,32,1024]{3,2,1,0:T(8,128)} %partial_scores.1), channel_id=1, replica_groups={{0,16,32,48},{1,17,33,49},{2,18,34,50},{3,19,35,51},{4,20,36,52},{5,21,..., dimensions={0} | all-to-all | bytes 3145728 | tf_op jit(solution)/shard_map/all_to_all | solution.py:44
  100.7 0.2 row_softmax.1.w0_ref
  101.0 1.0 collective-permute-start.4
  102.0 1.3 collective-permute-start.5
  103.2 9.3 %all-gather.7.cloned.1.call-done = bf16[32,3,2,128,128]{4,3,2,1,0:T(8,128)(2,1)} async-done(((bf16[4,3,2,128,128]{4,3,2,1,0:T(8,128)(2,1)}), bf16[32,3,2,128,128]{4,3,2,1,0:T(8,128)(2,1)}) %all-gather.7.cloned.1.call-update) | async-done | bytes 6291472 | tf_op jit(solution)/shard_map/all_gather | solution.py:48
  112.6 1.3 collective-permute-done.6.w3_ref
  113.9 0.7 copy-done.12
  114.6 5.8 %row_mix.1 = bf16[16,3,2,32,128]{4,3,2,1,0:T(8,128)(2,1)} custom-call(s32[4]{0:T(128)} %pad_add_fusion.place_ref, bf16[3,32,1024]{2,1,0:T(8,128)(2,1)} %copy-done.4, bf16[3,32,1024]{2,1,0:T(8,128)(2,1)} %copy-done.10, bf16[3,32,1024]{2,1,0:T(8,128)(2,1)} %copy-done.11, bf16[3,32,1024]{2,1,0:T(8,128)(2,1)} %copy-done.12, bf16[8,4,3,2,128,128]{5,4,3,2,1,0:T(8,128)(2,1)} %bitcast.27), custom_call_target="tpu_custom_call" | custom-call | tf_op jit(solution)/shard_map/row_mix/pallas_call | solution.py:252
  120.4 19.5 %all_to_all.26 = bf16[16,3,2,32,128]{4,3,2,1,0:T(8,128)(2,1)S(1)} all-to-all(bf16[16,3,2,32,128]{4,3,2,1,0:T(8,128)(2,1)} %row_mix.1), channel_id=1, replica_groups={{0,16,32,48,64,80,96,112,1,17,33,49,65,81,97,113},{2,18,34,50,66,82,98,..., dimensions={0} | all-to-all | bytes 1572864 | tf_op jit(solution)/shard_map/all_to_all | solution.py:44
  139.9 16.7 %column_part.1 = bf16[16,32,768]{2,1,0:T(8,128)(2,1)S(1)} custom-call(bf16[16,3,64,128]{3,2,1,0:T(8,128)(2,1)S(1)} %bitcast.26, bf16[16,32,768]{2,1,0:T(8,128)(2,1)S(1)} %all-to-all-done.1.x_ref, f32[768]{0:T(1024)S(1)} %copy-done.5, f32[768]{0:T(1024)S(1)} %copy-done.6, bf16[768,768]{1,0:T(8,128)(2,1)S(1)} %copy-done.1, bf16[768,2304]{1,0:T(8,128)(2,1)} %attend.1, ...), custom_call_target="tpu_custom_call" | custom-call | tf_op jit(solution)/shard_map/column_part/pallas_call | solution.py:355
  156.6 17.0 %all_to_all.27 = bf16[16,32,768]{2,1,0:T(8,128)(2,1)S(1)} all-to-all(bf16[16,32,768]{2,1,0:T(8,128)(2,1)S(1)} %column_part.1), channel_id=1, replica_groups=mesh['seq'=16,'col'=8] {'seq'}, dimensions={0} | all-to-all | bytes 1572864 | tf_op jit(solution)/shard_map/all_to_all | solution.py:415
  173.6 0.9 copy.14
  (33 shorter events, 0.1 us)
Async XLA Ops:
  6.5 63.3 %all-gather.5.cloned.1.call-start = ((), (), s32[]{:S(2)}) async-start(), calls=%async_computation.5 | async-start | bytes 7077888 | tf_op jit(solution)/shard_map/all_gather | solution.py:48
  7.1 9.4 %copy-start = (bf16[768,2304]{1,0:T(8,128)(2,1)S(1)}, bf16[768,2304]{1,0:T(8,128)(2,1)}, u32[]{:S(2)}) copy-start(bf16[768,2304]{1,0:T(8,128)(2,1)} %w_ref.3) | copy-start | bytes 10616836
  10.9 9.6 %collective-permute-start.2 = (bf16[3,2,128,128]{3,2,1,0:T(8,128)(2,1)}, bf16[3,2,128,128]{3,2,1,0:T(8,128)(2,1)S(1)}, u32[]{:S(2)}, u32[]{:S(2)}) collective-permute-start(bf16[3,2,128,128]{3,2,1,0:T(8,128)(2,1)} %get-tuple-element.22), channel_id=1, source_target_pairs={{0,64},{2,66},{4,68},{6,70},{8,72},{10,74},{12,76},{14,78},{16,80}... | collective-permute-start | bytes 589832 | tf_op jit(solution)/shard_map/ppermute | solution.py:52
  13.0 11.2 %collective-permute-start.1 = (bf16[3,2,128,128]{3,2,1,0:T(8,128)(2,1)}, bf16[3,2,128,128]{3,2,1,0:T(8,128)(2,1)S(1)}, u32[]{:S(2)}, u32[]{:S(2)}) collective-permute-start(bf16[3,2,128,128]{3,2,1,0:T(8,128)(2,1)} %get-tuple-element.21), channel_id=1, source_target_pairs={{0,1},{2,3},{4,5},{6,7},{8,9},{10,11},{12,13},{14,15},{16,17},{18,... | collective-permute-start | bytes 589832 | tf_op jit(solution)/shard_map/ppermute | solution.py:52
  15.4 8.7 %collective-permute-start = (bf16[3,2,128,128]{3,2,1,0:T(8,128)(2,1)}, bf16[3,2,128,128]{3,2,1,0:T(8,128)(2,1)S(1)}, u32[]{:S(2)}, u32[]{:S(2)}) collective-permute-start(bf16[3,2,128,128]{3,2,1,0:T(8,128)(2,1)} %get-tuple-element.20), channel_id=1, source_target_pairs={{0,65},{2,67},{4,69},{6,71},{8,73},{10,75},{12,77},{14,79},{16,81}... | collective-permute-start | bytes 589832 | tf_op jit(solution)/shard_map/ppermute | solution.py:52
  16.6 1.1 copy-start.3
  17.7 6.4 %copy-start.9 = (bf16[3,2,128,128]{3,2,1,0:T(8,128)(2,1)S(1)}, bf16[3,2,128,128]{3,2,1,0:T(8,128)(2,1)}, u32[]{:S(2)}) copy-start(bf16[3,2,128,128]{3,2,1,0:T(8,128)(2,1)} %get-tuple-element.19) | copy-start | bytes 589828
  25.2 3.8 %copy-start.7 = (bf16[4,128,768]{2,1,0:T(8,128)(2,1)S(1)}, bf16[4,128,768]{2,1,0:T(8,128)(2,1)}, u32[]{:S(2)}) copy-start(bf16[4,128,768]{2,1,0:T(8,128)(2,1)} %param.10) | copy-start | bytes 2359300
  25.2 22.6 %all-to-all-start = ((bf16[4,2,3,2,128,128]{5,4,3,2,1,0:T(8,128)(2,1)}), bf16[4,2,3,2,128,128]{5,4,3,2,1,0:T(8,128)(2,1)S(1)}, u32[]{:S(2)}, u32[]{:S(2)}) async-start(bf16[4,2,3,2,128,128]{5,4,3,2,1,0:T(8,128)(2,1)} %query_value_proj.1), calls=%async_computation | async-start | bytes 3145728 | tf_op jit(solution)/shard_map/all_to_all | solution.py:44
  28.9 83.6 %all-gather.7.cloned.1.call-start = ((), (), s32[]{:S(2)}) async-start(), calls=%async_computation.6 | async-start | bytes 7077888 | tf_op jit(solution)/shard_map/all_gather | solution.py:48
  48.8 20.7 %all-to-all-start.1 = ((bf16[16,32,768]{2,1,0:T(8,128)(2,1)}), bf16[16,32,768]{2,1,0:T(8,128)(2,1)S(1)}, u32[]{:S(2)}, u32[]{:S(2)}) async-start(bf16[16,32,768]{2,1,0:T(8,128)(2,1)} %bitcast.11), calls=%async_computation.1 | async-start | bytes 1572864 | tf_op jit(solution)/shard_map/all_to_all | solution.py:398
  57.3 1.7 collective-permute-start.3
  59.1 10.7 %copy-start.8 = (bf16[4,3,2,64,128]{4,3,2,1,0:T(8,128)(2,1)}, bf16[4,3,2,64,128]{4,3,2,1,0:T(8,128)(2,1)S(1)}, u32[]{:S(2)}) copy-start(bf16[4,3,2,64,128]{4,3,2,1,0:T(8,128)(2,1)S(1)} %collective-permute-done.3.q1_ref) | copy-start | bytes 1179652
  101.0 12.9 %copy-start.4 = (bf16[3,32,1024]{2,1,0:T(8,128)(2,1)}, bf16[3,32,1024]{2,1,0:T(8,128)(2,1)S(1)}, u32[]{:S(2)}) copy-start(bf16[3,32,1024]{2,1,0:T(8,128)(2,1)S(1)} %row_softmax.1.w0_ref) | copy-start | bytes 589828
  101.0 11.6 %collective-permute-start.4 = (bf16[3,32,1024]{2,1,0:T(8,128)(2,1)S(1)}, bf16[3,32,1024]{2,1,0:T(8,128)(2,1)S(1)}, u32[]{:S(2)}, u32[]{:S(2)}) collective-permute-start(bf16[3,32,1024]{2,1,0:T(8,128)(2,1)S(1)} %row_softmax.1.w0_ref), channel_id=1, source_target_pairs={{0,48},{2,50},{4,52},{6,54},{8,56},{10,58},{12,60},{14,62},{16,0},... | collective-permute-start | bytes 589832 | tf_op jit(solution)/shard_map/ppermute | solution.py:52
  102.0 10.6 %collective-permute-start.5 = (bf16[3,32,1024]{2,1,0:T(8,128)(2,1)S(1)}, bf16[3,32,1024]{2,1,0:T(8,128)(2,1)S(1)}, u32[]{:S(2)}, u32[]{:S(2)}) collective-permute-start(bf16[3,32,1024]{2,1,0:T(8,128)(2,1)S(1)} %row_softmax.1.w0_ref), channel_id=1, source_target_pairs={{0,32},{2,34},{4,36},{6,38},{8,40},{10,42},{12,44},{14,46},{16,48}... | collective-permute-start | bytes 589832 | tf_op jit(solution)/shard_map/ppermute | solution.py:52
  103.2 10.6 %collective-permute-start.6 = (bf16[3,32,1024]{2,1,0:T(8,128)(2,1)S(1)}, bf16[3,32,1024]{2,1,0:T(8,128)(2,1)S(1)}, u32[]{:S(2)}, u32[]{:S(2)}) collective-permute-start(bf16[3,32,1024]{2,1,0:T(8,128)(2,1)S(1)} %row_softmax.1.w0_ref), channel_id=1, source_target_pairs={{0,16},{2,18},{4,20},{6,22},{8,24},{10,26},{12,28},{14,30},{16,32}... | collective-permute-start | bytes 589832 | tf_op jit(solution)/shard_map/ppermute | solution.py:52
  112.6 1.3 copy-start.10
  112.6 1.3 copy-start.11
  113.9 0.7 copy-start.12
  114.6 25.3 %copy-start.2 = (bf16[768,768]{1,0:T(8,128)(2,1)S(1)}, bf16[768,768]{1,0:T(8,128)(2,1)}, u32[]{:S(2)}) copy-start(bf16[768,768]{1,0:T(8,128)(2,1)} %exit_col.1) | copy-start | bytes 3538948
  120.4 19.6 %copy-start.1 = (bf16[768,768]{1,0:T(8,128)(2,1)S(1)}, bf16[768,768]{1,0:T(8,128)(2,1)}, u32[]{:S(2)}) copy-start(bf16[768,768]{1,0:T(8,128)(2,1)} %exit_row.1) | copy-start | bytes 3538948
  120.4 19.5 %copy-start.5 = (f32[768]{0:T(1024)S(1)}, f32[768]{0:T(1024)}, u32[]{:S(2)}) copy-start(f32[768]{0:T(1024)} %gain_col_ref.1) | copy-start | bytes 9220
  120.4 19.5 %copy-start.6 = (f32[768]{0:T(1024)S(1)}, f32[768]{0:T(1024)}, u32[]{:S(2)}) copy-start(f32[768]{0:T(1024)} %gain_ffn_ref.1) | copy-start | bytes 9220
Sparse Core Ops, SparseCore 0:
  25.3 44.4 all-gather.4
  71.5 41.0 all-gather.6

commit v6 on v5

--- a/solution.py
+++ b/solution.py
@@ -81,18 +81,16 @@
 
 def write_pairs(normed, weight, out):
     low = lax.broadcasted_iota(jnp.int32, (128, 128), 1) < E
-    for rp in range(2):
-        first = mm(normed[2 * rp * 128 : (2 * rp + 1) * 128, :], weight)
-        second = mm(normed[(2 * rp + 1) * 128 : (2 * rp + 2) * 128, :], weight)
-        for t in range(6):
-            a, b = first[:, t * 128 : (t + 1) * 128], second[:, t * 128 : (t + 1) * 128]
-            pair = (
-                jnp.where(low, a, pltpu.roll(b, E, 1)),
-                jnp.where(low, pltpu.roll(a, E, 1), b),
-            )
-            for k in range(2):
-                g, h = (2 * t + k) // 3, (2 * t + k) % 3
-                out[g, h, rp] = pair[k].astype(BF)
+    first, second = mm(normed[:128, :], weight), mm(normed[128:, :], weight)
+    for t in range(6):
+        a, b = first[:, t * 128 : (t + 1) * 128], second[:, t * 128 : (t + 1) * 128]
+        pair = (
+            jnp.where(low, a, pltpu.roll(b, E, 1)),
+            jnp.where(low, pltpu.roll(a, E, 1), b),
+        )
+        for k in range(2):
+            g, h = (2 * t + k) // 3, (2 * t + k) % 3
+            out[g, h] = pair[k].astype(BF)
 
 
 def key_kernel(place_ref, x_ref, gain_ref, w_ref, normed_ref, *refs):
@@ -100,30 +98,32 @@
     outs, pieces = refs[:4], refs[4]
     write_pairs(normed_ref[...], w_ref[...], pieces)
     for s, out in enumerate(outs):
-        out[...] = pieces[(place_ref[X] + s) % 4]
+        out[:, 0] = pieces[(place_ref[X] + s) % 4]
 
 
 def key_proj(place, x, gain, weight):
     piece = (3, 2, 128, 128)
     return pl.pallas_call(
         key_kernel,
-        grid=(1,),
+        grid=(2,),
         in_specs=[
             SCALARS,
-            pl.BlockSpec((512, 768), lambda i: (0, 0)),
+            pl.BlockSpec((256, 768), lambda i: (i, 0)),
             pl.BlockSpec((768,), lambda i: (0,)),
             pl.BlockSpec((768, 768), lambda i: (0, 1)),
         ],
-        out_specs=[pl.BlockSpec((512, 768), lambda i: (0, 0))] + [pl.BlockSpec(piece, lambda i: (0, 0, 0, 0))] * 4,
+        out_specs=[pl.BlockSpec((256, 768), lambda i: (i, 0))]
+        + [pl.BlockSpec((3, 1, 128, 128), lambda i: (0, i, 0, 0))] * 4,
         out_shape=[jax.ShapeDtypeStruct((512, 768), BF)] + [jax.ShapeDtypeStruct(piece, BF)] * 4,
-        scratch_shapes=[pltpu.VMEM((4,) + piece, BF)],
-        compiler_params=params(56),
+        scratch_shapes=[pltpu.VMEM((4, 3, 128, 128), BF)],
+        compiler_params=params(52),
         name="key_proj",
     )(place, x, gain, weight)
 
 
 def query_value_kernel(normed_ref, w_ref, out_ref):
-    write_pairs(normed_ref[...], w_ref[...], out_ref.at[:, 0])
+    for rp in range(2):
+        write_pairs(normed_ref[rp * 256 : (rp + 1) * 256, :], w_ref[...], out_ref.at[:, 0, :, rp])
 
 
 def query_value_proj(normed, weight):
@@ -196,7 +196,7 @@
         out_specs=vmem,
         out_shape=jax.ShapeDtypeStruct((4, 3, 32, 1024), F32),
         scratch_shapes=[pltpu.VMEM(keys.shape, BF), pltpu.SemaphoreType.DMA((4,))],
-        compiler_params=params(56),
+        compiler_params=params(48),
         name="partial_scores",
     )(place, q0, q1, keys)
 
@@ -218,48 +218,34 @@
     )(parts)
 
 
-def mix_kernel(place_ref, w0_ref, w1_ref, w2_ref, w3_ref, values_hbm, out_ref, weights, values, sems):
-    order = [(c, xl) for c in range(2) for xl in range(2)]
-    copies = [
-        pltpu.make_async_copy(values_hbm.at[z * 2 + c, xh * 2 + xl], values.at[z * 2 + c, xh * 2 + xl], sems.at[i, z, xh])
-        for i, (c, xl) in enumerate(order)
-        for z in range(4)
-        for xh in range(2)
-    ]
-    for copy in copies:
-        copy.start()
+def mix_kernel(place_ref, w0_ref, w1_ref, w2_ref, w3_ref, values, out_ref, weights):
     for d, w in enumerate((w0_ref, w1_ref, w2_ref, w3_ref)):
         share = (place_ref[Y] + d) % 4
         weights[:, pl.ds(pl.multiple_of(share * 32, 32), 32), :] = w[...]
-    for i, (c, xl) in enumerate(order):
-        for copy in copies[i * 8 : i * 8 + 8]:
-            copy.wait()
-        for h in range(3):
-            right = [
-                jnp.concatenate([values[z * 2 + c, xh * 2 + xl, h, rp] for rp in range(2)], axis=1)
-                for z in range(4)
-                for xh in range(2)
-            ]
-            mixed = mm(weights[h], jnp.concatenate(right, axis=0))
-            pair = jnp.concatenate(
-                [mixed[:, :128].reshape(16, 8, 128), mixed[:, 128:].reshape(16, 8, 128)], axis=1
-            )
-            out_ref[:, h, c, xl * 16 : (xl + 1) * 16, :] = pair.astype(BF)
+    for c in range(2):
+        for xl in range(2):
+            for h in range(3):
+                right = [
+                    jnp.concatenate([values[z * 2 + c, xh * 2 + xl, h, rp] for rp in range(2)], axis=1)
+                    for z in range(4)
+                    for xh in range(2)
+                ]
+                mixed = mm(weights[h], jnp.concatenate(right, axis=0))
+                pair = jnp.concatenate(
+                    [mixed[:, :128].reshape(16, 8, 128), mixed[:, 128:].reshape(16, 8, 128)], axis=1
+                )
+                out_ref[:, h, c, xl * 16 : (xl + 1) * 16, :] = pair.astype(BF)
 
 
 def row_mix(place, weights, values):
     vmem = pl.BlockSpec(memory_space=pltpu.VMEM)
     return pl.pallas_call(
         mix_kernel,
-        in_specs=[SCALARS] + [vmem] * 4 + [pl.BlockSpec(memory_space=pltpu.HBM)],
+        in_specs=[SCALARS] + [vmem] * 5,
         out_specs=vmem,
         out_shape=jax.ShapeDtypeStruct((16, 3, 2, 32, 128), BF),
-        scratch_shapes=[
-            pltpu.VMEM((3, 128, 1024), BF),
-            pltpu.VMEM(values.shape, BF),
-            pltpu.SemaphoreType.DMA((4, 4, 2)),
-        ],
-        compiler_params=params(58),
+        scratch_shapes=[pltpu.VMEM((3, 128, 1024), BF)],
+        compiler_params=params(14),
         name="row_mix",
     )(place, *weights, values)
 

time: 182 us -> 179 us (0.984)
  Pallas kernels: 35.9 us -> 29.7 us
  waiting for transfers between devices: 44.4 us -> 46.8 us
    pallas_call x2, Pallas kernels: 9.57 us -> 4.97 us  [the longest x1 3.3 us: key_proj(): pl.pallas_call(key_kernel, grid=(2,), in_specs=[SCALARS, pl.BlockSpec((25...]
    all_gather x2, waiting for transfers between devices: 9.61 us -> 11.6 us  [gather(): lax.all_gather(array, AXES, axis=0, tiled=False, axis_index_groups=groups)]
  transfers between devices with their start and end apart: 11 -> 11, of which waited for: 7 -> 6; matrix products, arithmetic and copies ran while one was open for 2% -> 1% of each run, Pallas kernels for 5% -> 5%
where the time goes in v6:
time: 179 us; the launch traced here: 178 us
  blocking collectives  61 us (34%)
  waiting for transfers between devices  46.8 us (26%)
  Pallas kernels  29.7 us (17%)
  starting transfers between devices  19.4 us (11%)
  between operations  13.5 us (8%)
  local copies, waits for them, and re-layouts  6.49 us (4%)
    all_to_all x2, blocking collectives, swap(): lax.all_to_all(array, AXES, split_axis=0, concat_axis=0, tiled=True, axis...  44 us
    all_to_all x1, waiting for transfers between devices, swap(): lax.all_to_all(array, AXES, split_axis=0, concat_axis=0, tiled=True, axis...  18 us
    all_to_all x1, blocking collectives, local(): out = lax.all_to_all(out, 'seq', split_axis=0, concat_axis=0, tiled=True)  17 us
    pallas_call x1, Pallas kernels, column_part(): pl.pallas_call(column_kernel, in_specs=[vmem] * 7 + [pl.BlockSpec(memory_...  16.7 us
    all_gather x2, waiting for transfers between devices, gather(): lax.all_gather(array, AXES, axis=0, tiled=False, axis_index_groups=groups)  11.6 us
    all_to_all x1, waiting for transfers between devices, local(): x = lax.all_to_all(x, 'seq', split_axis=0, concat_axis=0, tiled=True)  11.1 us
    ppermute x7, starting transfers between devices, send(): return lax.ppermute(array, AXES, shifts(**by))  8.17 us
    all_to_all x1, starting transfers between devices, local(): x = lax.all_to_all(x, 'seq', split_axis=0, concat_axis=0, tiled=True)  7.3 us
  transfers between devices with their start and end apart: 11, of which 6 were waited for; matrix products, arithmetic and copies ran while one was open for 1% of the time, Pallas kernels for 5%

profile of v6, /device:TPU:1, one launch (start us, length us, event | category | flops | bytes accessed | tf_op | source)
XLA Modules:
  0.0 178.1 jit_solution(11487388139135939092)
XLA Ops:
  6.5 0.1 pad_add_fusion.place_ref
  6.6 0.7 copy-done.4
  7.3 3.3 %key_proj.1 = (bf16[512,768]{1,0:T(8,128)(2,1)S(1)}, bf16[3,2,128,128]{3,2,1,0:T(8,128)(2,1)S(1)}, bf16[3,2,128,128]{3,2,1,0:T(8,128)(2,1)S(1)}, bf16[3,2,128,12...) custom-call(s32[4]{0:T(128)S(1)} %pad_add_fusion.place_ref, bf16[512,768]{1,0:T(8,128)(2,1)} %bitcast.31, ...), custom_call_target="tpu_custom_call" | custom-call | tf_op jit(solution)/shard_map/key_proj/pallas_call | solution.py:106
  10.6 2.1 %collective-permute-start.2 = (bf16[3,2,128,128]{3,2,1,0:T(8,128)(2,1)S(1)}, bf16[3,2,128,128]{3,2,1,0:T(8,128)(2,1)S(1)}, u32[]{:S(2)}, u32[]{:S(2)}) collective-permute-start(bf16[3,2,128,128]{3,2,1,0:T(8,128)(2,1)S(1)} %get-tuple-element.22), channel_id=1, source_target_pairs={{0,64},{2,66},{4,68},{6,70},{8,72},{10,74},{12,76},{14,78},{16,80}... | collective-permute-start | bytes 589832 | tf_op jit(solution)/shard_map/ppermute | solution.py:52
  12.7 2.5 %collective-permute-start.1 = (bf16[3,2,128,128]{3,2,1,0:T(8,128)(2,1)S(1)}, bf16[3,2,128,128]{3,2,1,0:T(8,128)(2,1)S(1)}, u32[]{:S(2)}, u32[]{:S(2)}) collective-permute-start(bf16[3,2,128,128]{3,2,1,0:T(8,128)(2,1)S(1)} %get-tuple-element.21), channel_id=1, source_target_pairs={{0,1},{2,3},{4,5},{6,7},{8,9},{10,11},{12,13},{14,15},{16,17},{18,... | collective-permute-start | bytes 589832 | tf_op jit(solution)/shard_map/ppermute | solution.py:52
  15.2 1.2 collective-permute-start
  16.3 2.9 %query_value_proj.1 = bf16[4,2,3,2,128,128]{5,4,3,2,1,0:T(8,128)(2,1)} custom-call(bf16[512,768]{1,0:T(8,128)(2,1)S(1)} %get-tuple-element.23.normed_ref, bf16[768,2304]{1,0:T(8,128)(2,1)S(1)} %copy-done), custom_call_target="tpu_custom_call" | custom-call | tf_op jit(solution)/shard_map/query_value_proj/pallas_call | solution.py:130
  19.2 4.4 %collective-permute-done.1 = bf16[3,2,128,128]{3,2,1,0:T(8,128)(2,1)S(1)} collective-permute-done((bf16[3,2,128,128]{3,2,1,0:T(8,128)(2,1)S(1)}, bf16[3,2,128,128]{3,2,1,0:T(8,128)(2,1)S(1)}, u32[]{:S(2)}, u32[]{:S(2)}) %collective-permute-start.1) | collective-permute-done | bytes 196640 | tf_op jit(solution)/shard_map/ppermute | solution.py:52
  23.7 1.1 pad_maximum_fusion
  24.7 0.0 all-gather.5.cloned.1.call-update
  24.8 3.9 %all-to-all-start = ((bf16[4,2,3,2,128,128]{5,4,3,2,1,0:T(8,128)(2,1)}), bf16[4,2,3,2,128,128]{5,4,3,2,1,0:T(8,128)(2,1)S(1)}, u32[]{:S(2)}, u32[]{:S(2)}) async-start(bf16[4,2,3,2,128,128]{5,4,3,2,1,0:T(8,128)(2,1)} %query_value_proj.1), calls=%async_computation | async-start | bytes 3145728 | tf_op jit(solution)/shard_map/all_to_all | solution.py:44
  28.7 1.0 copy.13
  29.7 18.0 %all-to-all-done = bf16[4,2,3,2,128,128]{5,4,3,2,1,0:T(8,128)(2,1)S(1)} async-done(((bf16[4,2,3,2,128,128]{5,4,3,2,1,0:T(8,128)(2,1)}), bf16[4,2,3,2,128,128]{5,4,3,2,1,0:T(8,128)(2,1)S(1)}, u32[]{:S(2)}, u32[]{:S(2)}) %all-to-all-start) | async-done | bytes 1572896 | tf_op jit(solution)/shard_map/all_to_all | solution.py:44
  47.7 1.0 slice_bitcast_fusion
  48.8 7.3 %all-to-all-start.1 = ((bf16[16,32,768]{2,1,0:T(8,128)(2,1)}), bf16[16,32,768]{2,1,0:T(8,128)(2,1)S(1)}, u32[]{:S(2)}, u32[]{:S(2)}) async-start(bf16[16,32,768]{2,1,0:T(8,128)(2,1)} %bitcast.11), calls=%async_computation.1 | async-start | bytes 1572864 | tf_op jit(solution)/shard_map/all_to_all | solution.py:384
  56.1 0.1 dynamic-slice_bitcast_fusion
  56.1 0.2 collective-permute-start.3
  56.3 1.6 collective-permute-done.3.q1_ref
  57.9 11.1 %all-to-all-done.1.x_ref = bf16[16,32,768]{2,1,0:T(8,128)(2,1)S(1)} async-done(((bf16[16,32,768]{2,1,0:T(8,128)(2,1)}), bf16[16,32,768]{2,1,0:T(8,128)(2,1)S(1)}, u32[]{:S(2)}, u32[]{:S(2)}) %all-to-all-start.1) | async-done | bytes 786464 | tf_op jit(solution)/shard_map/all_to_all | solution.py:384
  69.1 0.3 all-gather.5.cloned.1.call-done
  69.4 4.9 %partial_scores.1 = f32[4,3,32,1024]{3,2,1,0:T(8,128)S(1)} custom-call(s32[4]{0:T(128)S(1)} %pad_add_fusion.place_ref, bf16[4,3,2,64,128]{4,3,2,1,0:T(8,128)(2,1)S(1)} %get-tuple-element.36.q0_ref, bf16[4,3,2,64,128]{4,3,2,1,0:T(8,128)(2,1)S(1)} %collective-permute-done.3.q1_ref, bf16[8,4,3,2,128,128]{5,4,3,2,1,0:T(8,128)(2,1)} %bitcast.29), custom_call_target="tpu_custom_call" | custom-call | tf_op jit(solution)/shard_map/partial_scores/pallas_call | solution.py:193
  74.3 24.1 %all_to_all.25.refs_0_ = f32[4,3,32,1024]{3,2,1,0:T(8,128)S(1)} all-to-all(f32[4,3,32,1024]{3,2,1,0:T(8,128)S(1)} %partial_scores.1), channel_id=1, replica_groups={{0,16,32,48},{1,17,33,49},{2,18,34,50},{3,19,35,51},{4,20,36,52},{5,21,..., dimensions={0} | all-to-all | bytes 3145728 | tf_op jit(solution)/shard_map/all_to_all | solution.py:44
  98.4 0.2 row_softmax.1.w0_ref
  98.6 1.0 collective-permute-start.4
  99.6 1.3 collective-permute-start.5
  100.9 11.3 %all-gather.7.cloned.1.call-done = bf16[32,3,2,128,128]{4,3,2,1,0:T(8,128)(2,1)} async-done(((bf16[4,3,2,128,128]{4,3,2,1,0:T(8,128)(2,1)}), bf16[32,3,2,128,128]{4,3,2,1,0:T(8,128)(2,1)}) %all-gather.7.cloned.1.call-update) | async-done | bytes 6291472 | tf_op jit(solution)/shard_map/all_gather | solution.py:48
  112.2 2.8 %copy-done.1 = bf16[32,3,2,128,128]{4,3,2,1,0:T(8,128)(2,1)S(1)} copy-done((bf16[32,3,2,128,128]{4,3,2,1,0:T(8,128)(2,1)S(1)}, bf16[32,3,2,128,128]{4,3,2,1,0:T(8,128)(2,1)}, u32[]{:S(2)}) %copy-start.1) | copy-done | bytes 6291480
  114.9 1.7 row_mix.1
  116.7 19.9 %all_to_all.26 = bf16[16,3,2,32,128]{4,3,2,1,0:T(8,128)(2,1)S(1)} all-to-all(bf16[16,3,2,32,128]{4,3,2,1,0:T(8,128)(2,1)S(1)} %row_mix.1), channel_id=1, replica_groups={{0,16,32,48,64,80,96,112,1,17,33,49,65,81,97,113},{2,18,34,50,66,82,98,..., dimensions={0} | all-to-all | bytes 1572864 | tf_op jit(solution)/shard_map/all_to_all | solution.py:44
  136.6 16.7 %column_part.1 = bf16[16,32,768]{2,1,0:T(8,128)(2,1)S(1)} custom-call(bf16[16,3,64,128]{3,2,1,0:T(8,128)(2,1)S(1)} %bitcast.27, bf16[16,32,768]{2,1,0:T(8,128)(2,1)S(1)} %all-to-all-done.1.x_ref, f32[768]{0:T(1024)S(1)} %copy-done.5, f32[768]{0:T(1024)S(1)} %copy-done.6, bf16[768,768]{1,0:T(8,128)(2,1)S(1)} %copy-done.2, bf16[768,2304]{1,0:T(8,128)(2,1)} %attend.1, ...), custom_call_target="tpu_custom_call" | custom-call | tf_op jit(solution)/shard_map/column_part/pallas_call | solution.py:341
  153.3 17.0 %all_to_all.27 = bf16[16,32,768]{2,1,0:T(8,128)(2,1)S(1)} all-to-all(bf16[16,32,768]{2,1,0:T(8,128)(2,1)S(1)} %column_part.1), channel_id=1, replica_groups=mesh['seq'=16,'col'=8] {'seq'}, dimensions={0} | all-to-all | bytes 1572864 | tf_op jit(solution)/shard_map/all_to_all | solution.py:401
  170.3 0.9 copy.14
  (23 shorter events, 0.1 us)
Async XLA Ops:
  6.5 62.8 %all-gather.5.cloned.1.call-start = ((), (), s32[]{:S(2)}) async-start(), calls=%async_computation.5 | async-start | bytes 7077888 | tf_op jit(solution)/shard_map/all_gather | solution.py:48
  6.6 0.7 copy-start.4
  7.3 9.0 %copy-start = (bf16[768,2304]{1,0:T(8,128)(2,1)S(1)}, bf16[768,2304]{1,0:T(8,128)(2,1)}, u32[]{:S(2)}) copy-start(bf16[768,2304]{1,0:T(8,128)(2,1)} %w_ref.3) | copy-start | bytes 10616836
  10.6 8.6 %collective-permute-start.2 = (bf16[3,2,128,128]{3,2,1,0:T(8,128)(2,1)S(1)}, bf16[3,2,128,128]{3,2,1,0:T(8,128)(2,1)S(1)}, u32[]{:S(2)}, u32[]{:S(2)}) collective-permute-start(bf16[3,2,128,128]{3,2,1,0:T(8,128)(2,1)S(1)} %get-tuple-element.22), channel_id=1, source_target_pairs={{0,64},{2,66},{4,68},{6,70},{8,72},{10,74},{12,76},{14,78},{16,80}... | collective-permute-start | bytes 589832 | tf_op jit(solution)/shard_map/ppermute | solution.py:52
  12.7 11.0 %collective-permute-start.1 = (bf16[3,2,128,128]{3,2,1,0:T(8,128)(2,1)S(1)}, bf16[3,2,128,128]{3,2,1,0:T(8,128)(2,1)S(1)}, u32[]{:S(2)}, u32[]{:S(2)}) collective-permute-start(bf16[3,2,128,128]{3,2,1,0:T(8,128)(2,1)S(1)} %get-tuple-element.21), channel_id=1, source_target_pairs={{0,1},{2,3},{4,5},{6,7},{8,9},{10,11},{12,13},{14,15},{16,17},{18,... | collective-permute-start | bytes 589832 | tf_op jit(solution)/shard_map/ppermute | solution.py:52
  15.2 8.5 %collective-permute-start = (bf16[3,2,128,128]{3,2,1,0:T(8,128)(2,1)S(1)}, bf16[3,2,128,128]{3,2,1,0:T(8,128)(2,1)S(1)}, u32[]{:S(2)}, u32[]{:S(2)}) collective-permute-start(bf16[3,2,128,128]{3,2,1,0:T(8,128)(2,1)S(1)} %get-tuple-element.20), channel_id=1, source_target_pairs={{0,65},{2,67},{4,69},{6,71},{8,73},{10,75},{12,77},{14,79},{16,81}... | collective-permute-start | bytes 589832 | tf_op jit(solution)/shard_map/ppermute | solution.py:52
  24.8 3.9 %copy-start.7 = (bf16[4,128,768]{2,1,0:T(8,128)(2,1)S(1)}, bf16[4,128,768]{2,1,0:T(8,128)(2,1)}, u32[]{:S(2)}) copy-start(bf16[4,128,768]{2,1,0:T(8,128)(2,1)} %param.10) | copy-start | bytes 2359300
  24.8 22.9 %all-to-all-start = ((bf16[4,2,3,2,128,128]{5,4,3,2,1,0:T(8,128)(2,1)}), bf16[4,2,3,2,128,128]{5,4,3,2,1,0:T(8,128)(2,1)S(1)}, u32[]{:S(2)}, u32[]{:S(2)}) async-start(bf16[4,2,3,2,128,128]{5,4,3,2,1,0:T(8,128)(2,1)} %query_value_proj.1), calls=%async_computation | async-start | bytes 3145728 | tf_op jit(solution)/shard_map/all_to_all | solution.py:44
  28.7 83.4 %all-gather.7.cloned.1.call-start = ((), (), s32[]{:S(2)}) async-start(), calls=%async_computation.6 | async-start | bytes 7077888 | tf_op jit(solution)/shard_map/all_gather | solution.py:48
  48.8 20.3 %all-to-all-start.1 = ((bf16[16,32,768]{2,1,0:T(8,128)(2,1)}), bf16[16,32,768]{2,1,0:T(8,128)(2,1)S(1)}, u32[]{:S(2)}, u32[]{:S(2)}) async-start(bf16[16,32,768]{2,1,0:T(8,128)(2,1)} %bitcast.11), calls=%async_computation.1 | async-start | bytes 1572864 | tf_op jit(solution)/shard_map/all_to_all | solution.py:384
  56.1 1.8 %collective-permute-start.3 = (bf16[4,3,2,64,128]{4,3,2,1,0:T(8,128)(2,1)S(1)}, bf16[4,3,2,64,128]{4,3,2,1,0:T(8,128)(2,1)S(1)}, u32[]{:S(2)}, u32[]{:S(2)}) collective-permute-start(bf16[4,3,2,64,128]{4,3,2,1,0:T(8,128)(2,1)S(1)} %get-tuple-element.35), channel_id=1, source_target_pairs={{0,8},{2,10},{4,12},{6,14},{8,0},{10,2},{12,4},{14,6},{16,24},{18,... | collective-permute-start | bytes 1179656 | tf_op jit(solution)/shard_map/ppermute | solution.py:52
  98.6 13.5 %collective-permute-start.4 = (bf16[3,32,1024]{2,1,0:T(8,128)(2,1)S(1)}, bf16[3,32,1024]{2,1,0:T(8,128)(2,1)S(1)}, u32[]{:S(2)}, u32[]{:S(2)}) collective-permute-start(bf16[3,32,1024]{2,1,0:T(8,128)(2,1)S(1)} %row_softmax.1.w0_ref), channel_id=1, source_target_pairs={{0,48},{2,50},{4,52},{6,54},{8,56},{10,58},{12,60},{14,62},{16,0},... | collective-permute-start | bytes 589832 | tf_op jit(solution)/shard_map/ppermute | solution.py:52
  99.6 12.6 %collective-permute-start.5 = (bf16[3,32,1024]{2,1,0:T(8,128)(2,1)S(1)}, bf16[3,32,1024]{2,1,0:T(8,128)(2,1)S(1)}, u32[]{:S(2)}, u32[]{:S(2)}) collective-permute-start(bf16[3,32,1024]{2,1,0:T(8,128)(2,1)S(1)} %row_softmax.1.w0_ref), channel_id=1, source_target_pairs={{0,32},{2,34},{4,36},{6,38},{8,40},{10,42},{12,44},{14,46},{16,48}... | collective-permute-start | bytes 589832 | tf_op jit(solution)/shard_map/ppermute | solution.py:52
  100.9 11.3 %collective-permute-start.6 = (bf16[3,32,1024]{2,1,0:T(8,128)(2,1)S(1)}, bf16[3,32,1024]{2,1,0:T(8,128)(2,1)S(1)}, u32[]{:S(2)}, u32[]{:S(2)}) collective-permute-start(bf16[3,32,1024]{2,1,0:T(8,128)(2,1)S(1)} %row_softmax.1.w0_ref), channel_id=1, source_target_pairs={{0,16},{2,18},{4,20},{6,22},{8,24},{10,26},{12,28},{14,30},{16,32}... | collective-permute-start | bytes 589832 | tf_op jit(solution)/shard_map/ppermute | solution.py:52
  112.1 2.8 %copy-start.1 = (bf16[32,3,2,128,128]{4,3,2,1,0:T(8,128)(2,1)S(1)}, bf16[32,3,2,128,128]{4,3,2,1,0:T(8,128)(2,1)}, u32[]{:S(2)}) copy-start(bf16[32,3,2,128,128]{4,3,2,1,0:T(8,128)(2,1)} %all-gather.7.cloned.1.call-done) | copy-start | bytes 18874372
  114.9 21.6 %copy-start.3 = (bf16[768,768]{1,0:T(8,128)(2,1)S(1)}, bf16[768,768]{1,0:T(8,128)(2,1)}, u32[]{:S(2)}) copy-start(bf16[768,768]{1,0:T(8,128)(2,1)} %exit_col.1) | copy-start | bytes 3538948
  116.6 19.9 %copy-start.2 = (bf16[768,768]{1,0:T(8,128)(2,1)S(1)}, bf16[768,768]{1,0:T(8,128)(2,1)}, u32[]{:S(2)}) copy-start(bf16[768,768]{1,0:T(8,128)(2,1)} %exit_row.1) | copy-start | bytes 3538948
  116.6 19.9 %copy-start.5 = (f32[768]{0:T(1024)S(1)}, f32[768]{0:T(1024)}, u32[]{:S(2)}) copy-start(f32[768]{0:T(1024)} %gain_col_ref.1) | copy-start | bytes 9220
  116.6 19.9 %copy-start.6 = (f32[768]{0:T(1024)S(1)}, f32[768]{0:T(1024)}, u32[]{:S(2)}) copy-start(f32[768]{0:T(1024)} %gain_ffn_ref.1) | copy-start | bytes 9220
Sparse Core Ops, SparseCore 0:
  24.9 44.4 all-gather.4
  71.1 41.0 all-gather.6

commit v7 on v5

--- a/solution.py
+++ b/solution.py
@@ -81,18 +81,16 @@
 
 def write_pairs(normed, weight, out):
     low = lax.broadcasted_iota(jnp.int32, (128, 128), 1) < E
-    for rp in range(2):
-        first = mm(normed[2 * rp * 128 : (2 * rp + 1) * 128, :], weight)
-        second = mm(normed[(2 * rp + 1) * 128 : (2 * rp + 2) * 128, :], weight)
-        for t in range(6):
-            a, b = first[:, t * 128 : (t + 1) * 128], second[:, t * 128 : (t + 1) * 128]
-            pair = (
-                jnp.where(low, a, pltpu.roll(b, E, 1)),
-                jnp.where(low, pltpu.roll(a, E, 1), b),
-            )
-            for k in range(2):
-                g, h = (2 * t + k) // 3, (2 * t + k) % 3
-                out[g, h, rp] = pair[k].astype(BF)
+    first, second = mm(normed[:128, :], weight), mm(normed[128:, :], weight)
+    for t in range(6):
+        a, b = first[:, t * 128 : (t + 1) * 128], second[:, t * 128 : (t + 1) * 128]
+        pair = (
+            jnp.where(low, a, pltpu.roll(b, E, 1)),
+            jnp.where(low, pltpu.roll(a, E, 1), b),
+        )
+        for k in range(2):
+            g, h = (2 * t + k) // 3, (2 * t + k) % 3
+            out[g, h] = pair[k].astype(BF)
 
 
 def key_kernel(place_ref, x_ref, gain_ref, w_ref, normed_ref, *refs):
@@ -100,30 +98,32 @@
     outs, pieces = refs[:4], refs[4]
     write_pairs(normed_ref[...], w_ref[...], pieces)
     for s, out in enumerate(outs):
-        out[...] = pieces[(place_ref[X] + s) % 4]
+        out[:, 0] = pieces[(place_ref[X] + s) % 4]
 
 
 def key_proj(place, x, gain, weight):
     piece = (3, 2, 128, 128)
     return pl.pallas_call(
         key_kernel,
-        grid=(1,),
+        grid=(2,),
         in_specs=[
             SCALARS,
-            pl.BlockSpec((512, 768), lambda i: (0, 0)),
+            pl.BlockSpec((256, 768), lambda i: (i, 0)),
             pl.BlockSpec((768,), lambda i: (0,)),
             pl.BlockSpec((768, 768), lambda i: (0, 1)),
         ],
-        out_specs=[pl.BlockSpec((512, 768), lambda i: (0, 0))] + [pl.BlockSpec(piece, lambda i: (0, 0, 0, 0))] * 4,
+        out_specs=[pl.BlockSpec((256, 768), lambda i: (i, 0))]
+        + [pl.BlockSpec((3, 1, 128, 128), lambda i: (0, i, 0, 0))] * 4,
         out_shape=[jax.ShapeDtypeStruct((512, 768), BF)] + [jax.ShapeDtypeStruct(piece, BF)] * 4,
-        scratch_shapes=[pltpu.VMEM((4,) + piece, BF)],
-        compiler_params=params(56),
+        scratch_shapes=[pltpu.VMEM((4, 3, 128, 128), BF)],
+        compiler_params=params(52),
         name="key_proj",
     )(place, x, gain, weight)
 
 
 def query_value_kernel(normed_ref, w_ref, out_ref):
-    write_pairs(normed_ref[...], w_ref[...], out_ref.at[:, 0])
+    for rp in range(2):
+        write_pairs(normed_ref[rp * 256 : (rp + 1) * 256, :], w_ref[...], out_ref.at[:, 0, :, rp])
 
 
 def query_value_proj(normed, weight):
@@ -145,12 +145,17 @@
     return [pieces[0], send(pieces[3], dx=3), send(pieces[2], dx=2), send(pieces[1], dx=1)]
 
 
-def scores_kernel(place_ref, q0_ref, q1_ref, keys_hbm, out_ref, keys, sems):
+def scores_kernel(place_ref, q0_ref, q1_ref, *refs):
+    own, keys_hbm, out_ref, keys, sems = refs[:8], *refs[8:]
     copies = [
-        pltpu.make_async_copy(keys_hbm.at[z * 2 : z * 2 + 2], keys.at[z * 2 : z * 2 + 2], sems.at[z]) for z in range(4)
+        pltpu.make_async_copy(keys_hbm.at[z * 2 : z * 2 + 2], keys.at[z * 2 : z * 2 + 2, 1:], sems.at[z])
+        for z in range(4)
     ]
     for copy in copies:
         copy.start()
+    for i, block in enumerate(own):
+        z = (place_ref[Z] + (0, 3, 1, 2)[i % 4]) % 4
+        keys[z * 2 + (place_ref[CORE] + i // 4) % 2, 0] = block[...]
     left = [
         jnp.concatenate(
             [
@@ -188,17 +193,17 @@
             out_ref[:, h, :, z * 256 : (z + 1) * 256] = scores.reshape(4, 32, 256)
 
 
-def partial_scores(place, q0, q1, keys):
+def partial_scores(place, q0, q1, own, keys):
     vmem = pl.BlockSpec(memory_space=pltpu.VMEM)
     return pl.pallas_call(
         scores_kernel,
-        in_specs=[SCALARS, vmem, vmem, pl.BlockSpec(memory_space=pltpu.HBM)],
+        in_specs=[SCALARS] + [vmem] * 10 + [pl.BlockSpec(memory_space=pltpu.HBM)],
         out_specs=vmem,
         out_shape=jax.ShapeDtypeStruct((4, 3, 32, 1024), F32),
-        scratch_shapes=[pltpu.VMEM(keys.shape, BF), pltpu.SemaphoreType.DMA((4,))],
-        compiler_params=params(56),
+        scratch_shapes=[pltpu.VMEM((8, 4, 3, 2, 128, 128), BF), pltpu.SemaphoreType.DMA((4,))],
+        compiler_params=params(48),
         name="partial_scores",
-    )(place, q0, q1, keys)
+    )(place, q0, q1, *own, keys)
 
 
 def softmax_kernel(scale, parts_ref, out_ref):
@@ -259,18 +264,19 @@
             pltpu.VMEM(values.shape, BF),
             pltpu.SemaphoreType.DMA((4, 4, 2)),
         ],
-        compiler_params=params(58),
+        compiler_params=params(52),
         name="row_mix",
     )(place, *weights, values)
 
 
 def column_kernel(
-    mix_ref, x_ref, gain_col_ref, gain_ffn_ref, exit_row, attend, exit_col, expand_hbm, shrink_hbm,
-    out_ref, qkv, stream, scratch, expand, shrink, sems,
+    mix_ref, x_ref, gain_col_ref, gain_ffn_ref, exit_row, exit_col, attend_hbm, expand_hbm, shrink_hbm,
+    out_ref, qkv, stream, scratch, attend, expand, shrink, sems,
 ):
     copies = [
-        pltpu.make_async_copy(expand_hbm, expand, sems.at[0]),
-        pltpu.make_async_copy(shrink_hbm, shrink, sems.at[1]),
+        pltpu.make_async_copy(attend_hbm, attend, sems.at[0]),
+        pltpu.make_async_copy(expand_hbm, expand, sems.at[1]),
+        pltpu.make_async_copy(shrink_hbm, shrink, sems.at[2]),
     ]
     for copy in copies:
         copy.start()
@@ -301,6 +307,7 @@
         ],
         axis=1,
     )
+    copies[0].wait()
     qkv[...] = mm(normed, attend[...]).astype(BF)
     group = lax.broadcasted_iota(jnp.int32, (256, 256), 0) // E == lax.broadcasted_iota(jnp.int32, (256, 256), 1) // E
     group = group.astype(F32).astype(BF)
@@ -338,8 +345,8 @@
     stream[...] += mm(mixed, exit_col[...])
 
     normed = normalize(stream[...], gain_ffn_ref[...][None, :])
-    for copy in copies:
-        copy.wait()
+    copies[1].wait()
+    copies[2].wait()
     for f in range(6):
         cols = slice(f * 512, (f + 1) * 512)
         pre = mm(normed, expand[:, cols])
@@ -354,20 +361,21 @@
     vmem = pl.BlockSpec(memory_space=pltpu.VMEM)
     return pl.pallas_call(
         column_kernel,
-        in_specs=[vmem] * 7 + [pl.BlockSpec(memory_space=pltpu.HBM)] * 2,
+        in_specs=[vmem] * 6 + [pl.BlockSpec(memory_space=pltpu.HBM)] * 3,
         out_specs=vmem,
         out_shape=jax.ShapeDtypeStruct((16, 32, 768), BF),
         scratch_shapes=[
             pltpu.VMEM((512, 2304), BF),
             pltpu.VMEM((512, 768), F32),
             pltpu.VMEM((6, 512, 128), F32),
+            pltpu.VMEM(attend.shape, BF),
             pltpu.VMEM(expand.shape, BF),
             pltpu.VMEM(shrink.shape, BF),
-            pltpu.SemaphoreType.DMA((2,)),
+            pltpu.SemaphoreType.DMA((3,)),
         ],
         compiler_params=params(48),
         name="column_part",
-    )(mix, x, gain_col, gain_ffn, exit_row, attend, exit_col, expand, shrink)
+    )(mix, x, gain_col, gain_ffn, exit_row, exit_col, attend, expand, shrink)
 
 
 def local(
@@ -391,10 +399,13 @@
     keys = over_x(keys)
     queries_values = query_value_proj(normed, attend_row)
     x = embeddings.reshape(4, 2, 8, 8, 768).transpose(2, 1, 0, 3, 4).reshape(16, 32, 768)
-    keys, queries_values = lax.optimization_barrier((jnp.stack(keys), queries_values))
+    own, *keys = keys
+    keys, own, queries_values = lax.optimization_barrier((jnp.stack(keys), own, queries_values))
 
     keys_all = gather(keys, Z_COLUMNS)
-    queries_values, x = lax.optimization_barrier((swap(queries_values, X_RINGS), x))
+    own = [own] + [send(own, dz=dz) for dz in (1, 3, 2)]
+    queries_values, x = lax.optimization_barrier((swap(queries_values, X_RINGS), x, *own))[:2]
+    own = own + [to_other_core(k) for k in own]
     x = lax.all_to_all(x, "seq", split_axis=0, concat_axis=0, tiled=True)
     queries, values = queries_values[:, 0], queries_values[:, 1]
     values = lax.optimization_barrier((values, keys))[0]
@@ -402,8 +413,8 @@
 
     queries0 = lax.dynamic_slice_in_dim(queries, core * 64, 64, axis=3)
     queries1 = to_other_core(lax.dynamic_slice_in_dim(queries, (1 - core) * 64, 64, axis=3))
-    keys = lax.optimization_barrier((keys_all, x, queries1))[0]
-    scores = partial_scores(place, queries0, queries1, keys)
+    keys = lax.optimization_barrier((keys_all, x, queries1, *own))[0]
+    scores = partial_scores(place, queries0, queries1, own, keys)
     scores, x = lax.optimization_barrier((scores, x))
     weights = row_softmax(swap(scores, Y_RINGS), scale)
     values = lax.optimization_barrier((values, weights))[0]

time: 182 us -> 173 us (0.951)
  starting transfers between devices: 19.4 us -> 25.9 us
  waiting for transfers between devices: 44.4 us -> 38.9 us
  Pallas kernels: 35.9 us -> 32.1 us
  blocking collectives: 60.8 us -> 57.8 us
  local copies, waits for them, and re-layouts: 5.62 us -> 3.7 us
    all_to_all x1, waiting for transfers between devices: 17.8 us -> 6.32 us  [swap(): lax.all_to_all(array, AXES, split_axis=0, concat_axis=0, tiled=True, axis...]
    ppermute x7 -> x14, waiting for transfers between devices: 6.53 us -> 14.2 us  [send(): return lax.ppermute(array, AXES, shifts(**by))]
    ppermute x7 -> x14, starting transfers between devices: 8.01 us -> 14.6 us  [send(): return lax.ppermute(array, AXES, shifts(**by))]
    all_to_all x2, blocking collectives: 43.8 us -> 40.7 us  [swap(): lax.all_to_all(array, AXES, split_axis=0, concat_axis=0, tiled=True, axis...]
    pallas_call x3, Pallas kernels: 27.1 us -> 24.8 us  [the longest x1 16.7 us: column_part(): pl.pallas_call(column_kernel, in_specs=[vmem] * 6 + [pl.BlockSpec(memory_...]
  transfers between devices with their start and end apart: 11 -> 18, of which waited for: 7 -> 11; matrix products, arithmetic and copies ran while one was open for 2% -> 1% of each run, Pallas kernels for 5% -> 5%
where the time goes in v7:
time: 173 us
  blocking collectives  57.8 us (33%)
  waiting for transfers between devices  38.9 us (22%)
  Pallas kernels  32.1 us (19%)
  starting transfers between devices  25.9 us (15%)
  between operations  13.5 us (8%)
  local copies, waits for them, and re-layouts  3.7 us (2%)
    all_to_all x2, blocking collectives, swap(): lax.all_to_all(array, AXES, split_axis=0, concat_axis=0, tiled=True, axis...  40.7 us
    all_to_all x1, blocking collectives, local(): out = lax.all_to_all(out, 'seq', split_axis=0, concat_axis=0, tiled=True)  17.2 us
    pallas_call x1, Pallas kernels, column_part(): pl.pallas_call(column_kernel, in_specs=[vmem] * 6 + [pl.BlockSpec(memory_...  16.7 us
    ppermute x14, starting transfers between devices, send(): return lax.ppermute(array, AXES, shifts(**by))  14.6 us
    ppermute x14, waiting for transfers between devices, send(): return lax.ppermute(array, AXES, shifts(**by))  14.2 us
    all_to_all x1, waiting for transfers between devices, local(): x = lax.all_to_all(x, 'seq', split_axis=0, concat_axis=0, tiled=True)  9.79 us
    all_gather x2, waiting for transfers between devices, gather(): lax.all_gather(array, AXES, axis=0, tiled=False, axis_index_groups=groups)  8.53 us
    all_to_all x1, starting transfers between devices, local(): x = lax.all_to_all(x, 'seq', split_axis=0, concat_axis=0, tiled=True)  7.3 us
  transfers between devices with their start and end apart: 18, of which 11 were waited for; matrix products, arithmetic and copies ran while one was open for 1% of the time, Pallas kernels for 5%

profile of v7, /device:TPU:1, one launch (start us, length us, event | category | flops | bytes accessed | tf_op | source)
XLA Modules:
  0.0 172.8 jit_solution(12485752483217685008)
XLA Ops:
  6.6 0.7 copy-done.3
  7.3 3.3 %key_proj.1 = (bf16[512,768]{1,0:T(8,128)(2,1)S(1)}, bf16[3,2,128,128]{3,2,1,0:T(8,128)(2,1)S(1)}, bf16[3,2,128,128]{3,2,1,0:T(8,128)(2,1)S(1)}, bf16[3,2,128,12...) custom-call(s32[4]{0:T(128)S(1)} %pad_add_fusion.place_ref, bf16[512,768]{1,0:T(8,128)(2,1)} %bitcast.29, ...), custom_call_target="tpu_custom_call" | custom-call | tf_op jit(solution)/shard_map/key_proj/pallas_call | solution.py:106
  10.6 2.1 %collective-permute-start.2 = (bf16[3,2,128,128]{3,2,1,0:T(8,128)(2,1)S(1)}, bf16[3,2,128,128]{3,2,1,0:T(8,128)(2,1)S(1)}, u32[]{:S(2)}, u32[]{:S(2)}) collective-permute-start(bf16[3,2,128,128]{3,2,1,0:T(8,128)(2,1)S(1)} %get-tuple-element.22), channel_id=1, source_target_pairs={{0,64},{2,66},{4,68},{6,70},{8,72},{10,74},{12,76},{14,78},{16,80}... | collective-permute-start | bytes 589832 | tf_op jit(solution)/shard_map/ppermute | solution.py:52
  12.7 2.5 %collective-permute-start.1 = (bf16[3,2,128,128]{3,2,1,0:T(8,128)(2,1)S(1)}, bf16[3,2,128,128]{3,2,1,0:T(8,128)(2,1)S(1)}, u32[]{:S(2)}, u32[]{:S(2)}) collective-permute-start(bf16[3,2,128,128]{3,2,1,0:T(8,128)(2,1)S(1)} %get-tuple-element.21), channel_id=1, source_target_pairs={{0,1},{2,3},{4,5},{6,7},{8,9},{10,11},{12,13},{14,15},{16,17},{18,... | collective-permute-start | bytes 589832 | tf_op jit(solution)/shard_map/ppermute | solution.py:52
  15.2 1.2 collective-permute-start
  16.3 2.9 %query_value_proj.1 = bf16[4,2,3,2,128,128]{5,4,3,2,1,0:T(8,128)(2,1)} custom-call(bf16[512,768]{1,0:T(8,128)(2,1)S(1)} %get-tuple-element.24.normed_ref, bf16[768,2304]{1,0:T(8,128)(2,1)S(1)} %copy-done), custom_call_target="tpu_custom_call" | custom-call | tf_op jit(solution)/shard_map/query_value_proj/pallas_call | solution.py:130
  19.2 4.5 %collective-permute-done.1 = bf16[3,2,128,128]{3,2,1,0:T(8,128)(2,1)S(1)} collective-permute-done((bf16[3,2,128,128]{3,2,1,0:T(8,128)(2,1)S(1)}, bf16[3,2,128,128]{3,2,1,0:T(8,128)(2,1)S(1)}, u32[]{:S(2)}, u32[]{:S(2)}) %collective-permute-start.1) | collective-permute-done | bytes 196640 | tf_op jit(solution)/shard_map/ppermute | solution.py:52
  23.7 0.9 pad_maximum_fusion
  24.6 3.9 %all-to-all-start = ((bf16[4,2,3,2,128,128]{5,4,3,2,1,0:T(8,128)(2,1)}), bf16[4,2,3,2,128,128]{5,4,3,2,1,0:T(8,128)(2,1)S(1)}, u32[]{:S(2)}, u32[]{:S(2)}) async-start(bf16[4,2,3,2,128,128]{5,4,3,2,1,0:T(8,128)(2,1)} %query_value_proj.1), calls=%async_computation | async-start | bytes 3145728 | tf_op jit(solution)/shard_map/all_to_all | solution.py:44
  28.5 1.8 %collective-permute-start.3 = (bf16[3,2,128,128]{3,2,1,0:T(8,128)(2,1)S(1)}, bf16[3,2,128,128]{3,2,1,0:T(8,128)(2,1)S(1)}, u32[]{:S(2)}, u32[]{:S(2)}) collective-permute-start(bf16[3,2,128,128]{3,2,1,0:T(8,128)(2,1)S(1)} %get-tuple-element.26.refs_0_), channel_id=1, source_target_pairs={{0,2},{2,4},{4,6},{6,0},{8,10},{10,12},{12,14},{14,8},{16,18},{18,... | collective-permute-start | bytes 589832 | tf_op jit(solution)/shard_map/ppermute | solution.py:52
  30.3 2.2 %collective-permute-start.4 = (bf16[3,2,128,128]{3,2,1,0:T(8,128)(2,1)S(1)}, bf16[3,2,128,128]{3,2,1,0:T(8,128)(2,1)S(1)}, u32[]{:S(2)}, u32[]{:S(2)}) collective-permute-start(bf16[3,2,128,128]{3,2,1,0:T(8,128)(2,1)S(1)} %get-tuple-element.26.refs_0_), channel_id=1, source_target_pairs={{0,6},{2,0},{4,2},{6,4},{8,14},{10,8},{12,10},{14,12},{16,22},{18,... | collective-permute-start | bytes 589832 | tf_op jit(solution)/shard_map/ppermute | solution.py:52
  32.5 1.2 collective-permute-start.5
  33.8 1.0 copy.13
  34.8 1.4 collective-permute-done.3.refs_1_
  36.1 5.1 %collective-permute-done.5.refs_3_ = bf16[3,2,128,128]{3,2,1,0:T(8,128)(2,1)S(1)} collective-permute-done((bf16[3,2,128,128]{3,2,1,0:T(8,128)(2,1)S(1)}, bf16[3,2,128,128]{3,2,1,0:T(8,128)(2,1)S(1)}, u32[]{:S(2)}, u32[]{:S(2)}) %collective-permute-start.5) | collective-permute-done | bytes 196640 | tf_op jit(solution)/shard_map/ppermute | solution.py:52
  41.2 6.3 %all-to-all-done = bf16[4,2,3,2,128,128]{5,4,3,2,1,0:T(8,128)(2,1)S(1)} async-done(((bf16[4,2,3,2,128,128]{5,4,3,2,1,0:T(8,128)(2,1)}), bf16[4,2,3,2,128,128]{5,4,3,2,1,0:T(8,128)(2,1)S(1)}, u32[]{:S(2)}, u32[]{:S(2)}) %all-to-all-start) | async-done | bytes 1572896 | tf_op jit(solution)/shard_map/all_to_all | solution.py:44
  47.6 1.0 slice_bitcast_fusion
  48.6 7.3 %all-to-all-start.1 = ((bf16[16,32,768]{2,1,0:T(8,128)(2,1)}), bf16[16,32,768]{2,1,0:T(8,128)(2,1)S(1)}, u32[]{:S(2)}, u32[]{:S(2)}) async-start(bf16[16,32,768]{2,1,0:T(8,128)(2,1)} %bitcast.10), calls=%async_computation.1 | async-start | bytes 1572864 | tf_op jit(solution)/shard_map/all_to_all | solution.py:409
  56.7 0.4 collective-permute-start.9
  57.2 1.1 collective-permute-done.7.refs_4_
  59.1 9.8 %all-to-all-done.1.x_ref = bf16[16,32,768]{2,1,0:T(8,128)(2,1)S(1)} async-done(((bf16[16,32,768]{2,1,0:T(8,128)(2,1)}), bf16[16,32,768]{2,1,0:T(8,128)(2,1)S(1)}, u32[]{:S(2)}, u32[]{:S(2)}) %all-to-all-start.1) | async-done | bytes 786464 | tf_op jit(solution)/shard_map/all_to_all | solution.py:409
  68.9 4.8 %partial_scores.1 = f32[4,3,32,1024]{3,2,1,0:T(8,128)S(1)} custom-call(s32[4]{0:T(128)S(1)} %pad_add_fusion.place_ref, bf16[4,3,2,64,128]{4,3,2,1,0:T(8,128)(2,1)S(1)} %get-tuple-element.38.q0_ref, bf16[4,3,2,64,128]{4,3,2,1,0:T(8,128)(2,1)S(1)} %collective-permute-done.6.q1_ref, bf16[3,2,128,128]{3,2,1,0:T(8,128)(2,1)S(1)} %get-tuple-element.26.refs_0_, ...), custom_call_target="tpu_custom_call" | custom-call | tf_op jit(solution)/shard_map/partial_scores/pallas_call | solution.py:198
  73.7 22.3 %all_to_all.25.refs_0_ = f32[4,3,32,1024]{3,2,1,0:T(8,128)S(1)} all-to-all(f32[4,3,32,1024]{3,2,1,0:T(8,128)S(1)} %partial_scores.1), channel_id=1, replica_groups={{0,16,32,48},{1,17,33,49},{2,18,34,50},{3,19,35,51},{4,20,36,52},{5,21,..., dimensions={0} | all-to-all | bytes 3145728 | tf_op jit(solution)/shard_map/all_to_all | solution.py:44
  96.2 1.0 collective-permute-start.11
  97.2 1.5 collective-permute-start.12
  98.7 8.5 %all-gather.7.cloned.1.call-done = bf16[32,3,2,128,128]{4,3,2,1,0:T(8,128)(2,1)} async-done(((bf16[4,3,2,128,128]{4,3,2,1,0:T(8,128)(2,1)}), bf16[32,3,2,128,128]{4,3,2,1,0:T(8,128)(2,1)}) %all-gather.7.cloned.1.call-update) | async-done | bytes 6291472 | tf_op jit(solution)/shard_map/all_gather | solution.py:48
  107.2 1.3 collective-permute-done.13.w3_ref
  108.6 4.1 %row_mix.1 = bf16[16,3,2,32,128]{4,3,2,1,0:T(8,128)(2,1)S(1)} custom-call(s32[4]{0:T(128)S(1)} %pad_add_fusion.place_ref, bf16[3,32,1024]{2,1,0:T(8,128)(2,1)S(1)} %row_softmax.1.w0_ref, bf16[3,32,1024]{2,1,0:T(8,128)(2,1)S(1)} %collective-permute-done.11.w1_ref, bf16[3,32,1024]{2,1,0:T(8,128)(2,1)S(1)} %collective-permute-done.12.w2_ref, ...), custom_call_target="tpu_custom_call" | custom-call | tf_op jit(solution)/shard_map/row_mix/pallas_call | solution.py:257
  112.7 18.4 %all_to_all.26 = bf16[16,3,2,32,128]{4,3,2,1,0:T(8,128)(2,1)S(1)} all-to-all(bf16[16,3,2,32,128]{4,3,2,1,0:T(8,128)(2,1)S(1)} %row_mix.1), channel_id=1, replica_groups={{0,16,32,48,64,80,96,112,1,17,33,49,65,81,97,113},{2,18,34,50,66,82,98,..., dimensions={0} | all-to-all | bytes 1572864 | tf_op jit(solution)/shard_map/all_to_all | solution.py:44
  131.2 16.7 %column_part.1 = bf16[16,32,768]{2,1,0:T(8,128)(2,1)S(1)} custom-call(bf16[16,3,64,128]{3,2,1,0:T(8,128)(2,1)S(1)} %bitcast.25, bf16[16,32,768]{2,1,0:T(8,128)(2,1)S(1)} %all-to-all-done.1.x_ref, f32[768]{0:T(1024)S(1)} %copy-done.4, f32[768]{0:T(1024)S(1)} %copy-done.5, bf16[768,768]{1,0:T(8,128)(2,1)S(1)} %copy-done.1, bf16[768,768]{1,0:T(8,128)(2,1)S(1)} %copy-done.2, ...), custom_call_target="tpu_custom_call" | custom-call | tf_op jit(solution)/shard_map/column_part/pallas_call | solution.py:362
  147.9 17.2 %all_to_all.27 = bf16[16,32,768]{2,1,0:T(8,128)(2,1)S(1)} all-to-all(bf16[16,32,768]{2,1,0:T(8,128)(2,1)S(1)} %column_part.1), channel_id=1, replica_groups=mesh['seq'=16,'col'=8] {'seq'}, dimensions={0} | all-to-all | bytes 1572864 | tf_op jit(solution)/shard_map/all_to_all | solution.py:426
  165.1 0.9 copy.14
  (35 shorter events, 2.1 us)
Async XLA Ops:
  6.5 62.4 %all-gather.5.cloned.1.call-start = ((), (), s32[]{:S(2)}) async-start(), calls=%async_computation.5 | async-start | bytes 5308416 | tf_op jit(solution)/shard_map/all_gather | solution.py:48
  6.6 0.7 copy-start.3
  7.3 9.0 %copy-start = (bf16[768,2304]{1,0:T(8,128)(2,1)S(1)}, bf16[768,2304]{1,0:T(8,128)(2,1)}, u32[]{:S(2)}) copy-start(bf16[768,2304]{1,0:T(8,128)(2,1)} %w_ref.3) | copy-start | bytes 10616836
  10.6 8.6 %collective-permute-start.2 = (bf16[3,2,128,128]{3,2,1,0:T(8,128)(2,1)S(1)}, bf16[3,2,128,128]{3,2,1,0:T(8,128)(2,1)S(1)}, u32[]{:S(2)}, u32[]{:S(2)}) collective-permute-start(bf16[3,2,128,128]{3,2,1,0:T(8,128)(2,1)S(1)} %get-tuple-element.22), channel_id=1, source_target_pairs={{0,64},{2,66},{4,68},{6,70},{8,72},{10,74},{12,76},{14,78},{16,80}... | collective-permute-start | bytes 589832 | tf_op jit(solution)/shard_map/ppermute | solution.py:52
  12.7 11.0 %collective-permute-start.1 = (bf16[3,2,128,128]{3,2,1,0:T(8,128)(2,1)S(1)}, bf16[3,2,128,128]{3,2,1,0:T(8,128)(2,1)S(1)}, u32[]{:S(2)}, u32[]{:S(2)}) collective-permute-start(bf16[3,2,128,128]{3,2,1,0:T(8,128)(2,1)S(1)} %get-tuple-element.21), channel_id=1, source_target_pairs={{0,1},{2,3},{4,5},{6,7},{8,9},{10,11},{12,13},{14,15},{16,17},{18,... | collective-permute-start | bytes 589832 | tf_op jit(solution)/shard_map/ppermute | solution.py:52
  15.2 8.5 %collective-permute-start = (bf16[3,2,128,128]{3,2,1,0:T(8,128)(2,1)S(1)}, bf16[3,2,128,128]{3,2,1,0:T(8,128)(2,1)S(1)}, u32[]{:S(2)}, u32[]{:S(2)}) collective-permute-start(bf16[3,2,128,128]{3,2,1,0:T(8,128)(2,1)S(1)} %get-tuple-element.20), channel_id=1, source_target_pairs={{0,65},{2,67},{4,69},{6,71},{8,73},{10,75},{12,77},{14,79},{16,81}... | collective-permute-start | bytes 589832 | tf_op jit(solution)/shard_map/ppermute | solution.py:52
  24.6 9.2 %copy-start.6 = (bf16[4,128,768]{2,1,0:T(8,128)(2,1)S(1)}, bf16[4,128,768]{2,1,0:T(8,128)(2,1)}, u32[]{:S(2)}) copy-start(bf16[4,128,768]{2,1,0:T(8,128)(2,1)} %param.10) | copy-start | bytes 2359300
  24.6 22.9 %all-to-all-start = ((bf16[4,2,3,2,128,128]{5,4,3,2,1,0:T(8,128)(2,1)}), bf16[4,2,3,2,128,128]{5,4,3,2,1,0:T(8,128)(2,1)S(1)}, u32[]{:S(2)}, u32[]{:S(2)}) async-start(bf16[4,2,3,2,128,128]{5,4,3,2,1,0:T(8,128)(2,1)} %query_value_proj.1), calls=%async_computation | async-start | bytes 3145728 | tf_op jit(solution)/shard_map/all_to_all | solution.py:44
  28.5 78.7 %all-gather.7.cloned.1.call-start = ((), (), s32[]{:S(2)}) async-start(), calls=%async_computation.6 | async-start | bytes 7077888 | tf_op jit(solution)/shard_map/all_gather | solution.py:48
  28.5 7.6 %collective-permute-start.3 = (bf16[3,2,128,128]{3,2,1,0:T(8,128)(2,1)S(1)}, bf16[3,2,128,128]{3,2,1,0:T(8,128)(2,1)S(1)}, u32[]{:S(2)}, u32[]{:S(2)}) collective-permute-start(bf16[3,2,128,128]{3,2,1,0:T(8,128)(2,1)S(1)} %get-tuple-element.26.refs_0_), channel_id=1, source_target_pairs={{0,2},{2,4},{4,6},{6,0},{8,10},{10,12},{12,14},{14,8},{16,18},{18,... | collective-permute-start | bytes 589832 | tf_op jit(solution)/shard_map/ppermute | solution.py:52
  30.3 5.8 %collective-permute-start.4 = (bf16[3,2,128,128]{3,2,1,0:T(8,128)(2,1)S(1)}, bf16[3,2,128,128]{3,2,1,0:T(8,128)(2,1)S(1)}, u32[]{:S(2)}, u32[]{:S(2)}) collective-permute-start(bf16[3,2,128,128]{3,2,1,0:T(8,128)(2,1)S(1)} %get-tuple-element.26.refs_0_), channel_id=1, source_target_pairs={{0,6},{2,0},{4,2},{6,4},{8,14},{10,8},{12,10},{14,12},{16,22},{18,... | collective-permute-start | bytes 589832 | tf_op jit(solution)/shard_map/ppermute | solution.py:52
  32.5 8.7 %collective-permute-start.5 = (bf16[3,2,128,128]{3,2,1,0:T(8,128)(2,1)S(1)}, bf16[3,2,128,128]{3,2,1,0:T(8,128)(2,1)S(1)}, u32[]{:S(2)}, u32[]{:S(2)}) collective-permute-start(bf16[3,2,128,128]{3,2,1,0:T(8,128)(2,1)S(1)} %get-tuple-element.26.refs_0_), channel_id=1, source_target_pairs={{0,4},{2,6},{4,0},{6,2},{8,12},{10,14},{12,8},{14,10},{16,20},{18,... | collective-permute-start | bytes 589832 | tf_op jit(solution)/shard_map/ppermute | solution.py:52
  48.6 20.3 %all-to-all-start.1 = ((bf16[16,32,768]{2,1,0:T(8,128)(2,1)}), bf16[16,32,768]{2,1,0:T(8,128)(2,1)S(1)}, u32[]{:S(2)}, u32[]{:S(2)}) async-start(bf16[16,32,768]{2,1,0:T(8,128)(2,1)} %bitcast.10), calls=%async_computation.1 | async-start | bytes 1572864 | tf_op jit(solution)/shard_map/all_to_all | solution.py:409
  56.0 3.1 %collective-permute-start.6 = (bf16[4,3,2,64,128]{4,3,2,1,0:T(8,128)(2,1)S(1)}, bf16[4,3,2,64,128]{4,3,2,1,0:T(8,128)(2,1)S(1)}, u32[]{:S(2)}, u32[]{:S(2)}) collective-permute-start(bf16[4,3,2,64,128]{4,3,2,1,0:T(8,128)(2,1)S(1)} %get-tuple-element.37), channel_id=1, source_target_pairs={{0,8},{2,10},{4,12},{6,14},{8,0},{10,2},{12,4},{14,6},{16,24},{18,... | collective-permute-start | bytes 1179656 | tf_op jit(solution)/shard_map/ppermute | solution.py:52
  56.2 2.1 %collective-permute-start.7 = (bf16[3,2,128,128]{3,2,1,0:T(8,128)(2,1)S(1)}, bf16[3,2,128,128]{3,2,1,0:T(8,128)(2,1)S(1)}, u32[]{:S(2)}, u32[]{:S(2)}) collective-permute-start(bf16[3,2,128,128]{3,2,1,0:T(8,128)(2,1)S(1)} %get-tuple-element.26.refs_0_), channel_id=1, source_target_pairs={{0,8},{2,10},{4,12},{6,14},{8,0},{10,2},{12,4},{14,6},{16,24},{18,... | collective-permute-start | bytes 589832 | tf_op jit(solution)/shard_map/ppermute | solution.py:52
  56.6 2.0 %collective-permute-start.8 = (bf16[3,2,128,128]{3,2,1,0:T(8,128)(2,1)S(1)}, bf16[3,2,128,128]{3,2,1,0:T(8,128)(2,1)S(1)}, u32[]{:S(2)}, u32[]{:S(2)}) collective-permute-start(bf16[3,2,128,128]{3,2,1,0:T(8,128)(2,1)S(1)} %collective-permute-done.3.refs_1_), channel_id=1, source_target_pairs={{0,8},{2,10},{4,12},{6,14},{8,0},{10,2},{12,4},{14,6},{16,24},{18,... | collective-permute-start | bytes 589832 | tf_op jit(solution)/shard_map/ppermute | solution.py:52
  56.7 2.1 %collective-permute-start.9 = (bf16[3,2,128,128]{3,2,1,0:T(8,128)(2,1)S(1)}, bf16[3,2,128,128]{3,2,1,0:T(8,128)(2,1)S(1)}, u32[]{:S(2)}, u32[]{:S(2)}) collective-permute-start(bf16[3,2,128,128]{3,2,1,0:T(8,128)(2,1)S(1)} %collective-permute-done.4.refs_2_), channel_id=1, source_target_pairs={{0,8},{2,10},{4,12},{6,14},{8,0},{10,2},{12,4},{14,6},{16,24},{18,... | collective-permute-start | bytes 589832 | tf_op jit(solution)/shard_map/ppermute | solution.py:52
  57.1 2.0 %collective-permute-start.10 = (bf16[3,2,128,128]{3,2,1,0:T(8,128)(2,1)S(1)}, bf16[3,2,128,128]{3,2,1,0:T(8,128)(2,1)S(1)}, u32[]{:S(2)}, u32[]{:S(2)}) collective-permute-start(bf16[3,2,128,128]{3,2,1,0:T(8,128)(2,1)S(1)} %collective-permute-done.5.refs_3_), channel_id=1, source_target_pairs={{0,8},{2,10},{4,12},{6,14},{8,0},{10,2},{12,4},{14,6},{16,24},{18,... | collective-permute-start | bytes 589832 | tf_op jit(solution)/shard_map/ppermute | solution.py:52
  96.2 11.0 %collective-permute-start.11 = (bf16[3,32,1024]{2,1,0:T(8,128)(2,1)S(1)}, bf16[3,32,1024]{2,1,0:T(8,128)(2,1)S(1)}, u32[]{:S(2)}, u32[]{:S(2)}) collective-permute-start(bf16[3,32,1024]{2,1,0:T(8,128)(2,1)S(1)} %row_softmax.1.w0_ref), channel_id=1, source_target_pairs={{0,48},{2,50},{4,52},{6,54},{8,56},{10,58},{12,60},{14,62},{16,0},... | collective-permute-start | bytes 589832 | tf_op jit(solution)/shard_map/ppermute | solution.py:52
  97.2 10.1 %collective-permute-start.12 = (bf16[3,32,1024]{2,1,0:T(8,128)(2,1)S(1)}, bf16[3,32,1024]{2,1,0:T(8,128)(2,1)S(1)}, u32[]{:S(2)}, u32[]{:S(2)}) collective-permute-start(bf16[3,32,1024]{2,1,0:T(8,128)(2,1)S(1)} %row_softmax.1.w0_ref), channel_id=1, source_target_pairs={{0,32},{2,34},{4,36},{6,38},{8,40},{10,42},{12,44},{14,46},{16,48}... | collective-permute-start | bytes 589832 | tf_op jit(solution)/shard_map/ppermute | solution.py:52
  98.7 9.9 %collective-permute-start.13 = (bf16[3,32,1024]{2,1,0:T(8,128)(2,1)S(1)}, bf16[3,32,1024]{2,1,0:T(8,128)(2,1)S(1)}, u32[]{:S(2)}, u32[]{:S(2)}) collective-permute-start(bf16[3,32,1024]{2,1,0:T(8,128)(2,1)S(1)} %row_softmax.1.w0_ref), channel_id=1, source_target_pairs={{0,16},{2,18},{4,20},{6,22},{8,24},{10,26},{12,28},{14,30},{16,32}... | collective-permute-start | bytes 589832 | tf_op jit(solution)/shard_map/ppermute | solution.py:52
  108.6 22.6 %copy-start.2 = (bf16[768,768]{1,0:T(8,128)(2,1)S(1)}, bf16[768,768]{1,0:T(8,128)(2,1)}, u32[]{:S(2)}) copy-start(bf16[768,768]{1,0:T(8,128)(2,1)} %exit_col.1) | copy-start | bytes 3538948
  112.7 18.4 %copy-start.1 = (bf16[768,768]{1,0:T(8,128)(2,1)S(1)}, bf16[768,768]{1,0:T(8,128)(2,1)}, u32[]{:S(2)}) copy-start(bf16[768,768]{1,0:T(8,128)(2,1)} %exit_row.1) | copy-start | bytes 3538948
  112.7 18.4 %copy-start.4 = (f32[768]{0:T(1024)S(1)}, f32[768]{0:T(1024)}, u32[]{:S(2)}) copy-start(f32[768]{0:T(1024)} %gain_col_ref.1) | copy-start | bytes 9220
  112.7 18.4 %copy-start.5 = (f32[768]{0:T(1024)S(1)}, f32[768]{0:T(1024)}, u32[]{:S(2)}) copy-start(f32[768]{0:T(1024)} %gain_ffn_ref.1) | copy-start | bytes 9220
Sparse Core Ops, SparseCore 0:
  24.7 39.3 all-gather.4
  65.8 41.3 all-gather.6

commit v8 on v7

--- a/solution.py
+++ b/solution.py
@@ -270,13 +270,12 @@
 
 
 def column_kernel(
-    mix_ref, x_ref, gain_col_ref, gain_ffn_ref, exit_row, exit_col, attend_hbm, expand_hbm, shrink_hbm,
-    out_ref, qkv, stream, scratch, attend, expand, shrink, sems,
+    mix_ref, x_ref, gain_col_ref, gain_ffn_ref, exit_row, exit_col, attend, expand_hbm, shrink_hbm,
+    out_ref, qkv, stream, scratch, expand, shrink, sems,
 ):
     copies = [
-        pltpu.make_async_copy(attend_hbm, attend, sems.at[0]),
-        pltpu.make_async_copy(expand_hbm, expand, sems.at[1]),
-        pltpu.make_async_copy(shrink_hbm, shrink, sems.at[2]),
+        pltpu.make_async_copy(expand_hbm, expand, sems.at[0]),
+        pltpu.make_async_copy(shrink_hbm, shrink, sems.at[1]),
     ]
     for copy in copies:
         copy.start()
@@ -307,7 +306,6 @@
         ],
         axis=1,
     )
-    copies[0].wait()
     qkv[...] = mm(normed, attend[...]).astype(BF)
     group = lax.broadcasted_iota(jnp.int32, (256, 256), 0) // E == lax.broadcasted_iota(jnp.int32, (256, 256), 1) // E
     group = group.astype(F32).astype(BF)
@@ -345,13 +343,13 @@
     stream[...] += mm(mixed, exit_col[...])
 
     normed = normalize(stream[...], gain_ffn_ref[...][None, :])
-    copies[1].wait()
-    copies[2].wait()
-    for f in range(6):
-        cols = slice(f * 512, (f + 1) * 512)
-        pre = mm(normed, expand[:, cols])
+    for copy in copies:
+        copy.wait()
+    for r in range(4):
+        rows = slice(r * 128, (r + 1) * 128)
+        pre = mm(normed[rows, :], expand[...])
         hidden = (0.5 * pre * (1.0 + lax.erf(pre * math.sqrt(0.5)))).astype(BF)
-        stream[...] += mm(hidden, shrink[cols, :])
+        stream[rows, :] += mm(hidden, shrink[...])
     done = stream[...].astype(BF)
     for i, (y, c, xl) in enumerate((y, c, xl) for y in range(4) for c in range(2) for xl in range(2)):
         out_ref[(xl * 4 + y) * 2 + c] = done[i * 32 : (i + 1) * 32, :]
@@ -361,19 +359,18 @@
     vmem = pl.BlockSpec(memory_space=pltpu.VMEM)
     return pl.pallas_call(
         column_kernel,
-        in_specs=[vmem] * 6 + [pl.BlockSpec(memory_space=pltpu.HBM)] * 3,
+        in_specs=[vmem] * 7 + [pl.BlockSpec(memory_space=pltpu.HBM)] * 2,
         out_specs=vmem,
         out_shape=jax.ShapeDtypeStruct((16, 32, 768), BF),
         scratch_shapes=[
             pltpu.VMEM((512, 2304), BF),
             pltpu.VMEM((512, 768), F32),
             pltpu.VMEM((6, 512, 128), F32),
-            pltpu.VMEM(attend.shape, BF),
             pltpu.VMEM(expand.shape, BF),
             pltpu.VMEM(shrink.shape, BF),
-            pltpu.SemaphoreType.DMA((3,)),
+            pltpu.SemaphoreType.DMA((2,)),
         ],
-        compiler_params=params(48),
+        compiler_params=params(44),
         name="column_part",
     )(mix, x, gain_col, gain_ffn, exit_row, exit_col, attend, expand, shrink)
 

time: 173 us -> 171 us (0.988)
  Pallas kernels: 32.1 us -> 29.9 us
    pallas_call x1, Pallas kernels: 16.7 us -> 14.3 us  [column_part(): pl.pallas_call(column_kernel, in_specs=[vmem] * 7 + [pl.BlockSpec(memory_...]
where the time goes in v8:
time: 171 us
  blocking collectives  57.8 us (34%)
  waiting for transfers between devices  38.9 us (23%)
  Pallas kernels  29.9 us (17%)
  starting transfers between devices  25.9 us (15%)
  between operations  13.5 us (8%)
  local copies, waits for them, and re-layouts  3.7 us (2%)
    all_to_all x2, blocking collectives, swap(): lax.all_to_all(array, AXES, split_axis=0, concat_axis=0, tiled=True, axis...  40.7 us
    all_to_all x1, blocking collectives, local(): out = lax.all_to_all(out, 'seq', split_axis=0, concat_axis=0, tiled=True)  17.1 us
    ppermute x14, starting transfers between devices, send(): return lax.ppermute(array, AXES, shifts(**by))  14.6 us
    pallas_call x1, Pallas kernels, column_part(): pl.pallas_call(column_kernel, in_specs=[vmem] * 7 + [pl.BlockSpec(memory_...  14.3 us
    ppermute x14, waiting for transfers between devices, send(): return lax.ppermute(array, AXES, shifts(**by))  14.2 us
    all_to_all x1, waiting for transfers between devices, local(): x = lax.all_to_all(x, 'seq', split_axis=0, concat_axis=0, tiled=True)  9.79 us
    all_gather x2, waiting for transfers between devices, gather(): lax.all_gather(array, AXES, axis=0, tiled=False, axis_index_groups=groups)  8.53 us
    all_to_all x1, starting transfers between devices, local(): x = lax.all_to_all(x, 'seq', split_axis=0, concat_axis=0, tiled=True)  7.3 us
  transfers between devices with their start and end apart: 18, of which 11 were waited for; matrix products, arithmetic and copies ran while one was open for 1% of the time, Pallas kernels for 5%

profile of v8, /device:TPU:1, one launch (start us, length us, event | category | flops | bytes accessed | tf_op | source)
XLA Modules:
  0.0 170.7 jit_solution(12597214464795994487)
XLA Ops:
  6.6 0.7 copy-done.4
  7.3 3.3 %key_proj.1 = (bf16[512,768]{1,0:T(8,128)(2,1)S(1)}, bf16[3,2,128,128]{3,2,1,0:T(8,128)(2,1)S(1)}, bf16[3,2,128,128]{3,2,1,0:T(8,128)(2,1)S(1)}, bf16[3,2,128,12...) custom-call(s32[4]{0:T(128)S(1)} %pad_add_fusion.place_ref, bf16[512,768]{1,0:T(8,128)(2,1)} %bitcast.29, ...), custom_call_target="tpu_custom_call" | custom-call | tf_op jit(solution)/shard_map/key_proj/pallas_call | solution.py:106
  10.6 2.1 %collective-permute-start.2 = (bf16[3,2,128,128]{3,2,1,0:T(8,128)(2,1)S(1)}, bf16[3,2,128,128]{3,2,1,0:T(8,128)(2,1)S(1)}, u32[]{:S(2)}, u32[]{:S(2)}) collective-permute-start(bf16[3,2,128,128]{3,2,1,0:T(8,128)(2,1)S(1)} %get-tuple-element.22), channel_id=1, source_target_pairs={{0,64},{2,66},{4,68},{6,70},{8,72},{10,74},{12,76},{14,78},{16,80}... | collective-permute-start | bytes 589832 | tf_op jit(solution)/shard_map/ppermute | solution.py:52
  12.7 2.5 %collective-permute-start.1 = (bf16[3,2,128,128]{3,2,1,0:T(8,128)(2,1)S(1)}, bf16[3,2,128,128]{3,2,1,0:T(8,128)(2,1)S(1)}, u32[]{:S(2)}, u32[]{:S(2)}) collective-permute-start(bf16[3,2,128,128]{3,2,1,0:T(8,128)(2,1)S(1)} %get-tuple-element.21), channel_id=1, source_target_pairs={{0,1},{2,3},{4,5},{6,7},{8,9},{10,11},{12,13},{14,15},{16,17},{18,... | collective-permute-start | bytes 589832 | tf_op jit(solution)/shard_map/ppermute | solution.py:52
  15.2 1.2 collective-permute-start
  16.3 2.9 %query_value_proj.1 = bf16[4,2,3,2,128,128]{5,4,3,2,1,0:T(8,128)(2,1)} custom-call(bf16[512,768]{1,0:T(8,128)(2,1)S(1)} %get-tuple-element.24.normed_ref, bf16[768,2304]{1,0:T(8,128)(2,1)S(1)} %copy-done), custom_call_target="tpu_custom_call" | custom-call | tf_op jit(solution)/shard_map/query_value_proj/pallas_call | solution.py:130
  19.2 4.4 %collective-permute-done.1 = bf16[3,2,128,128]{3,2,1,0:T(8,128)(2,1)S(1)} collective-permute-done((bf16[3,2,128,128]{3,2,1,0:T(8,128)(2,1)S(1)}, bf16[3,2,128,128]{3,2,1,0:T(8,128)(2,1)S(1)}, u32[]{:S(2)}, u32[]{:S(2)}) %collective-permute-start.1) | collective-permute-done | bytes 196640 | tf_op jit(solution)/shard_map/ppermute | solution.py:52
  23.7 0.9 pad_maximum_fusion
  24.6 3.9 %all-to-all-start = ((bf16[4,2,3,2,128,128]{5,4,3,2,1,0:T(8,128)(2,1)}), bf16[4,2,3,2,128,128]{5,4,3,2,1,0:T(8,128)(2,1)S(1)}, u32[]{:S(2)}, u32[]{:S(2)}) async-start(bf16[4,2,3,2,128,128]{5,4,3,2,1,0:T(8,128)(2,1)} %query_value_proj.1), calls=%async_computation | async-start | bytes 3145728 | tf_op jit(solution)/shard_map/all_to_all | solution.py:44
  28.6 1.8 %collective-permute-start.3 = (bf16[3,2,128,128]{3,2,1,0:T(8,128)(2,1)S(1)}, bf16[3,2,128,128]{3,2,1,0:T(8,128)(2,1)S(1)}, u32[]{:S(2)}, u32[]{:S(2)}) collective-permute-start(bf16[3,2,128,128]{3,2,1,0:T(8,128)(2,1)S(1)} %get-tuple-element.26.refs_0_), channel_id=1, source_target_pairs={{0,2},{2,4},{4,6},{6,0},{8,10},{10,12},{12,14},{14,8},{16,18},{18,... | collective-permute-start | bytes 589832 | tf_op jit(solution)/shard_map/ppermute | solution.py:52
  30.4 2.2 %collective-permute-start.4 = (bf16[3,2,128,128]{3,2,1,0:T(8,128)(2,1)S(1)}, bf16[3,2,128,128]{3,2,1,0:T(8,128)(2,1)S(1)}, u32[]{:S(2)}, u32[]{:S(2)}) collective-permute-start(bf16[3,2,128,128]{3,2,1,0:T(8,128)(2,1)S(1)} %get-tuple-element.26.refs_0_), channel_id=1, source_target_pairs={{0,6},{2,0},{4,2},{6,4},{8,14},{10,8},{12,10},{14,12},{16,22},{18,... | collective-permute-start | bytes 589832 | tf_op jit(solution)/shard_map/ppermute | solution.py:52
  32.6 1.2 collective-permute-start.5
  33.8 1.0 copy.13
  34.8 1.4 collective-permute-done.3.refs_1_
  36.2 5.1 %collective-permute-done.5.refs_3_ = bf16[3,2,128,128]{3,2,1,0:T(8,128)(2,1)S(1)} collective-permute-done((bf16[3,2,128,128]{3,2,1,0:T(8,128)(2,1)S(1)}, bf16[3,2,128,128]{3,2,1,0:T(8,128)(2,1)S(1)}, u32[]{:S(2)}, u32[]{:S(2)}) %collective-permute-start.5) | collective-permute-done | bytes 196640 | tf_op jit(solution)/shard_map/ppermute | solution.py:52
  41.3 6.3 %all-to-all-done = bf16[4,2,3,2,128,128]{5,4,3,2,1,0:T(8,128)(2,1)S(1)} async-done(((bf16[4,2,3,2,128,128]{5,4,3,2,1,0:T(8,128)(2,1)}), bf16[4,2,3,2,128,128]{5,4,3,2,1,0:T(8,128)(2,1)S(1)}, u32[]{:S(2)}, u32[]{:S(2)}) %all-to-all-start) | async-done | bytes 1572896 | tf_op jit(solution)/shard_map/all_to_all | solution.py:44
  47.6 1.0 slice_bitcast_fusion
  48.6 7.3 %all-to-all-start.1 = ((bf16[16,32,768]{2,1,0:T(8,128)(2,1)}), bf16[16,32,768]{2,1,0:T(8,128)(2,1)S(1)}, u32[]{:S(2)}, u32[]{:S(2)}) async-start(bf16[16,32,768]{2,1,0:T(8,128)(2,1)} %bitcast.10), calls=%async_computation.1 | async-start | bytes 1572864 | tf_op jit(solution)/shard_map/all_to_all | solution.py:406
  56.7 0.4 collective-permute-start.9
  57.2 1.1 collective-permute-done.7.refs_4_
  59.1 9.8 %all-to-all-done.1.x_ref = bf16[16,32,768]{2,1,0:T(8,128)(2,1)S(1)} async-done(((bf16[16,32,768]{2,1,0:T(8,128)(2,1)}), bf16[16,32,768]{2,1,0:T(8,128)(2,1)S(1)}, u32[]{:S(2)}, u32[]{:S(2)}) %all-to-all-start.1) | async-done | bytes 786464 | tf_op jit(solution)/shard_map/all_to_all | solution.py:406
  68.9 4.8 %partial_scores.1 = f32[4,3,32,1024]{3,2,1,0:T(8,128)S(1)} custom-call(s32[4]{0:T(128)S(1)} %pad_add_fusion.place_ref, bf16[4,3,2,64,128]{4,3,2,1,0:T(8,128)(2,1)S(1)} %get-tuple-element.38.q0_ref, bf16[4,3,2,64,128]{4,3,2,1,0:T(8,128)(2,1)S(1)} %collective-permute-done.6.q1_ref, bf16[3,2,128,128]{3,2,1,0:T(8,128)(2,1)S(1)} %get-tuple-element.26.refs_0_, ...), custom_call_target="tpu_custom_call" | custom-call | tf_op jit(solution)/shard_map/partial_scores/pallas_call | solution.py:198
  73.7 22.3 %all_to_all.25.refs_0_ = f32[4,3,32,1024]{3,2,1,0:T(8,128)S(1)} all-to-all(f32[4,3,32,1024]{3,2,1,0:T(8,128)S(1)} %partial_scores.1), channel_id=1, replica_groups={{0,16,32,48},{1,17,33,49},{2,18,34,50},{3,19,35,51},{4,20,36,52},{5,21,..., dimensions={0} | all-to-all | bytes 3145728 | tf_op jit(solution)/shard_map/all_to_all | solution.py:44
  96.2 1.0 collective-permute-start.11
  97.2 1.5 collective-permute-start.12
  98.7 8.5 %all-gather.7.cloned.1.call-done = bf16[32,3,2,128,128]{4,3,2,1,0:T(8,128)(2,1)} async-done(((bf16[4,3,2,128,128]{4,3,2,1,0:T(8,128)(2,1)}), bf16[32,3,2,128,128]{4,3,2,1,0:T(8,128)(2,1)}) %all-gather.7.cloned.1.call-update) | async-done | bytes 6291472 | tf_op jit(solution)/shard_map/all_gather | solution.py:48
  107.2 1.3 collective-permute-done.13.w3_ref
  108.6 4.4 %row_mix.1 = bf16[16,3,2,32,128]{4,3,2,1,0:T(8,128)(2,1)S(1)} custom-call(s32[4]{0:T(128)S(1)} %pad_add_fusion.place_ref, bf16[3,32,1024]{2,1,0:T(8,128)(2,1)S(1)} %row_softmax.1.w0_ref, bf16[3,32,1024]{2,1,0:T(8,128)(2,1)S(1)} %collective-permute-done.11.w1_ref, bf16[3,32,1024]{2,1,0:T(8,128)(2,1)S(1)} %collective-permute-done.12.w2_ref, ...), custom_call_target="tpu_custom_call" | custom-call | tf_op jit(solution)/shard_map/row_mix/pallas_call | solution.py:257
  113.0 18.4 %all_to_all.26 = bf16[16,3,2,32,128]{4,3,2,1,0:T(8,128)(2,1)S(1)} all-to-all(bf16[16,3,2,32,128]{4,3,2,1,0:T(8,128)(2,1)S(1)} %row_mix.1), channel_id=1, replica_groups={{0,16,32,48,64,80,96,112,1,17,33,49,65,81,97,113},{2,18,34,50,66,82,98,..., dimensions={0} | all-to-all | bytes 1572864 | tf_op jit(solution)/shard_map/all_to_all | solution.py:44
  131.5 14.3 %column_part.1 = bf16[16,32,768]{2,1,0:T(8,128)(2,1)S(1)} custom-call(bf16[16,3,64,128]{3,2,1,0:T(8,128)(2,1)S(1)} %bitcast.25, bf16[16,32,768]{2,1,0:T(8,128)(2,1)S(1)} %all-to-all-done.1.x_ref, f32[768]{0:T(1024)S(1)} %copy-done.5, f32[768]{0:T(1024)S(1)} %copy-done.6, bf16[768,768]{1,0:T(8,128)(2,1)S(1)} %copy-done.2, bf16[768,768]{1,0:T(8,128)(2,1)S(1)} %copy-done.3, ...), custom_call_target="tpu_custom_call" | custom-call | tf_op jit(solution)/shard_map/column_part/pallas_call | solution.py:360
  145.8 17.1 %all_to_all.27 = bf16[16,32,768]{2,1,0:T(8,128)(2,1)S(1)} all-to-all(bf16[16,32,768]{2,1,0:T(8,128)(2,1)S(1)} %column_part.1), channel_id=1, replica_groups=mesh['seq'=16,'col'=8] {'seq'}, dimensions={0} | all-to-all | bytes 1572864 | tf_op jit(solution)/shard_map/all_to_all | solution.py:423
  162.9 0.9 copy.14
  (37 shorter events, 2.1 us)
Async XLA Ops:
  6.5 62.4 %all-gather.5.cloned.1.call-start = ((), (), s32[]{:S(2)}) async-start(), calls=%async_computation.5 | async-start | bytes 5308416 | tf_op jit(solution)/shard_map/all_gather | solution.py:48
  6.6 0.7 copy-start.4
  7.3 9.0 %copy-start = (bf16[768,2304]{1,0:T(8,128)(2,1)S(1)}, bf16[768,2304]{1,0:T(8,128)(2,1)}, u32[]{:S(2)}) copy-start(bf16[768,2304]{1,0:T(8,128)(2,1)} %w_ref.3) | copy-start | bytes 10616836
  10.6 8.6 %collective-permute-start.2 = (bf16[3,2,128,128]{3,2,1,0:T(8,128)(2,1)S(1)}, bf16[3,2,128,128]{3,2,1,0:T(8,128)(2,1)S(1)}, u32[]{:S(2)}, u32[]{:S(2)}) collective-permute-start(bf16[3,2,128,128]{3,2,1,0:T(8,128)(2,1)S(1)} %get-tuple-element.22), channel_id=1, source_target_pairs={{0,64},{2,66},{4,68},{6,70},{8,72},{10,74},{12,76},{14,78},{16,80}... | collective-permute-start | bytes 589832 | tf_op jit(solution)/shard_map/ppermute | solution.py:52
  12.7 11.0 %collective-permute-start.1 = (bf16[3,2,128,128]{3,2,1,0:T(8,128)(2,1)S(1)}, bf16[3,2,128,128]{3,2,1,0:T(8,128)(2,1)S(1)}, u32[]{:S(2)}, u32[]{:S(2)}) collective-permute-start(bf16[3,2,128,128]{3,2,1,0:T(8,128)(2,1)S(1)} %get-tuple-element.21), channel_id=1, source_target_pairs={{0,1},{2,3},{4,5},{6,7},{8,9},{10,11},{12,13},{14,15},{16,17},{18,... | collective-permute-start | bytes 589832 | tf_op jit(solution)/shard_map/ppermute | solution.py:52
  15.2 8.5 %collective-permute-start = (bf16[3,2,128,128]{3,2,1,0:T(8,128)(2,1)S(1)}, bf16[3,2,128,128]{3,2,1,0:T(8,128)(2,1)S(1)}, u32[]{:S(2)}, u32[]{:S(2)}) collective-permute-start(bf16[3,2,128,128]{3,2,1,0:T(8,128)(2,1)S(1)} %get-tuple-element.20), channel_id=1, source_target_pairs={{0,65},{2,67},{4,69},{6,71},{8,73},{10,75},{12,77},{14,79},{16,81}... | collective-permute-start | bytes 589832 | tf_op jit(solution)/shard_map/ppermute | solution.py:52
  24.6 9.2 %copy-start.7 = (bf16[4,128,768]{2,1,0:T(8,128)(2,1)S(1)}, bf16[4,128,768]{2,1,0:T(8,128)(2,1)}, u32[]{:S(2)}) copy-start(bf16[4,128,768]{2,1,0:T(8,128)(2,1)} %param.10) | copy-start | bytes 2359300
  24.6 22.9 %all-to-all-start = ((bf16[4,2,3,2,128,128]{5,4,3,2,1,0:T(8,128)(2,1)}), bf16[4,2,3,2,128,128]{5,4,3,2,1,0:T(8,128)(2,1)S(1)}, u32[]{:S(2)}, u32[]{:S(2)}) async-start(bf16[4,2,3,2,128,128]{5,4,3,2,1,0:T(8,128)(2,1)} %query_value_proj.1), calls=%async_computation | async-start | bytes 3145728 | tf_op jit(solution)/shard_map/all_to_all | solution.py:44
  28.6 78.7 %all-gather.7.cloned.1.call-start = ((), (), s32[]{:S(2)}) async-start(), calls=%async_computation.6 | async-start | bytes 7077888 | tf_op jit(solution)/shard_map/all_gather | solution.py:48
  28.6 7.6 %collective-permute-start.3 = (bf16[3,2,128,128]{3,2,1,0:T(8,128)(2,1)S(1)}, bf16[3,2,128,128]{3,2,1,0:T(8,128)(2,1)S(1)}, u32[]{:S(2)}, u32[]{:S(2)}) collective-permute-start(bf16[3,2,128,128]{3,2,1,0:T(8,128)(2,1)S(1)} %get-tuple-element.26.refs_0_), channel_id=1, source_target_pairs={{0,2},{2,4},{4,6},{6,0},{8,10},{10,12},{12,14},{14,8},{16,18},{18,... | collective-permute-start | bytes 589832 | tf_op jit(solution)/shard_map/ppermute | solution.py:52
  30.4 5.8 %collective-permute-start.4 = (bf16[3,2,128,128]{3,2,1,0:T(8,128)(2,1)S(1)}, bf16[3,2,128,128]{3,2,1,0:T(8,128)(2,1)S(1)}, u32[]{:S(2)}, u32[]{:S(2)}) collective-permute-start(bf16[3,2,128,128]{3,2,1,0:T(8,128)(2,1)S(1)} %get-tuple-element.26.refs_0_), channel_id=1, source_target_pairs={{0,6},{2,0},{4,2},{6,4},{8,14},{10,8},{12,10},{14,12},{16,22},{18,... | collective-permute-start | bytes 589832 | tf_op jit(solution)/shard_map/ppermute | solution.py:52
  32.6 8.7 %collective-permute-start.5 = (bf16[3,2,128,128]{3,2,1,0:T(8,128)(2,1)S(1)}, bf16[3,2,128,128]{3,2,1,0:T(8,128)(2,1)S(1)}, u32[]{:S(2)}, u32[]{:S(2)}) collective-permute-start(bf16[3,2,128,128]{3,2,1,0:T(8,128)(2,1)S(1)} %get-tuple-element.26.refs_0_), channel_id=1, source_target_pairs={{0,4},{2,6},{4,0},{6,2},{8,12},{10,14},{12,8},{14,10},{16,20},{18,... | collective-permute-start | bytes 589832 | tf_op jit(solution)/shard_map/ppermute | solution.py:52
  48.6 20.3 %all-to-all-start.1 = ((bf16[16,32,768]{2,1,0:T(8,128)(2,1)}), bf16[16,32,768]{2,1,0:T(8,128)(2,1)S(1)}, u32[]{:S(2)}, u32[]{:S(2)}) async-start(bf16[16,32,768]{2,1,0:T(8,128)(2,1)} %bitcast.10), calls=%async_computation.1 | async-start | bytes 1572864 | tf_op jit(solution)/shard_map/all_to_all | solution.py:406
  56.0 3.1 %collective-permute-start.6 = (bf16[4,3,2,64,128]{4,3,2,1,0:T(8,128)(2,1)S(1)}, bf16[4,3,2,64,128]{4,3,2,1,0:T(8,128)(2,1)S(1)}, u32[]{:S(2)}, u32[]{:S(2)}) collective-permute-start(bf16[4,3,2,64,128]{4,3,2,1,0:T(8,128)(2,1)S(1)} %get-tuple-element.37), channel_id=1, source_target_pairs={{0,8},{2,10},{4,12},{6,14},{8,0},{10,2},{12,4},{14,6},{16,24},{18,... | collective-permute-start | bytes 1179656 | tf_op jit(solution)/shard_map/ppermute | solution.py:52
  56.2 2.1 %collective-permute-start.7 = (bf16[3,2,128,128]{3,2,1,0:T(8,128)(2,1)S(1)}, bf16[3,2,128,128]{3,2,1,0:T(8,128)(2,1)S(1)}, u32[]{:S(2)}, u32[]{:S(2)}) collective-permute-start(bf16[3,2,128,128]{3,2,1,0:T(8,128)(2,1)S(1)} %get-tuple-element.26.refs_0_), channel_id=1, source_target_pairs={{0,8},{2,10},{4,12},{6,14},{8,0},{10,2},{12,4},{14,6},{16,24},{18,... | collective-permute-start | bytes 589832 | tf_op jit(solution)/shard_map/ppermute | solution.py:52
  56.6 2.0 %collective-permute-start.8 = (bf16[3,2,128,128]{3,2,1,0:T(8,128)(2,1)S(1)}, bf16[3,2,128,128]{3,2,1,0:T(8,128)(2,1)S(1)}, u32[]{:S(2)}, u32[]{:S(2)}) collective-permute-start(bf16[3,2,128,128]{3,2,1,0:T(8,128)(2,1)S(1)} %collective-permute-done.3.refs_1_), channel_id=1, source_target_pairs={{0,8},{2,10},{4,12},{6,14},{8,0},{10,2},{12,4},{14,6},{16,24},{18,... | collective-permute-start | bytes 589832 | tf_op jit(solution)/shard_map/ppermute | solution.py:52
  56.7 2.1 %collective-permute-start.9 = (bf16[3,2,128,128]{3,2,1,0:T(8,128)(2,1)S(1)}, bf16[3,2,128,128]{3,2,1,0:T(8,128)(2,1)S(1)}, u32[]{:S(2)}, u32[]{:S(2)}) collective-permute-start(bf16[3,2,128,128]{3,2,1,0:T(8,128)(2,1)S(1)} %collective-permute-done.4.refs_2_), channel_id=1, source_target_pairs={{0,8},{2,10},{4,12},{6,14},{8,0},{10,2},{12,4},{14,6},{16,24},{18,... | collective-permute-start | bytes 589832 | tf_op jit(solution)/shard_map/ppermute | solution.py:52
  57.1 2.0 %collective-permute-start.10 = (bf16[3,2,128,128]{3,2,1,0:T(8,128)(2,1)S(1)}, bf16[3,2,128,128]{3,2,1,0:T(8,128)(2,1)S(1)}, u32[]{:S(2)}, u32[]{:S(2)}) collective-permute-start(bf16[3,2,128,128]{3,2,1,0:T(8,128)(2,1)S(1)} %collective-permute-done.5.refs_3_), channel_id=1, source_target_pairs={{0,8},{2,10},{4,12},{6,14},{8,0},{10,2},{12,4},{14,6},{16,24},{18,... | collective-permute-start | bytes 589832 | tf_op jit(solution)/shard_map/ppermute | solution.py:52
  96.2 11.0 %collective-permute-start.11 = (bf16[3,32,1024]{2,1,0:T(8,128)(2,1)S(1)}, bf16[3,32,1024]{2,1,0:T(8,128)(2,1)S(1)}, u32[]{:S(2)}, u32[]{:S(2)}) collective-permute-start(bf16[3,32,1024]{2,1,0:T(8,128)(2,1)S(1)} %row_softmax.1.w0_ref), channel_id=1, source_target_pairs={{0,48},{2,50},{4,52},{6,54},{8,56},{10,58},{12,60},{14,62},{16,0},... | collective-permute-start | bytes 589832 | tf_op jit(solution)/shard_map/ppermute | solution.py:52
  97.2 10.1 %collective-permute-start.12 = (bf16[3,32,1024]{2,1,0:T(8,128)(2,1)S(1)}, bf16[3,32,1024]{2,1,0:T(8,128)(2,1)S(1)}, u32[]{:S(2)}, u32[]{:S(2)}) collective-permute-start(bf16[3,32,1024]{2,1,0:T(8,128)(2,1)S(1)} %row_softmax.1.w0_ref), channel_id=1, source_target_pairs={{0,32},{2,34},{4,36},{6,38},{8,40},{10,42},{12,44},{14,46},{16,48}... | collective-permute-start | bytes 589832 | tf_op jit(solution)/shard_map/ppermute | solution.py:52
  98.7 9.9 %collective-permute-start.13 = (bf16[3,32,1024]{2,1,0:T(8,128)(2,1)S(1)}, bf16[3,32,1024]{2,1,0:T(8,128)(2,1)S(1)}, u32[]{:S(2)}, u32[]{:S(2)}) collective-permute-start(bf16[3,32,1024]{2,1,0:T(8,128)(2,1)S(1)} %row_softmax.1.w0_ref), channel_id=1, source_target_pairs={{0,16},{2,18},{4,20},{6,22},{8,24},{10,26},{12,28},{14,30},{16,32}... | collective-permute-start | bytes 589832 | tf_op jit(solution)/shard_map/ppermute | solution.py:52
  108.6 22.9 %copy-start.1 = (bf16[768,2304]{1,0:T(8,128)(2,1)S(1)}, bf16[768,2304]{1,0:T(8,128)(2,1)}, u32[]{:S(2)}) copy-start(bf16[768,2304]{1,0:T(8,128)(2,1)} %attend.1) | copy-start | bytes 10616836
  108.6 22.9 %copy-start.3 = (bf16[768,768]{1,0:T(8,128)(2,1)S(1)}, bf16[768,768]{1,0:T(8,128)(2,1)}, u32[]{:S(2)}) copy-start(bf16[768,768]{1,0:T(8,128)(2,1)} %exit_col.1) | copy-start | bytes 3538948
  113.0 18.5 %copy-start.2 = (bf16[768,768]{1,0:T(8,128)(2,1)S(1)}, bf16[768,768]{1,0:T(8,128)(2,1)}, u32[]{:S(2)}) copy-start(bf16[768,768]{1,0:T(8,128)(2,1)} %exit_row.1) | copy-start | bytes 3538948
  113.0 18.5 %copy-start.5 = (f32[768]{0:T(1024)S(1)}, f32[768]{0:T(1024)}, u32[]{:S(2)}) copy-start(f32[768]{0:T(1024)} %gain_col_ref.1) | copy-start | bytes 9220
  113.0 18.5 %copy-start.6 = (f32[768]{0:T(1024)S(1)}, f32[768]{0:T(1024)}, u32[]{:S(2)}) copy-start(f32[768]{0:T(1024)} %gain_ffn_ref.1) | copy-start | bytes 9220
Sparse Core Ops, SparseCore 0:
  24.7 39.3 all-gather.4
  65.8 41.3 all-gather.6

commit v9 on v8

--- a/solution.py
+++ b/solution.py
@@ -343,16 +343,16 @@
     stream[...] += mm(mixed, exit_col[...])
 
     normed = normalize(stream[...], gain_ffn_ref[...][None, :])
-    for copy in copies:
-        copy.wait()
+    copies[0].wait()
     for r in range(4):
         rows = slice(r * 128, (r + 1) * 128)
         pre = mm(normed[rows, :], expand[...])
         hidden = (0.5 * pre * (1.0 + lax.erf(pre * math.sqrt(0.5)))).astype(BF)
-        stream[rows, :] += mm(hidden, shrink[...])
-    done = stream[...].astype(BF)
-    for i, (y, c, xl) in enumerate((y, c, xl) for y in range(4) for c in range(2) for xl in range(2)):
-        out_ref[(xl * 4 + y) * 2 + c] = done[i * 32 : (i + 1) * 32, :]
+        if r == 0:
+            copies[1].wait()
+        done = (stream[rows, :] + mm(hidden, shrink[...])).astype(BF)
+        for i, (c, xl) in enumerate((c, xl) for c in range(2) for xl in range(2)):
+            out_ref[(xl * 4 + r) * 2 + c] = done[i * 32 : (i + 1) * 32, :]
 
 
 def column_part(mix, x, gain_col, gain_ffn, exit_row, attend, exit_col, expand, shrink):

time: 171 us -> 171 us (level)
  no operation moved by 1% of the time
where the time goes in v9:
time: 171 us
  blocking collectives  57.8 us (34%)
  waiting for transfers between devices  38.9 us (23%)
  Pallas kernels  30.3 us (18%)
  starting transfers between devices  25.9 us (15%)
  between operations  13.5 us (8%)
  local copies, waits for them, and re-layouts  3.7 us (2%)
    all_to_all x2, blocking collectives, swap(): lax.all_to_all(array, AXES, split_axis=0, concat_axis=0, tiled=True, axis...  40.7 us
    all_to_all x1, blocking collectives, local(): out = lax.all_to_all(out, 'seq', split_axis=0, concat_axis=0, tiled=True)  17.1 us
    pallas_call x1, Pallas kernels, column_part(): pl.pallas_call(column_kernel, in_specs=[vmem] * 7 + [pl.BlockSpec(memory_...  14.7 us
    ppermute x14, starting transfers between devices, send(): return lax.ppermute(array, AXES, shifts(**by))  14.6 us
    ppermute x14, waiting for transfers between devices, send(): return lax.ppermute(array, AXES, shifts(**by))  14.2 us
    all_to_all x1, waiting for transfers between devices, local(): x = lax.all_to_all(x, 'seq', split_axis=0, concat_axis=0, tiled=True)  9.79 us
    all_gather x2, waiting for transfers between devices, gather(): lax.all_gather(array, AXES, axis=0, tiled=False, axis_index_groups=groups)  8.53 us
    all_to_all x1, starting transfers between devices, local(): x = lax.all_to_all(x, 'seq', split_axis=0, concat_axis=0, tiled=True)  7.3 us
  transfers between devices with their start and end apart: 18, of which 11 were waited for; matrix products, arithmetic and copies ran while one was open for 1% of the time, Pallas kernels for 5%

profile of v9, /device:TPU:1, one launch (start us, length us, event | category | flops | bytes accessed | tf_op | source)
XLA Modules:
  0.0 171.1 jit_solution(1421123814684079607)
XLA Ops:
  6.6 0.7 copy-done.4
  7.3 3.3 %key_proj.1 = (bf16[512,768]{1,0:T(8,128)(2,1)S(1)}, bf16[3,2,128,128]{3,2,1,0:T(8,128)(2,1)S(1)}, bf16[3,2,128,128]{3,2,1,0:T(8,128)(2,1)S(1)}, bf16[3,2,128,12...) custom-call(s32[4]{0:T(128)S(1)} %pad_add_fusion.place_ref, bf16[512,768]{1,0:T(8,128)(2,1)} %bitcast.29, ...), custom_call_target="tpu_custom_call" | custom-call | tf_op jit(solution)/shard_map/key_proj/pallas_call | solution.py:106
  10.6 2.1 %collective-permute-start.2 = (bf16[3,2,128,128]{3,2,1,0:T(8,128)(2,1)S(1)}, bf16[3,2,128,128]{3,2,1,0:T(8,128)(2,1)S(1)}, u32[]{:S(2)}, u32[]{:S(2)}) collective-permute-start(bf16[3,2,128,128]{3,2,1,0:T(8,128)(2,1)S(1)} %get-tuple-element.22), channel_id=1, source_target_pairs={{0,64},{2,66},{4,68},{6,70},{8,72},{10,74},{12,76},{14,78},{16,80}... | collective-permute-start | bytes 589832 | tf_op jit(solution)/shard_map/ppermute | solution.py:52
  12.7 2.5 %collective-permute-start.1 = (bf16[3,2,128,128]{3,2,1,0:T(8,128)(2,1)S(1)}, bf16[3,2,128,128]{3,2,1,0:T(8,128)(2,1)S(1)}, u32[]{:S(2)}, u32[]{:S(2)}) collective-permute-start(bf16[3,2,128,128]{3,2,1,0:T(8,128)(2,1)S(1)} %get-tuple-element.21), channel_id=1, source_target_pairs={{0,1},{2,3},{4,5},{6,7},{8,9},{10,11},{12,13},{14,15},{16,17},{18,... | collective-permute-start | bytes 589832 | tf_op jit(solution)/shard_map/ppermute | solution.py:52
  15.2 1.2 collective-permute-start
  16.3 2.9 %query_value_proj.1 = bf16[4,2,3,2,128,128]{5,4,3,2,1,0:T(8,128)(2,1)} custom-call(bf16[512,768]{1,0:T(8,128)(2,1)S(1)} %get-tuple-element.24.normed_ref, bf16[768,2304]{1,0:T(8,128)(2,1)S(1)} %copy-done), custom_call_target="tpu_custom_call" | custom-call | tf_op jit(solution)/shard_map/query_value_proj/pallas_call | solution.py:130
  19.2 4.4 %collective-permute-done.1 = bf16[3,2,128,128]{3,2,1,0:T(8,128)(2,1)S(1)} collective-permute-done((bf16[3,2,128,128]{3,2,1,0:T(8,128)(2,1)S(1)}, bf16[3,2,128,128]{3,2,1,0:T(8,128)(2,1)S(1)}, u32[]{:S(2)}, u32[]{:S(2)}) %collective-permute-start.1) | collective-permute-done | bytes 196640 | tf_op jit(solution)/shard_map/ppermute | solution.py:52
  23.7 0.9 pad_maximum_fusion
  24.6 3.9 %all-to-all-start = ((bf16[4,2,3,2,128,128]{5,4,3,2,1,0:T(8,128)(2,1)}), bf16[4,2,3,2,128,128]{5,4,3,2,1,0:T(8,128)(2,1)S(1)}, u32[]{:S(2)}, u32[]{:S(2)}) async-start(bf16[4,2,3,2,128,128]{5,4,3,2,1,0:T(8,128)(2,1)} %query_value_proj.1), calls=%async_computation | async-start | bytes 3145728 | tf_op jit(solution)/shard_map/all_to_all | solution.py:44
  28.6 1.8 %collective-permute-start.3 = (bf16[3,2,128,128]{3,2,1,0:T(8,128)(2,1)S(1)}, bf16[3,2,128,128]{3,2,1,0:T(8,128)(2,1)S(1)}, u32[]{:S(2)}, u32[]{:S(2)}) collective-permute-start(bf16[3,2,128,128]{3,2,1,0:T(8,128)(2,1)S(1)} %get-tuple-element.26.refs_0_), channel_id=1, source_target_pairs={{0,2},{2,4},{4,6},{6,0},{8,10},{10,12},{12,14},{14,8},{16,18},{18,... | collective-permute-start | bytes 589832 | tf_op jit(solution)/shard_map/ppermute | solution.py:52
  30.4 2.2 %collective-permute-start.4 = (bf16[3,2,128,128]{3,2,1,0:T(8,128)(2,1)S(1)}, bf16[3,2,128,128]{3,2,1,0:T(8,128)(2,1)S(1)}, u32[]{:S(2)}, u32[]{:S(2)}) collective-permute-start(bf16[3,2,128,128]{3,2,1,0:T(8,128)(2,1)S(1)} %get-tuple-element.26.refs_0_), channel_id=1, source_target_pairs={{0,6},{2,0},{4,2},{6,4},{8,14},{10,8},{12,10},{14,12},{16,22},{18,... | collective-permute-start | bytes 589832 | tf_op jit(solution)/shard_map/ppermute | solution.py:52
  32.6 1.2 collective-permute-start.5
  33.8 1.0 copy.13
  34.8 1.4 collective-permute-done.3.refs_1_
  36.2 5.1 %collective-permute-done.5.refs_3_ = bf16[3,2,128,128]{3,2,1,0:T(8,128)(2,1)S(1)} collective-permute-done((bf16[3,2,128,128]{3,2,1,0:T(8,128)(2,1)S(1)}, bf16[3,2,128,128]{3,2,1,0:T(8,128)(2,1)S(1)}, u32[]{:S(2)}, u32[]{:S(2)}) %collective-permute-start.5) | collective-permute-done | bytes 196640 | tf_op jit(solution)/shard_map/ppermute | solution.py:52
  41.3 6.3 %all-to-all-done = bf16[4,2,3,2,128,128]{5,4,3,2,1,0:T(8,128)(2,1)S(1)} async-done(((bf16[4,2,3,2,128,128]{5,4,3,2,1,0:T(8,128)(2,1)}), bf16[4,2,3,2,128,128]{5,4,3,2,1,0:T(8,128)(2,1)S(1)}, u32[]{:S(2)}, u32[]{:S(2)}) %all-to-all-start) | async-done | bytes 1572896 | tf_op jit(solution)/shard_map/all_to_all | solution.py:44
  47.6 1.0 slice_bitcast_fusion
  48.6 7.3 %all-to-all-start.1 = ((bf16[16,32,768]{2,1,0:T(8,128)(2,1)}), bf16[16,32,768]{2,1,0:T(8,128)(2,1)S(1)}, u32[]{:S(2)}, u32[]{:S(2)}) async-start(bf16[16,32,768]{2,1,0:T(8,128)(2,1)} %bitcast.10), calls=%async_computation.1 | async-start | bytes 1572864 | tf_op jit(solution)/shard_map/all_to_all | solution.py:406
  56.2 0.4 collective-permute-start.7
  57.2 1.1 collective-permute-done.7.refs_4_
  59.1 9.8 %all-to-all-done.1.x_ref = bf16[16,32,768]{2,1,0:T(8,128)(2,1)S(1)} async-done(((bf16[16,32,768]{2,1,0:T(8,128)(2,1)}), bf16[16,32,768]{2,1,0:T(8,128)(2,1)S(1)}, u32[]{:S(2)}, u32[]{:S(2)}) %all-to-all-start.1) | async-done | bytes 786464 | tf_op jit(solution)/shard_map/all_to_all | solution.py:406
  68.9 4.8 %partial_scores.1 = f32[4,3,32,1024]{3,2,1,0:T(8,128)S(1)} custom-call(s32[4]{0:T(128)S(1)} %pad_add_fusion.place_ref, bf16[4,3,2,64,128]{4,3,2,1,0:T(8,128)(2,1)S(1)} %get-tuple-element.38.q0_ref, bf16[4,3,2,64,128]{4,3,2,1,0:T(8,128)(2,1)S(1)} %collective-permute-done.6.q1_ref, bf16[3,2,128,128]{3,2,1,0:T(8,128)(2,1)S(1)} %get-tuple-element.26.refs_0_, ...), custom_call_target="tpu_custom_call" | custom-call | tf_op jit(solution)/shard_map/partial_scores/pallas_call | solution.py:198
  73.7 22.3 %all_to_all.25.refs_0_ = f32[4,3,32,1024]{3,2,1,0:T(8,128)S(1)} all-to-all(f32[4,3,32,1024]{3,2,1,0:T(8,128)S(1)} %partial_scores.1), channel_id=1, replica_groups={{0,16,32,48},{1,17,33,49},{2,18,34,50},{3,19,35,51},{4,20,36,52},{5,21,..., dimensions={0} | all-to-all | bytes 3145728 | tf_op jit(solution)/shard_map/all_to_all | solution.py:44
  96.2 1.0 collective-permute-start.11
  97.2 1.5 collective-permute-start.12
  98.7 8.5 %all-gather.7.cloned.1.call-done = bf16[32,3,2,128,128]{4,3,2,1,0:T(8,128)(2,1)} async-done(((bf16[4,3,2,128,128]{4,3,2,1,0:T(8,128)(2,1)}), bf16[32,3,2,128,128]{4,3,2,1,0:T(8,128)(2,1)}) %all-gather.7.cloned.1.call-update) | async-done | bytes 6291472 | tf_op jit(solution)/shard_map/all_gather | solution.py:48
  107.2 1.3 collective-permute-done.13.w3_ref
  108.6 4.4 %row_mix.1 = bf16[16,3,2,32,128]{4,3,2,1,0:T(8,128)(2,1)S(1)} custom-call(s32[4]{0:T(128)S(1)} %pad_add_fusion.place_ref, bf16[3,32,1024]{2,1,0:T(8,128)(2,1)S(1)} %row_softmax.1.w0_ref, bf16[3,32,1024]{2,1,0:T(8,128)(2,1)S(1)} %collective-permute-done.11.w1_ref, bf16[3,32,1024]{2,1,0:T(8,128)(2,1)S(1)} %collective-permute-done.12.w2_ref, ...), custom_call_target="tpu_custom_call" | custom-call | tf_op jit(solution)/shard_map/row_mix/pallas_call | solution.py:257
  113.0 18.4 %all_to_all.26 = bf16[16,3,2,32,128]{4,3,2,1,0:T(8,128)(2,1)S(1)} all-to-all(bf16[16,3,2,32,128]{4,3,2,1,0:T(8,128)(2,1)S(1)} %row_mix.1), channel_id=1, replica_groups={{0,16,32,48,64,80,96,112,1,17,33,49,65,81,97,113},{2,18,34,50,66,82,98,..., dimensions={0} | all-to-all | bytes 1572864 | tf_op jit(solution)/shard_map/all_to_all | solution.py:44
  131.5 14.7 %column_part.1 = bf16[16,32,768]{2,1,0:T(8,128)(2,1)S(1)} custom-call(bf16[16,3,64,128]{3,2,1,0:T(8,128)(2,1)S(1)} %bitcast.25, bf16[16,32,768]{2,1,0:T(8,128)(2,1)S(1)} %all-to-all-done.1.x_ref, f32[768]{0:T(1024)S(1)} %copy-done.5, f32[768]{0:T(1024)S(1)} %copy-done.6, bf16[768,768]{1,0:T(8,128)(2,1)S(1)} %copy-done.2, bf16[768,768]{1,0:T(8,128)(2,1)S(1)} %copy-done.3, ...), custom_call_target="tpu_custom_call" | custom-call | tf_op jit(solution)/shard_map/column_part/pallas_call | solution.py:360
  146.2 17.1 %all_to_all.27 = bf16[16,32,768]{2,1,0:T(8,128)(2,1)S(1)} all-to-all(bf16[16,32,768]{2,1,0:T(8,128)(2,1)S(1)} %column_part.1), channel_id=1, replica_groups=mesh['seq'=16,'col'=8] {'seq'}, dimensions={0} | all-to-all | bytes 1572864 | tf_op jit(solution)/shard_map/all_to_all | solution.py:423
  163.3 0.9 copy.14
  (37 shorter events, 2.1 us)
Async XLA Ops:
  6.5 62.4 %all-gather.5.cloned.1.call-start = ((), (), s32[]{:S(2)}) async-start(), calls=%async_computation.5 | async-start | bytes 5308416 | tf_op jit(solution)/shard_map/all_gather | solution.py:48
  6.6 0.7 copy-start.4
  7.3 9.0 %copy-start = (bf16[768,2304]{1,0:T(8,128)(2,1)S(1)}, bf16[768,2304]{1,0:T(8,128)(2,1)}, u32[]{:S(2)}) copy-start(bf16[768,2304]{1,0:T(8,128)(2,1)} %w_ref.3) | copy-start | bytes 10616836
  10.6 8.6 %collective-permute-start.2 = (bf16[3,2,128,128]{3,2,1,0:T(8,128)(2,1)S(1)}, bf16[3,2,128,128]{3,2,1,0:T(8,128)(2,1)S(1)}, u32[]{:S(2)}, u32[]{:S(2)}) collective-permute-start(bf16[3,2,128,128]{3,2,1,0:T(8,128)(2,1)S(1)} %get-tuple-element.22), channel_id=1, source_target_pairs={{0,64},{2,66},{4,68},{6,70},{8,72},{10,74},{12,76},{14,78},{16,80}... | collective-permute-start | bytes 589832 | tf_op jit(solution)/shard_map/ppermute | solution.py:52
  12.7 11.0 %collective-permute-start.1 = (bf16[3,2,128,128]{3,2,1,0:T(8,128)(2,1)S(1)}, bf16[3,2,128,128]{3,2,1,0:T(8,128)(2,1)S(1)}, u32[]{:S(2)}, u32[]{:S(2)}) collective-permute-start(bf16[3,2,128,128]{3,2,1,0:T(8,128)(2,1)S(1)} %get-tuple-element.21), channel_id=1, source_target_pairs={{0,1},{2,3},{4,5},{6,7},{8,9},{10,11},{12,13},{14,15},{16,17},{18,... | collective-permute-start | bytes 589832 | tf_op jit(solution)/shard_map/ppermute | solution.py:52
  15.2 8.5 %collective-permute-start = (bf16[3,2,128,128]{3,2,1,0:T(8,128)(2,1)S(1)}, bf16[3,2,128,128]{3,2,1,0:T(8,128)(2,1)S(1)}, u32[]{:S(2)}, u32[]{:S(2)}) collective-permute-start(bf16[3,2,128,128]{3,2,1,0:T(8,128)(2,1)S(1)} %get-tuple-element.20), channel_id=1, source_target_pairs={{0,65},{2,67},{4,69},{6,71},{8,73},{10,75},{12,77},{14,79},{16,81}... | collective-permute-start | bytes 589832 | tf_op jit(solution)/shard_map/ppermute | solution.py:52
  24.6 9.2 %copy-start.7 = (bf16[4,128,768]{2,1,0:T(8,128)(2,1)S(1)}, bf16[4,128,768]{2,1,0:T(8,128)(2,1)}, u32[]{:S(2)}) copy-start(bf16[4,128,768]{2,1,0:T(8,128)(2,1)} %param.10) | copy-start | bytes 2359300
  24.6 22.9 %all-to-all-start = ((bf16[4,2,3,2,128,128]{5,4,3,2,1,0:T(8,128)(2,1)}), bf16[4,2,3,2,128,128]{5,4,3,2,1,0:T(8,128)(2,1)S(1)}, u32[]{:S(2)}, u32[]{:S(2)}) async-start(bf16[4,2,3,2,128,128]{5,4,3,2,1,0:T(8,128)(2,1)} %query_value_proj.1), calls=%async_computation | async-start | bytes 3145728 | tf_op jit(solution)/shard_map/all_to_all | solution.py:44
  28.6 78.7 %all-gather.7.cloned.1.call-start = ((), (), s32[]{:S(2)}) async-start(), calls=%async_computation.6 | async-start | bytes 7077888 | tf_op jit(solution)/shard_map/all_gather | solution.py:48
  28.6 7.6 %collective-permute-start.3 = (bf16[3,2,128,128]{3,2,1,0:T(8,128)(2,1)S(1)}, bf16[3,2,128,128]{3,2,1,0:T(8,128)(2,1)S(1)}, u32[]{:S(2)}, u32[]{:S(2)}) collective-permute-start(bf16[3,2,128,128]{3,2,1,0:T(8,128)(2,1)S(1)} %get-tuple-element.26.refs_0_), channel_id=1, source_target_pairs={{0,2},{2,4},{4,6},{6,0},{8,10},{10,12},{12,14},{14,8},{16,18},{18,... | collective-permute-start | bytes 589832 | tf_op jit(solution)/shard_map/ppermute | solution.py:52
  30.4 5.8 %collective-permute-start.4 = (bf16[3,2,128,128]{3,2,1,0:T(8,128)(2,1)S(1)}, bf16[3,2,128,128]{3,2,1,0:T(8,128)(2,1)S(1)}, u32[]{:S(2)}, u32[]{:S(2)}) collective-permute-start(bf16[3,2,128,128]{3,2,1,0:T(8,128)(2,1)S(1)} %get-tuple-element.26.refs_0_), channel_id=1, source_target_pairs={{0,6},{2,0},{4,2},{6,4},{8,14},{10,8},{12,10},{14,12},{16,22},{18,... | collective-permute-start | bytes 589832 | tf_op jit(solution)/shard_map/ppermute | solution.py:52
  32.6 8.7 %collective-permute-start.5 = (bf16[3,2,128,128]{3,2,1,0:T(8,128)(2,1)S(1)}, bf16[3,2,128,128]{3,2,1,0:T(8,128)(2,1)S(1)}, u32[]{:S(2)}, u32[]{:S(2)}) collective-permute-start(bf16[3,2,128,128]{3,2,1,0:T(8,128)(2,1)S(1)} %get-tuple-element.26.refs_0_), channel_id=1, source_target_pairs={{0,4},{2,6},{4,0},{6,2},{8,12},{10,14},{12,8},{14,10},{16,20},{18,... | collective-permute-start | bytes 589832 | tf_op jit(solution)/shard_map/ppermute | solution.py:52
  48.6 20.3 %all-to-all-start.1 = ((bf16[16,32,768]{2,1,0:T(8,128)(2,1)}), bf16[16,32,768]{2,1,0:T(8,128)(2,1)S(1)}, u32[]{:S(2)}, u32[]{:S(2)}) async-start(bf16[16,32,768]{2,1,0:T(8,128)(2,1)} %bitcast.10), calls=%async_computation.1 | async-start | bytes 1572864 | tf_op jit(solution)/shard_map/all_to_all | solution.py:406
  56.0 3.1 %collective-permute-start.6 = (bf16[4,3,2,64,128]{4,3,2,1,0:T(8,128)(2,1)S(1)}, bf16[4,3,2,64,128]{4,3,2,1,0:T(8,128)(2,1)S(1)}, u32[]{:S(2)}, u32[]{:S(2)}) collective-permute-start(bf16[4,3,2,64,128]{4,3,2,1,0:T(8,128)(2,1)S(1)} %get-tuple-element.37), channel_id=1, source_target_pairs={{0,8},{2,10},{4,12},{6,14},{8,0},{10,2},{12,4},{14,6},{16,24},{18,... | collective-permute-start | bytes 1179656 | tf_op jit(solution)/shard_map/ppermute | solution.py:52
  56.2 2.1 %collective-permute-start.7 = (bf16[3,2,128,128]{3,2,1,0:T(8,128)(2,1)S(1)}, bf16[3,2,128,128]{3,2,1,0:T(8,128)(2,1)S(1)}, u32[]{:S(2)}, u32[]{:S(2)}) collective-permute-start(bf16[3,2,128,128]{3,2,1,0:T(8,128)(2,1)S(1)} %get-tuple-element.26.refs_0_), channel_id=1, source_target_pairs={{0,8},{2,10},{4,12},{6,14},{8,0},{10,2},{12,4},{14,6},{16,24},{18,... | collective-permute-start | bytes 589832 | tf_op jit(solution)/shard_map/ppermute | solution.py:52
  56.6 2.0 %collective-permute-start.8 = (bf16[3,2,128,128]{3,2,1,0:T(8,128)(2,1)S(1)}, bf16[3,2,128,128]{3,2,1,0:T(8,128)(2,1)S(1)}, u32[]{:S(2)}, u32[]{:S(2)}) collective-permute-start(bf16[3,2,128,128]{3,2,1,0:T(8,128)(2,1)S(1)} %collective-permute-done.3.refs_1_), channel_id=1, source_target_pairs={{0,8},{2,10},{4,12},{6,14},{8,0},{10,2},{12,4},{14,6},{16,24},{18,... | collective-permute-start | bytes 589832 | tf_op jit(solution)/shard_map/ppermute | solution.py:52
  56.7 2.1 %collective-permute-start.9 = (bf16[3,2,128,128]{3,2,1,0:T(8,128)(2,1)S(1)}, bf16[3,2,128,128]{3,2,1,0:T(8,128)(2,1)S(1)}, u32[]{:S(2)}, u32[]{:S(2)}) collective-permute-start(bf16[3,2,128,128]{3,2,1,0:T(8,128)(2,1)S(1)} %collective-permute-done.4.refs_2_), channel_id=1, source_target_pairs={{0,8},{2,10},{4,12},{6,14},{8,0},{10,2},{12,4},{14,6},{16,24},{18,... | collective-permute-start | bytes 589832 | tf_op jit(solution)/shard_map/ppermute | solution.py:52
  57.1 2.0 %collective-permute-start.10 = (bf16[3,2,128,128]{3,2,1,0:T(8,128)(2,1)S(1)}, bf16[3,2,128,128]{3,2,1,0:T(8,128)(2,1)S(1)}, u32[]{:S(2)}, u32[]{:S(2)}) collective-permute-start(bf16[3,2,128,128]{3,2,1,0:T(8,128)(2,1)S(1)} %collective-permute-done.5.refs_3_), channel_id=1, source_target_pairs={{0,8},{2,10},{4,12},{6,14},{8,0},{10,2},{12,4},{14,6},{16,24},{18,... | collective-permute-start | bytes 589832 | tf_op jit(solution)/shard_map/ppermute | solution.py:52
  96.2 11.0 %collective-permute-start.11 = (bf16[3,32,1024]{2,1,0:T(8,128)(2,1)S(1)}, bf16[3,32,1024]{2,1,0:T(8,128)(2,1)S(1)}, u32[]{:S(2)}, u32[]{:S(2)}) collective-permute-start(bf16[3,32,1024]{2,1,0:T(8,128)(2,1)S(1)} %row_softmax.1.w0_ref), channel_id=1, source_target_pairs={{0,48},{2,50},{4,52},{6,54},{8,56},{10,58},{12,60},{14,62},{16,0},... | collective-permute-start | bytes 589832 | tf_op jit(solution)/shard_map/ppermute | solution.py:52
  97.2 10.1 %collective-permute-start.12 = (bf16[3,32,1024]{2,1,0:T(8,128)(2,1)S(1)}, bf16[3,32,1024]{2,1,0:T(8,128)(2,1)S(1)}, u32[]{:S(2)}, u32[]{:S(2)}) collective-permute-start(bf16[3,32,1024]{2,1,0:T(8,128)(2,1)S(1)} %row_softmax.1.w0_ref), channel_id=1, source_target_pairs={{0,32},{2,34},{4,36},{6,38},{8,40},{10,42},{12,44},{14,46},{16,48}... | collective-permute-start | bytes 589832 | tf_op jit(solution)/shard_map/ppermute | solution.py:52
  98.7 9.9 %collective-permute-start.13 = (bf16[3,32,1024]{2,1,0:T(8,128)(2,1)S(1)}, bf16[3,32,1024]{2,1,0:T(8,128)(2,1)S(1)}, u32[]{:S(2)}, u32[]{:S(2)}) collective-permute-start(bf16[3,32,1024]{2,1,0:T(8,128)(2,1)S(1)} %row_softmax.1.w0_ref), channel_id=1, source_target_pairs={{0,16},{2,18},{4,20},{6,22},{8,24},{10,26},{12,28},{14,30},{16,32}... | collective-permute-start | bytes 589832 | tf_op jit(solution)/shard_map/ppermute | solution.py:52
  108.6 22.9 %copy-start.1 = (bf16[768,2304]{1,0:T(8,128)(2,1)S(1)}, bf16[768,2304]{1,0:T(8,128)(2,1)}, u32[]{:S(2)}) copy-start(bf16[768,2304]{1,0:T(8,128)(2,1)} %attend.1) | copy-start | bytes 10616836
  108.6 22.9 %copy-start.3 = (bf16[768,768]{1,0:T(8,128)(2,1)S(1)}, bf16[768,768]{1,0:T(8,128)(2,1)}, u32[]{:S(2)}) copy-start(bf16[768,768]{1,0:T(8,128)(2,1)} %exit_col.1) | copy-start | bytes 3538948
  113.0 18.5 %copy-start.2 = (bf16[768,768]{1,0:T(8,128)(2,1)S(1)}, bf16[768,768]{1,0:T(8,128)(2,1)}, u32[]{:S(2)}) copy-start(bf16[768,768]{1,0:T(8,128)(2,1)} %exit_row.1) | copy-start | bytes 3538948
  113.0 18.5 %copy-start.5 = (f32[768]{0:T(1024)S(1)}, f32[768]{0:T(1024)}, u32[]{:S(2)}) copy-start(f32[768]{0:T(1024)} %gain_col_ref.1) | copy-start | bytes 9220
  113.0 18.5 %copy-start.6 = (f32[768]{0:T(1024)S(1)}, f32[768]{0:T(1024)}, u32[]{:S(2)}) copy-start(f32[768]{0:T(1024)} %gain_ffn_ref.1) | copy-start | bytes 9220
Sparse Core Ops, SparseCore 0:
  24.7 39.3 all-gather.4
  65.8 41.3 all-gather.6
